TPU v7x, 128 devices: a whole 4x4x4 slice. The times are simulated.
128 devices in a mesh: dp: 2 (over z_hi), ctx: 64 (over y, z_lo, x, core).
Axes of the slice: x: 4, y: 4, z: 4 (z_hi: 2, z_lo: 2; z = z_hi * 2 + z_lo), core: 2. Of those that a mesh axis runs over, the one named last changes fastest.
Arguments:
- query: bfloat16 [8192, 16384], P(None, ('dp', 'ctx')), may hold values from -6 to 6
- key_in: bfloat16 [8192, 16384], P(None, ('dp', 'ctx')), may hold values from -6 to 6
- value_in: bfloat16 [8192, 16384], P(None, ('dp', 'ctx')), may hold values from -6 to 6
- cotangent: bfloat16 [8192, 16384], P(None, ('dp', 'ctx')), may hold values from -6 to 6
- residue: float32 [8192, 16], P('ctx'), may hold values from -4 to 4
- log_rate: float32 [8192, 16], P('ctx'), as said below
- bias: float32 [8192], P('ctx'), may hold values from 0.25 to 1.5
Outputs:
- gated: bfloat16 [8192, 16384], P(None, ('dp', 'ctx'))
- grad_query: bfloat16 [8192, 16384], P(None, ('dp', 'ctx'))
- grad_key: bfloat16 [8192, 16384], P(None, ('dp', 'ctx'))
- grad_value: bfloat16 [8192, 16384], P(None, ('dp', 'ctx'))
- grad_residue: float32 [8192, 16], P('ctx')
- grad_log_rate: float32 [8192, 16], P('ctx')
- grad_bias: float32 [8192], P('ctx')
Inputs may be any that keep to these rules, and one draw needn't show every extreme that they name: exp(log_rate) lies between 0.1 / 8192 and 1 / 30.
All inputs are finite; a program needn't handle non-finite values.
Results may differ from a plain program's by a relative error of at most 0.0065.
Values may be sent and summed in bfloat16 or wider, within the bound.
A program may use at most 128 MiB of HBM per device.

v0:
```python
import math

import jax
import jax.numpy as jnp
from jax import lax
from jax.sharding import PartitionSpec as P

precise = lax.Precision.HIGH


def make_tables(shards, shard_rows):
    full_len = 2 * shards * shard_rows
    freq_index = jnp.arange(2 * shards, dtype=jnp.int32)
    place_index = jnp.arange(shards, dtype=jnp.int32)
    inner_index = jnp.arange(shard_rows, dtype=jnp.int32)
    first_angle = (freq_index[:, None] * place_index[None, :] % (2 * shards)).astype(
        jnp.float32
    ) * (math.pi / shards)
    twist_angle = (freq_index[:, None] * inner_index[None, :] % full_len).astype(jnp.float32) * (
        2.0 * math.pi / full_len
    )
    second_angle = (inner_index[:, None] * inner_index[None, :] % shard_rows).astype(
        jnp.float32
    ) * (2.0 * math.pi / shard_rows)
    omega_angle = (freq_index[:, None] + 2 * shards * inner_index[None, :]).astype(jnp.float32) * (
        2.0 * math.pi / full_len
    )
    parity = (1 - 2 * (freq_index % 2)).astype(jnp.float32)[:, None] * jnp.ones(
        (1, shard_rows), jnp.float32
    )
    return (
        jnp.cos(first_angle),
        jnp.sin(first_angle),
        jnp.cos(twist_angle),
        jnp.sin(twist_angle),
        jnp.cos(second_angle),
        jnp.sin(second_angle),
        jnp.cos(omega_angle),
        jnp.sin(omega_angle),
        jnp.sin(0.5 * omega_angle),
        parity,
    )


def split_section(table, signal):
    upper = table.astype(jnp.bfloat16)
    lower = (table - upper.astype(jnp.float32)).astype(jnp.bfloat16)
    return jnp.einsum(
        "kp,cps->cks", upper, signal, preferred_element_type=jnp.float32
    ) + jnp.einsum("kp,cps->cks", lower, signal, preferred_element_type=jnp.float32)


def forward_spectrum(signal, tables):
    first_cos, first_sin, twist_cos, twist_sin, second_cos, second_sin = tables[:6]
    head_re = split_section(first_cos, signal)
    head_im = -split_section(first_sin, signal)
    middle_re = head_re * twist_cos + head_im * twist_sin
    middle_im = head_im * twist_cos - head_re * twist_sin
    spec_re = jnp.einsum("cks,sj->ckj", middle_re, second_cos, precision=precise) + jnp.einsum(
        "cks,sj->ckj", middle_im, second_sin, precision=precise
    )
    spec_im = jnp.einsum("cks,sj->ckj", middle_im, second_cos, precision=precise) - jnp.einsum(
        "cks,sj->ckj", middle_re, second_sin, precision=precise
    )
    return (spec_re, spec_im)


def inverse_real(spec_re, spec_im, tables):
    first_cos, first_sin, twist_cos, twist_sin, second_cos, second_sin = tables[:6]
    full_len = spec_re.shape[1] * spec_re.shape[2]
    back_re = jnp.einsum("ckj,sj->cks", spec_re, second_cos, precision=precise) - jnp.einsum(
        "ckj,sj->cks", spec_im, second_sin, precision=precise
    )
    back_im = jnp.einsum("ckj,sj->cks", spec_im, second_cos, precision=precise) + jnp.einsum(
        "ckj,sj->cks", spec_re, second_sin, precision=precise
    )
    turned_re = back_re * twist_cos - back_im * twist_sin
    turned_im = back_im * twist_cos + back_re * twist_sin
    signal = jnp.einsum("kp,cks->cps", first_cos, turned_re, precision=precise) - jnp.einsum(
        "kp,cks->cps", first_sin, turned_im, precision=precise
    )
    return signal / full_len


def mode_parts(rates_log, tables, seq_len):
    omega_sin, half_sin, parity = (tables[7], tables[8], tables[9])
    decay_rate = jnp.exp(rates_log)[:, :, None, None]
    decay_factor = jnp.exp(-decay_rate)
    tail_term = jnp.exp(-decay_rate * seq_len) * parity
    denom_re = -jnp.expm1(-decay_rate) + 2.0 * decay_factor * half_sin * half_sin
    denom_im = decay_factor * omega_sin
    magnitude = denom_re * denom_re + denom_im * denom_im
    numer_term = 1.0 - tail_term
    phi_re = numer_term * denom_re / magnitude
    phi_im = -numer_term * denom_im / magnitude
    return (decay_rate, decay_factor, tail_term, denom_re, denom_im, magnitude, phi_re, phi_im)


def filter_spectrum(residues, rates_log, tables, seq_len):
    parts_all = mode_parts(rates_log, tables, seq_len)
    decay_rate, phi_re, phi_im = (parts_all[0], parts_all[6], parts_all[7])
    gain_scale = residues[:, :, None, None] * jnp.sqrt(-jnp.expm1(-2.0 * decay_rate))
    return (jnp.sum(gain_scale * phi_re, axis=1), jnp.sum(gain_scale * phi_im, axis=1))


def filter_grads(cross_re, cross_im, residues, rates_log, tables, seq_len):
    omega_cos, omega_sin = (tables[6], tables[7])
    decay_rate, decay_factor, tail_term, denom_re, denom_im, magnitude, phi_re, phi_im = mode_parts(
        rates_log, tables, seq_len
    )
    weight_re = cross_re[:, None]
    weight_im = cross_im[:, None]
    along_mode = jnp.sum(weight_re * phi_re + weight_im * phi_im, axis=(2, 3))
    lam_re = decay_factor * omega_cos
    lam_im = -decay_factor * omega_sin
    prod_re = phi_re * lam_re - phi_im * lam_im
    prod_im = phi_re * lam_im + phi_im * lam_re
    numer_re = seq_len * tail_term - prod_re
    numer_im = -prod_im
    psi_re = (numer_re * denom_re + numer_im * denom_im) / magnitude
    psi_im = (numer_im * denom_re - numer_re * denom_im) / magnitude
    slope_mode = jnp.sum(weight_re * psi_re + weight_im * psi_im, axis=(2, 3))
    total_len = cross_re.shape[1] * cross_re.shape[2]
    plain_rate = decay_rate[:, :, 0, 0]
    root_norm = jnp.sqrt(-jnp.expm1(-2.0 * plain_rate))
    grad_res = root_norm * along_mode / total_len
    grad_rate = (
        residues * root_norm * slope_mode
        + residues * jnp.exp(-2.0 * plain_rate) / root_norm * along_mode
    ) / total_len
    return (grad_res, plain_rate * grad_rate)


def body(query, key_in, value_in, cotangent, residue, log_rate, bias):
    shards = lax.axis_size("ctx")
    channels, shard_rows = query.shape
    local_width = channels // shards
    block_size = math.gcd(local_width, max(1, 131072 // (2 * shards * shard_rows)))
    block_count = local_width // block_size
    seq_len = float(shards * shard_rows)
    tables = make_tables(shards, shard_rows)
    product = (key_in.astype(jnp.float32) * value_in.astype(jnp.float32)).astype(jnp.bfloat16)
    mixed_grad = (cotangent.astype(jnp.float32) * query.astype(jnp.float32)).astype(jnp.bfloat16)
    residue_blocks = residue.reshape(block_count, block_size, -1)
    rate_blocks = log_rate.reshape(block_count, block_size, -1)
    bias_blocks = bias.reshape(block_count, block_size)

    def blocked(channel_major):
        return channel_major.reshape(block_count, block_size, shards, shard_rows)

    def unblocked(stacked):
        return stacked.reshape(local_width, shards * shard_rows)

    def backward_part(signal, grad_in, x_re, x_im, h_re, h_im, residues, rates_log, skip_gain):
        d_re, d_im = forward_spectrum(grad_in, tables)
        grad_wide = grad_in.astype(jnp.float32)
        back_grad = inverse_real(d_re * h_re + d_im * h_im, d_im * h_re - d_re * h_im, tables)
        back_grad = back_grad + skip_gain[:, None, None] * grad_wide
        cross_re = d_re * x_re + d_im * x_im
        cross_im = d_im * x_re - d_re * x_im
        grad_res, grad_rate = filter_grads(cross_re, cross_im, residues, rates_log, tables, seq_len)
        skip_sum = jnp.sum(grad_wide * signal.astype(jnp.float32), axis=(1, 2))
        return (back_grad.astype(jnp.bfloat16), grad_res, grad_rate, skip_sum)

    signal_chan = lax.all_to_all(product, "ctx", split_axis=0, concat_axis=1, tiled=True)
    signal_blocks = blocked(signal_chan)

    def forward_block(packed):
        signal, residues, rates_log, skip_gain = packed
        x_re, x_im = forward_spectrum(signal, tables)
        h_re, h_im = filter_spectrum(residues, rates_log, tables, seq_len)
        mixed = inverse_real(x_re * h_re - x_im * h_im, x_re * h_im + x_im * h_re, tables)
        mixed = (mixed + skip_gain[:, None, None] * signal.astype(jnp.float32)).astype(jnp.bfloat16)
        return (mixed, x_re, x_im)

    mixed_all, spec_re, spec_im = lax.map(
        forward_block, (signal_blocks, residue_blocks, rate_blocks, bias_blocks)
    )
    mixed_tok = lax.all_to_all(unblocked(mixed_all), "ctx", split_axis=1, concat_axis=0, tiled=True)
    grad_chan = lax.all_to_all(mixed_grad, "ctx", split_axis=0, concat_axis=1, tiled=True)

    def backward_block(packed):
        signal, grad_in, x_re, x_im, residues, rates_log, skip_gain = packed
        h_re, h_im = filter_spectrum(residues, rates_log, tables, seq_len)
        return backward_part(
            signal, grad_in, x_re, x_im, h_re, h_im, residues, rates_log, skip_gain
        )

    back_all, grad_res, grad_rate, grad_skip = lax.map(
        backward_block,
        (
            signal_blocks,
            blocked(grad_chan),
            spec_re,
            spec_im,
            residue_blocks,
            rate_blocks,
            bias_blocks,
        ),
    )
    back_tok = lax.all_to_all(unblocked(back_all), "ctx", split_axis=1, concat_axis=0, tiled=True)
    summed_res, summed_rate, summed_skip = lax.psum(
        (
            grad_res.reshape(local_width, -1),
            grad_rate.reshape(local_width, -1),
            grad_skip.reshape(local_width),
        ),
        "dp",
    )
    norm_scale = 1.0 / math.sqrt(float(shards * shard_rows * lax.axis_size("dp")))
    mixed_f = mixed_tok.astype(jnp.float32)
    back_f = back_tok.astype(jnp.float32)
    gated = (query.astype(jnp.float32) * mixed_f).astype(jnp.bfloat16)
    grad_query = (cotangent.astype(jnp.float32) * mixed_f).astype(jnp.bfloat16)
    grad_key = (back_f * value_in.astype(jnp.float32)).astype(jnp.bfloat16)
    grad_value = (back_f * key_in.astype(jnp.float32)).astype(jnp.bfloat16)
    return (
        gated,
        grad_query,
        grad_key,
        grad_value,
        summed_res * norm_scale,
        summed_rate * norm_scale,
        summed_skip * norm_scale,
    )


def solution(mesh):
    return jax.shard_map(
        body,
        mesh=mesh,
        in_specs=(
            P(None, ("dp", "ctx")),
            P(None, ("dp", "ctx")),
            P(None, ("dp", "ctx")),
            P(None, ("dp", "ctx")),
            P("ctx", None),
            P("ctx", None),
            P("ctx"),
        ),
        out_specs=(
            P(None, ("dp", "ctx")),
            P(None, ("dp", "ctx")),
            P(None, ("dp", "ctx")),
            P(None, ("dp", "ctx")),
            P("ctx", None),
            P("ctx", None),
            P("ctx"),
        ),
        check_vma=False,
    )
```

profile of v0, /device:TPU:0, one launch (start us, length us, event | category | flops | bytes accessed | tf_op | source)
XLA Modules:
  0.0 1202.0 jit_solution(2712928329271541961)
XLA Ops:
  14.5 28.6 %all-to-all-done = bf16[64,128,128]{2,1,0:T(8,128)(2,1)S(1)} async-done(((bf16[64,128,128]{2,1,0:T(8,128)(2,1)}), bf16[64,128,128]{2,1,0:T(8,128)(2,1)S(1)}, u32[]{:S(2)}, u32[]{:S(2)}) %all-to-all-start) | async-done | bytes 2097184 | tf_op jit(solution)/shard_map/all_to_all | solution.py:165
  49.2 498.8 %while.38 = (s32[]{:T(128)}, bf16[16,8,64,128]{3,2,1,0:T(8,128)(2,1)}, f32[16,8,128,128]{3,2,1,0:T(8,128)}, f32[16,8,128,128]{3,2,1,0:T(8,128)}, bf16[16,8,64,12...) while((s32[]{:T(128)}, ...), condition=%wide.region_3.4_spmd.clone.clone.clone, body=%wide.region_0.3_spmd.clone.clone.clone.sunk | while | flops 1017922560 | bytes 25568488 | solution.py:176
  55.1 19.7 %fusion.492 = (f32[8,128,128]{2,1,0:T(8,128)S(1)}, f32[8,128,128]{2,1,0:T(8,128)S(1)}) fusion(f32[128]{0:T(128)S(1)} %get-tuple-element.1181, f32[128,128]{1,0:T(8,128)S(1)} %get-tuple-element.1100, f32[8,16]{1,0:T(8,128)S(1)} %get-tuple-element.1101, f32[128,128]{1,0:T(8,128)S(1)} %get-tuple-element.1102, f32[8,16]{1,0:T(8,128)S(1)} %get-tuple-element.1103, ...), kind=kLoop, calls=%fused_computation.31.clone.1 | loop fusion | flops 37486592 | bytes 1182720 | tf_op jit(solution)/shard_map/while/body/eval_jaxpr/reduce_sum | solution.py:103
  86.2 19.7 %fusion.492 = (f32[8,128,128]{2,1,0:T(8,128)S(1)}, f32[8,128,128]{2,1,0:T(8,128)S(1)}) fusion(f32[128]{0:T(128)S(1)} %get-tuple-element.1181, f32[128,128]{1,0:T(8,128)S(1)} %get-tuple-element.1100, f32[8,16]{1,0:T(8,128)S(1)} %get-tuple-element.1101, f32[128,128]{1,0:T(8,128)S(1)} %get-tuple-element.1102, f32[8,16]{1,0:T(8,128)S(1)} %get-tuple-element.1103, ...), kind=kLoop, calls=%fused_computation.31.clone.1 | loop fusion | flops 37486592 | bytes 1182720 | tf_op jit(solution)/shard_map/while/body/eval_jaxpr/reduce_sum | solution.py:103
  117.4 19.7 %fusion.492 = (f32[8,128,128]{2,1,0:T(8,128)S(1)}, f32[8,128,128]{2,1,0:T(8,128)S(1)}) fusion(f32[128]{0:T(128)S(1)} %get-tuple-element.1181, f32[128,128]{1,0:T(8,128)S(1)} %get-tuple-element.1100, f32[8,16]{1,0:T(8,128)S(1)} %get-tuple-element.1101, f32[128,128]{1,0:T(8,128)S(1)} %get-tuple-element.1102, f32[8,16]{1,0:T(8,128)S(1)} %get-tuple-element.1103, ...), kind=kLoop, calls=%fused_computation.31.clone.1 | loop fusion | flops 37486592 | bytes 1182720 | tf_op jit(solution)/shard_map/while/body/eval_jaxpr/reduce_sum | solution.py:103
  148.6 19.7 %fusion.492 = (f32[8,128,128]{2,1,0:T(8,128)S(1)}, f32[8,128,128]{2,1,0:T(8,128)S(1)}) fusion(f32[128]{0:T(128)S(1)} %get-tuple-element.1181, f32[128,128]{1,0:T(8,128)S(1)} %get-tuple-element.1100, f32[8,16]{1,0:T(8,128)S(1)} %get-tuple-element.1101, f32[128,128]{1,0:T(8,128)S(1)} %get-tuple-element.1102, f32[8,16]{1,0:T(8,128)S(1)} %get-tuple-element.1103, ...), kind=kLoop, calls=%fused_computation.31.clone.1 | loop fusion | flops 37486592 | bytes 1182720 | tf_op jit(solution)/shard_map/while/body/eval_jaxpr/reduce_sum | solution.py:103
  179.7 19.7 %fusion.492 = (f32[8,128,128]{2,1,0:T(8,128)S(1)}, f32[8,128,128]{2,1,0:T(8,128)S(1)}) fusion(f32[128]{0:T(128)S(1)} %get-tuple-element.1181, f32[128,128]{1,0:T(8,128)S(1)} %get-tuple-element.1100, f32[8,16]{1,0:T(8,128)S(1)} %get-tuple-element.1101, f32[128,128]{1,0:T(8,128)S(1)} %get-tuple-element.1102, f32[8,16]{1,0:T(8,128)S(1)} %get-tuple-element.1103, ...), kind=kLoop, calls=%fused_computation.31.clone.1 | loop fusion | flops 37486592 | bytes 1182720 | tf_op jit(solution)/shard_map/while/body/eval_jaxpr/reduce_sum | solution.py:103
  210.8 19.7 %fusion.492 = (f32[8,128,128]{2,1,0:T(8,128)S(1)}, f32[8,128,128]{2,1,0:T(8,128)S(1)}) fusion(f32[128]{0:T(128)S(1)} %get-tuple-element.1181, f32[128,128]{1,0:T(8,128)S(1)} %get-tuple-element.1100, f32[8,16]{1,0:T(8,128)S(1)} %get-tuple-element.1101, f32[128,128]{1,0:T(8,128)S(1)} %get-tuple-element.1102, f32[8,16]{1,0:T(8,128)S(1)} %get-tuple-element.1103, ...), kind=kLoop, calls=%fused_computation.31.clone.1 | loop fusion | flops 37486592 | bytes 1182720 | tf_op jit(solution)/shard_map/while/body/eval_jaxpr/reduce_sum | solution.py:103
  241.9 19.7 %fusion.492 = (f32[8,128,128]{2,1,0:T(8,128)S(1)}, f32[8,128,128]{2,1,0:T(8,128)S(1)}) fusion(f32[128]{0:T(128)S(1)} %get-tuple-element.1181, f32[128,128]{1,0:T(8,128)S(1)} %get-tuple-element.1100, f32[8,16]{1,0:T(8,128)S(1)} %get-tuple-element.1101, f32[128,128]{1,0:T(8,128)S(1)} %get-tuple-element.1102, f32[8,16]{1,0:T(8,128)S(1)} %get-tuple-element.1103, ...), kind=kLoop, calls=%fused_computation.31.clone.1 | loop fusion | flops 37486592 | bytes 1182720 | tf_op jit(solution)/shard_map/while/body/eval_jaxpr/reduce_sum | solution.py:103
  273.0 19.7 %fusion.492 = (f32[8,128,128]{2,1,0:T(8,128)S(1)}, f32[8,128,128]{2,1,0:T(8,128)S(1)}) fusion(f32[128]{0:T(128)S(1)} %get-tuple-element.1181, f32[128,128]{1,0:T(8,128)S(1)} %get-tuple-element.1100, f32[8,16]{1,0:T(8,128)S(1)} %get-tuple-element.1101, f32[128,128]{1,0:T(8,128)S(1)} %get-tuple-element.1102, f32[8,16]{1,0:T(8,128)S(1)} %get-tuple-element.1103, ...), kind=kLoop, calls=%fused_computation.31.clone.1 | loop fusion | flops 37486592 | bytes 1182720 | tf_op jit(solution)/shard_map/while/body/eval_jaxpr/reduce_sum | solution.py:103
  304.2 19.7 %fusion.492 = (f32[8,128,128]{2,1,0:T(8,128)S(1)}, f32[8,128,128]{2,1,0:T(8,128)S(1)}) fusion(f32[128]{0:T(128)S(1)} %get-tuple-element.1181, f32[128,128]{1,0:T(8,128)S(1)} %get-tuple-element.1100, f32[8,16]{1,0:T(8,128)S(1)} %get-tuple-element.1101, f32[128,128]{1,0:T(8,128)S(1)} %get-tuple-element.1102, f32[8,16]{1,0:T(8,128)S(1)} %get-tuple-element.1103, ...), kind=kLoop, calls=%fused_computation.31.clone.1 | loop fusion | flops 37486592 | bytes 1182720 | tf_op jit(solution)/shard_map/while/body/eval_jaxpr/reduce_sum | solution.py:103
  335.3 19.7 %fusion.492 = (f32[8,128,128]{2,1,0:T(8,128)S(1)}, f32[8,128,128]{2,1,0:T(8,128)S(1)}) fusion(f32[128]{0:T(128)S(1)} %get-tuple-element.1181, f32[128,128]{1,0:T(8,128)S(1)} %get-tuple-element.1100, f32[8,16]{1,0:T(8,128)S(1)} %get-tuple-element.1101, f32[128,128]{1,0:T(8,128)S(1)} %get-tuple-element.1102, f32[8,16]{1,0:T(8,128)S(1)} %get-tuple-element.1103, ...), kind=kLoop, calls=%fused_computation.31.clone.1 | loop fusion | flops 37486592 | bytes 1182720 | tf_op jit(solution)/shard_map/while/body/eval_jaxpr/reduce_sum | solution.py:103
  366.5 19.7 %fusion.492 = (f32[8,128,128]{2,1,0:T(8,128)S(1)}, f32[8,128,128]{2,1,0:T(8,128)S(1)}) fusion(f32[128]{0:T(128)S(1)} %get-tuple-element.1181, f32[128,128]{1,0:T(8,128)S(1)} %get-tuple-element.1100, f32[8,16]{1,0:T(8,128)S(1)} %get-tuple-element.1101, f32[128,128]{1,0:T(8,128)S(1)} %get-tuple-element.1102, f32[8,16]{1,0:T(8,128)S(1)} %get-tuple-element.1103, ...), kind=kLoop, calls=%fused_computation.31.clone.1 | loop fusion | flops 37486592 | bytes 1182720 | tf_op jit(solution)/shard_map/while/body/eval_jaxpr/reduce_sum | solution.py:103
  397.6 19.7 %fusion.492 = (f32[8,128,128]{2,1,0:T(8,128)S(1)}, f32[8,128,128]{2,1,0:T(8,128)S(1)}) fusion(f32[128]{0:T(128)S(1)} %get-tuple-element.1181, f32[128,128]{1,0:T(8,128)S(1)} %get-tuple-element.1100, f32[8,16]{1,0:T(8,128)S(1)} %get-tuple-element.1101, f32[128,128]{1,0:T(8,128)S(1)} %get-tuple-element.1102, f32[8,16]{1,0:T(8,128)S(1)} %get-tuple-element.1103, ...), kind=kLoop, calls=%fused_computation.31.clone.1 | loop fusion | flops 37486592 | bytes 1182720 | tf_op jit(solution)/shard_map/while/body/eval_jaxpr/reduce_sum | solution.py:103
  428.7 19.7 %fusion.492 = (f32[8,128,128]{2,1,0:T(8,128)S(1)}, f32[8,128,128]{2,1,0:T(8,128)S(1)}) fusion(f32[128]{0:T(128)S(1)} %get-tuple-element.1181, f32[128,128]{1,0:T(8,128)S(1)} %get-tuple-element.1100, f32[8,16]{1,0:T(8,128)S(1)} %get-tuple-element.1101, f32[128,128]{1,0:T(8,128)S(1)} %get-tuple-element.1102, f32[8,16]{1,0:T(8,128)S(1)} %get-tuple-element.1103, ...), kind=kLoop, calls=%fused_computation.31.clone.1 | loop fusion | flops 37486592 | bytes 1182720 | tf_op jit(solution)/shard_map/while/body/eval_jaxpr/reduce_sum | solution.py:103
  459.9 19.7 %fusion.492 = (f32[8,128,128]{2,1,0:T(8,128)S(1)}, f32[8,128,128]{2,1,0:T(8,128)S(1)}) fusion(f32[128]{0:T(128)S(1)} %get-tuple-element.1181, f32[128,128]{1,0:T(8,128)S(1)} %get-tuple-element.1100, f32[8,16]{1,0:T(8,128)S(1)} %get-tuple-element.1101, f32[128,128]{1,0:T(8,128)S(1)} %get-tuple-element.1102, f32[8,16]{1,0:T(8,128)S(1)} %get-tuple-element.1103, ...), kind=kLoop, calls=%fused_computation.31.clone.1 | loop fusion | flops 37486592 | bytes 1182720 | tf_op jit(solution)/shard_map/while/body/eval_jaxpr/reduce_sum | solution.py:103
  491.0 19.7 %fusion.492 = (f32[8,128,128]{2,1,0:T(8,128)S(1)}, f32[8,128,128]{2,1,0:T(8,128)S(1)}) fusion(f32[128]{0:T(128)S(1)} %get-tuple-element.1181, f32[128,128]{1,0:T(8,128)S(1)} %get-tuple-element.1100, f32[8,16]{1,0:T(8,128)S(1)} %get-tuple-element.1101, f32[128,128]{1,0:T(8,128)S(1)} %get-tuple-element.1102, f32[8,16]{1,0:T(8,128)S(1)} %get-tuple-element.1103, ...), kind=kLoop, calls=%fused_computation.31.clone.1 | loop fusion | flops 37486592 | bytes 1182720 | tf_op jit(solution)/shard_map/while/body/eval_jaxpr/reduce_sum | solution.py:103
  522.2 19.7 %fusion.492 = (f32[8,128,128]{2,1,0:T(8,128)S(1)}, f32[8,128,128]{2,1,0:T(8,128)S(1)}) fusion(f32[128]{0:T(128)S(1)} %get-tuple-element.1181, f32[128,128]{1,0:T(8,128)S(1)} %get-tuple-element.1100, f32[8,16]{1,0:T(8,128)S(1)} %get-tuple-element.1101, f32[128,128]{1,0:T(8,128)S(1)} %get-tuple-element.1102, f32[8,16]{1,0:T(8,128)S(1)} %get-tuple-element.1103, ...), kind=kLoop, calls=%fused_computation.31.clone.1 | loop fusion | flops 37486592 | bytes 1182720 | tf_op jit(solution)/shard_map/while/body/eval_jaxpr/reduce_sum | solution.py:103
  551.2 33.8 %all_to_all.58 = bf16[128,64,128]{2,0,1:T(8,128)(2,1)S(1)} all-to-all(bf16[128,64,128]{2,0,1:T(8,128)(2,1)S(1)} %copy.93), channel_id=1, replica_groups=mesh['dp'=2,'ctx'=64] {'ctx'}, dimensions={1} | all-to-all | bytes 4194304 | tf_op jit(solution)/shard_map/all_to_all | solution.py:179
  594.6 28.8 %all-to-all-done.2 = bf16[64,128,128]{2,1,0:T(8,128)(2,1)} async-done(((bf16[64,128,128]{2,1,0:T(8,128)(2,1)}), bf16[64,128,128]{2,1,0:T(8,128)(2,1)}, u32[]{:S(2)}, u32[]{:S(2)}) %all-to-all-start.2) | async-done | bytes 2097184 | tf_op jit(solution)/shard_map/all_to_all | solution.py:180
  629.5 523.5 %while.39 = (s32[]{:T(128)}, bf16[16,8,64,128]{3,2,1,0:T(8,128)(2,1)}, f32[16,8,16]{2,1,0:T(8,128)S(1)}, f32[16,8,16]{2,1,0:T(8,128)S(1)}, f32[16,8]{1,0:T(8,128...) while((s32[]{:T(128)}, ...), condition=%wide.region_10.11_spmd.clone.clone.clone, body=%wide.region_4.10_spmd.clone.clone.clone.sunk | while | flops 1075595648 | bytes 28611440 | solution.py:189
  640.0 14.6 %fusion.537 = (f32[8,16]{1,0:T(8,128)S(1)}, f32[8,16]{1,0:T(8,128)S(1)}, f32[8,128,128]{2,1,0:T(8,128)S(1)}, f32[8,128,128]{2,1,0:T(8,128)S(1)}) fusion(f32[128]{0:T(128)S(1)} %get-tuple-element.1228, f32[8,16]{1,0:T(8,128)S(1)} %neg.259, f32[128,128]{1,0:T(8,128)S(1)} %get-tuple-element.1134, f32[8,128,128]{2,1,0:T(8,128)S(1)} %get-tuple-element.1135, ...), kind=kLoop, calls=%fused_computation.227.clone.1 | loop fusion | flops 94109440 | bytes 2298368 | tf_op jit(solution)/shard_map/while/body/eval_jaxpr/reduce_sum | solution.py:122
  672.6 14.6 %fusion.537 = (f32[8,16]{1,0:T(8,128)S(1)}, f32[8,16]{1,0:T(8,128)S(1)}, f32[8,128,128]{2,1,0:T(8,128)S(1)}, f32[8,128,128]{2,1,0:T(8,128)S(1)}) fusion(f32[128]{0:T(128)S(1)} %get-tuple-element.1228, f32[8,16]{1,0:T(8,128)S(1)} %neg.259, f32[128,128]{1,0:T(8,128)S(1)} %get-tuple-element.1134, f32[8,128,128]{2,1,0:T(8,128)S(1)} %get-tuple-element.1135, ...), kind=kLoop, calls=%fused_computation.227.clone.1 | loop fusion | flops 94109440 | bytes 2298368 | tf_op jit(solution)/shard_map/while/body/eval_jaxpr/reduce_sum | solution.py:122
  705.3 14.6 %fusion.537 = (f32[8,16]{1,0:T(8,128)S(1)}, f32[8,16]{1,0:T(8,128)S(1)}, f32[8,128,128]{2,1,0:T(8,128)S(1)}, f32[8,128,128]{2,1,0:T(8,128)S(1)}) fusion(f32[128]{0:T(128)S(1)} %get-tuple-element.1228, f32[8,16]{1,0:T(8,128)S(1)} %neg.259, f32[128,128]{1,0:T(8,128)S(1)} %get-tuple-element.1134, f32[8,128,128]{2,1,0:T(8,128)S(1)} %get-tuple-element.1135, ...), kind=kLoop, calls=%fused_computation.227.clone.1 | loop fusion | flops 94109440 | bytes 2298368 | tf_op jit(solution)/shard_map/while/body/eval_jaxpr/reduce_sum | solution.py:122
  738.0 14.6 %fusion.537 = (f32[8,16]{1,0:T(8,128)S(1)}, f32[8,16]{1,0:T(8,128)S(1)}, f32[8,128,128]{2,1,0:T(8,128)S(1)}, f32[8,128,128]{2,1,0:T(8,128)S(1)}) fusion(f32[128]{0:T(128)S(1)} %get-tuple-element.1228, f32[8,16]{1,0:T(8,128)S(1)} %neg.259, f32[128,128]{1,0:T(8,128)S(1)} %get-tuple-element.1134, f32[8,128,128]{2,1,0:T(8,128)S(1)} %get-tuple-element.1135, ...), kind=kLoop, calls=%fused_computation.227.clone.1 | loop fusion | flops 94109440 | bytes 2298368 | tf_op jit(solution)/shard_map/while/body/eval_jaxpr/reduce_sum | solution.py:122
  803.4 14.6 %fusion.537 = (f32[8,16]{1,0:T(8,128)S(1)}, f32[8,16]{1,0:T(8,128)S(1)}, f32[8,128,128]{2,1,0:T(8,128)S(1)}, f32[8,128,128]{2,1,0:T(8,128)S(1)}) fusion(f32[128]{0:T(128)S(1)} %get-tuple-element.1228, f32[8,16]{1,0:T(8,128)S(1)} %neg.259, f32[128,128]{1,0:T(8,128)S(1)} %get-tuple-element.1134, f32[8,128,128]{2,1,0:T(8,128)S(1)} %get-tuple-element.1135, ...), kind=kLoop, calls=%fused_computation.227.clone.1 | loop fusion | flops 94109440 | bytes 2298368 | tf_op jit(solution)/shard_map/while/body/eval_jaxpr/reduce_sum | solution.py:122
  836.1 14.6 %fusion.537 = (f32[8,16]{1,0:T(8,128)S(1)}, f32[8,16]{1,0:T(8,128)S(1)}, f32[8,128,128]{2,1,0:T(8,128)S(1)}, f32[8,128,128]{2,1,0:T(8,128)S(1)}) fusion(f32[128]{0:T(128)S(1)} %get-tuple-element.1228, f32[8,16]{1,0:T(8,128)S(1)} %neg.259, f32[128,128]{1,0:T(8,128)S(1)} %get-tuple-element.1134, f32[8,128,128]{2,1,0:T(8,128)S(1)} %get-tuple-element.1135, ...), kind=kLoop, calls=%fused_computation.227.clone.1 | loop fusion | flops 94109440 | bytes 2298368 | tf_op jit(solution)/shard_map/while/body/eval_jaxpr/reduce_sum | solution.py:122
  901.5 14.6 %fusion.537 = (f32[8,16]{1,0:T(8,128)S(1)}, f32[8,16]{1,0:T(8,128)S(1)}, f32[8,128,128]{2,1,0:T(8,128)S(1)}, f32[8,128,128]{2,1,0:T(8,128)S(1)}) fusion(f32[128]{0:T(128)S(1)} %get-tuple-element.1228, f32[8,16]{1,0:T(8,128)S(1)} %neg.259, f32[128,128]{1,0:T(8,128)S(1)} %get-tuple-element.1134, f32[8,128,128]{2,1,0:T(8,128)S(1)} %get-tuple-element.1135, ...), kind=kLoop, calls=%fused_computation.227.clone.1 | loop fusion | flops 94109440 | bytes 2298368 | tf_op jit(solution)/shard_map/while/body/eval_jaxpr/reduce_sum | solution.py:122
  934.2 14.6 %fusion.537 = (f32[8,16]{1,0:T(8,128)S(1)}, f32[8,16]{1,0:T(8,128)S(1)}, f32[8,128,128]{2,1,0:T(8,128)S(1)}, f32[8,128,128]{2,1,0:T(8,128)S(1)}) fusion(f32[128]{0:T(128)S(1)} %get-tuple-element.1228, f32[8,16]{1,0:T(8,128)S(1)} %neg.259, f32[128,128]{1,0:T(8,128)S(1)} %get-tuple-element.1134, f32[8,128,128]{2,1,0:T(8,128)S(1)} %get-tuple-element.1135, ...), kind=kLoop, calls=%fused_computation.227.clone.1 | loop fusion | flops 94109440 | bytes 2298368 | tf_op jit(solution)/shard_map/while/body/eval_jaxpr/reduce_sum | solution.py:122
  1032.2 14.6 %fusion.537 = (f32[8,16]{1,0:T(8,128)S(1)}, f32[8,16]{1,0:T(8,128)S(1)}, f32[8,128,128]{2,1,0:T(8,128)S(1)}, f32[8,128,128]{2,1,0:T(8,128)S(1)}) fusion(f32[128]{0:T(128)S(1)} %get-tuple-element.1228, f32[8,16]{1,0:T(8,128)S(1)} %neg.259, f32[128,128]{1,0:T(8,128)S(1)} %get-tuple-element.1134, f32[8,128,128]{2,1,0:T(8,128)S(1)} %get-tuple-element.1135, ...), kind=kLoop, calls=%fused_computation.227.clone.1 | loop fusion | flops 94109440 | bytes 2298368 | tf_op jit(solution)/shard_map/while/body/eval_jaxpr/reduce_sum | solution.py:122
  1130.3 14.6 %fusion.537 = (f32[8,16]{1,0:T(8,128)S(1)}, f32[8,16]{1,0:T(8,128)S(1)}, f32[8,128,128]{2,1,0:T(8,128)S(1)}, f32[8,128,128]{2,1,0:T(8,128)S(1)}) fusion(f32[128]{0:T(128)S(1)} %get-tuple-element.1228, f32[8,16]{1,0:T(8,128)S(1)} %neg.259, f32[128,128]{1,0:T(8,128)S(1)} %get-tuple-element.1134, f32[8,128,128]{2,1,0:T(8,128)S(1)} %get-tuple-element.1135, ...), kind=kLoop, calls=%fused_computation.227.clone.1 | loop fusion | flops 94109440 | bytes 2298368 | tf_op jit(solution)/shard_map/while/body/eval_jaxpr/reduce_sum | solution.py:122
  1163.1 31.5 %all-reduce = (f32[128,16]{1,0:T(8,128)S(1)}, f32[128,16]{1,0:T(8,128)S(1)}, f32[128]{0:T(128)S(1)}) all-reduce(f32[128,16]{1,0:T(8,128)S(1)} %bitcast.370, f32[128,16]{1,0:T(8,128)S(1)} %bitcast.371, f32[128]{0:T(128)S(1)} %reshape.245), channel_id=1, replica_groups=mesh['dp'=2,'ctx'=64] {'dp'}, use_global_device_ids=true, to_apply=%region_11.12 | all-reduce | flops 4224 | bytes 33792 | tf_op jit(solution)/shard_map/psum | solution.py:202
  (754 shorter events, 611.2 us)
Async XLA Ops:
  0.6 13.5 %copy-start.4 = (f32[128,16]{0,1:T(8,128)S(1)}, f32[128,16]{0,1:T(8,128)}, u32[]{:S(2)}) copy-start(f32[128,16]{0,1:T(8,128)} %param.15) | copy-start | bytes 24580
  0.6 13.6 %copy-start.5 = (f32[128,16]{0,1:T(8,128)S(1)}, f32[128,16]{0,1:T(8,128)}, u32[]{:S(2)}) copy-start(f32[128,16]{0,1:T(8,128)} %param.16) | copy-start | bytes 24580
  0.7 13.7 %copy-start.7 = (f32[128]{0:T(128)S(1)}, f32[128]{0:T(128)}, u32[]{:S(2)}) copy-start(f32[128]{0:T(128)} %param.17) | copy-start | bytes 1540
  4.8 38.4 %all-to-all-start = ((bf16[64,128,128]{2,1,0:T(8,128)(2,1)}), bf16[64,128,128]{2,1,0:T(8,128)(2,1)S(1)}, u32[]{:S(2)}, u32[]{:S(2)}) async-start(bf16[64,128,128]{2,1,0:T(8,128)(2,1)} %bitcast), calls=%async_computation | async-start | bytes 4194304 | tf_op jit(solution)/shard_map/all_to_all | solution.py:165
  43.1 1.3 copy-start.1
  548.1 36.9 %copy-start.2 = (bf16[8192,128]{1,0:T(8,128)(2,1)S(1)}, bf16[8192,128]{1,0:T(8,128)(2,1)}, u32[]{:S(2)}) copy-start(bf16[8192,128]{1,0:T(8,128)(2,1)} %param.11) | copy-start | bytes 6291460
  548.1 36.9 %copy-start.3 = (bf16[8192,128]{1,0:T(8,128)(2,1)S(1)}, bf16[8192,128]{1,0:T(8,128)(2,1)}, u32[]{:S(2)}) copy-start(bf16[8192,128]{1,0:T(8,128)(2,1)} %param.14) | copy-start | bytes 6291460
  589.0 34.4 %all-to-all-start.2 = ((bf16[64,128,128]{2,1,0:T(8,128)(2,1)}), bf16[64,128,128]{2,1,0:T(8,128)(2,1)}, u32[]{:S(2)}, u32[]{:S(2)}) async-start(bf16[64,128,128]{2,1,0:T(8,128)(2,1)} %bitcast.367), calls=%async_computation.2 | async-start | bytes 4194304 | tf_op jit(solution)/shard_map/all_to_all | solution.py:180
  1153.0 10.0 copy-start.6
  1153.0 43.5 %copy-start = (bf16[8192,128]{1,0:T(8,128)(2,1)S(1)}, bf16[8192,128]{1,0:T(8,128)(2,1)}, u32[]{:S(2)}) copy-start(bf16[8192,128]{1,0:T(8,128)(2,1)} %param.13) | copy-start | bytes 6291460
  1157.5 39.1 %all-to-all-start.3 = ((bf16[128,64,128]{2,0,1:T(8,128)(2,1)}), bf16[128,64,128]{2,0,1:T(8,128)(2,1)}, u32[]{:S(2)}, u32[]{:S(2)}) async-start(bf16[128,64,128]{2,0,1:T(8,128)(2,1)} %copy.95), calls=%async_computation.3 | async-start | bytes 4194304 | tf_op jit(solution)/shard_map/all_to_all | solution.py:201
where the time goes:
time: 1210 us; the launch traced here: 1200 us
  other arithmetic  608 us (50%)
  matrix products  389 us (32%)
  blocking collectives  65.3 us (5%)
  waiting for transfers between devices  57.4 us (5%)
  local copies, waits for them, and re-layouts  56 us (5%)
  starting transfers between devices  20.5 us (2%)
    reduce_sum x16, other arithmetic, filter_spectrum(): jnp.sum(gain_scale * phi_im, axis=1)  315 us
    reduce_sum x16, other arithmetic, filter_grads(): slope_mode = jnp.sum(weight_re * psi_re + weight_im * psi_im, axis=(2, 3))  234 us
    dot_general x32, matrix products, inverse_real(): jnp.einsum('kp,cks->cps', first_sin, turned_im, precision=precise)  54.1 us
    dot_general x64, matrix products, split_section(): jnp.einsum('kp,cps->cks', lower, signal, preferred_element_type=jnp.float32)  51.6 us
    dot_general x64, matrix products, split_section(): jnp.einsum('kp,cps->cks', upper, signal, preferred_element_type=jnp.float32)  50.8 us
    dot_general x32, matrix products, forward_spectrum(): jnp.einsum('cks,sj->ckj', middle_re, second_sin, precision=precise)  44.6 us
    dot_general x32, matrix products, forward_spectrum(): jnp.einsum('cks,sj->ckj', middle_im, second_sin, precision=precise)  38.2 us
    all_to_all x1, blocking collectives, body(): lax.all_to_all(unblocked(mixed_all), 'ctx', split_axis=1, concat_axis=0,...  33.8 us
  transfers between devices with their start and end apart: 3, of which 2 were waited for; matrix products, arithmetic and copies ran while one was open for 0% of the time, Pallas kernels for 0%

commit v1 on v0

v1 whole, which is shorter than its diff:
```python
import functools
import math

import jax
import jax.numpy as jnp
import numpy as np
from jax import lax
from jax.experimental import pallas as pl
from jax.experimental.pallas import tpu as pltpu
from jax.sharding import PartitionSpec as P

bf16 = jnp.bfloat16
f32 = jnp.float32
W = 128
HALF = 8
LANES = 256


def tables():
    n = np.arange(W)[:, None]
    f = np.arange(W)[None, :]
    angle = ((2 * f + 1) * n % (4 * W)) * (2.0 * math.pi / (4 * W))
    fwd = np.concatenate([np.cos(angle), -np.sin(angle)], axis=1)
    inv = fwd.T / W
    flip = np.eye(W)[::-1]
    cast = lambda z: jnp.asarray(np.ascontiguousarray(z), f32).astype(bf16)
    return cast(fwd), cast(fwd[::-1]), cast(inv), cast(inv[:, ::-1]), cast(flip)


def dot(a, b):
    return jnp.dot(a, b, preferred_element_type=f32)


def dot_nt(a, b):
    return lax.dot_general(a, b, (((1,), (1,)), ((), ())), preferred_element_type=f32)


def powers(rate_row):
    rate8 = jnp.broadcast_to(rate_row, (8, LANES))
    row = lax.broadcasted_iota(jnp.int32, (8, LANES), 0).astype(f32)
    out = jnp.exp(-rate8 * row)
    for step in (8, 16, 32, 64):
        mult = jnp.exp(-rate8 * float(step))
        parts = [out[i : i + 8] * mult for i in range(0, step, 8)]
        out = jnp.concatenate([out] + parts, axis=0)
    return out.astype(bf16)


def diag_mask():
    row = lax.broadcasted_iota(jnp.int32, (16, LANES), 0)
    lane = lax.broadcasted_iota(jnp.int32, (16, LANES), 1)
    return row == lane // 16


def diag_row(mask, rows):
    return jnp.sum(jnp.where(mask, rows, 0.0), axis=0, keepdims=True)


def mul16(a, b):
    return (a.astype(f32) * b.astype(f32)).astype(bf16)


def states_kernel(q_ref, k_ref, v_ref, c_ref, par_ref, flip_ref, out_ref):
    mask = diag_mask()

    def step(i, carry):
        sl = pl.ds(pl.multiple_of(i * 128, 128), 128)
        x = mul16(k_ref[sl, :], v_ref[sl, :])
        m = mul16(c_ref[sl, :], q_ref[sl, :])
        xr = dot(x, flip_ref[...]).astype(bf16)
        ahead, back = [], []
        for g in range(HALF):
            e = powers(par_ref[i, g : g + 1, :])
            rows = slice(16 * g, 16 * g + 16)
            res = dot(jnp.concatenate([xr[rows], m[rows]], axis=0), e)
            ahead.append(diag_row(mask, res[:16]))
            back.append(diag_row(mask, res[16:]))
        out_ref[i] = jnp.concatenate(ahead + back, axis=0).astype(bf16)
        return carry

    lax.fori_loop(0, out_ref.shape[0], step, 0)


def scan_kernel(st_ref, rate_ref, out_ref, hold):
    parts = st_ref.shape[0]
    decay = jnp.exp(-float(W) * rate_ref[...])

    def ahead(p, s):
        hold[p] = s
        return s * decay + st_ref[p].astype(f32)[:HALF]

    lax.fori_loop(0, parts, ahead, jnp.zeros((HALF, LANES), f32))

    def back(i, s):
        p = parts - 1 - i
        out_ref[p] = jnp.concatenate([hold[p], s], axis=0).astype(bf16)
        return s * decay + st_ref[p].astype(f32)[HALF:]

    lax.fori_loop(0, parts, back, jnp.zeros((HALF, LANES), f32))


def cmul(a, b):
    ar, ai, br, bi = a[:, :W], a[:, W:], b[:, :W], b[:, W:]
    return jnp.concatenate([ar * br - ai * bi, ar * bi + ai * br], axis=1).astype(bf16)


def mix_kernel(
    q_ref, k_ref, v_ref, c_ref, par_ref, own_ref, st_ref, fwd_ref, fwdr_ref, inv_ref, invr_ref,
    flip_ref, gated_ref, gq_ref, gk_ref, gv_ref, grad_ref, taps_s, yc_s, pc_s,
):
    mask = diag_mask()
    eye = lax.broadcasted_iota(jnp.int32, (W, W), 0) == lax.broadcasted_iota(jnp.int32, (W, W), 1)
    lag_no = lax.broadcasted_iota(jnp.int32, (W, W), 1).astype(f32)

    def step(i, carry):
        sl = pl.ds(pl.multiple_of(i * 128, 128), 128)
        q, k, v, c = q_ref[sl, :], k_ref[sl, :], v_ref[sl, :], c_ref[sl, :]
        x, m = mul16(k, v), mul16(c, q)
        xf, mf = x.astype(f32), m.astype(f32)
        xr = dot(x, flip_ref[...])
        spec_x = dot(x, fwd_ref[...])
        spec_m = dot(m, fwdr_ref[...])
        lag = dot(cmul(spec_x, spec_m), invr_ref[...])
        lag0 = lag.astype(bf16)
        lag1 = (lag * lag_no).astype(bf16)
        m1 = (mf * (lag_no + 1.0)).astype(bf16)
        x1 = (xr * lag_no).astype(bf16)
        rate = par_ref[i, 0:8, :]
        weight = par_ref[i, 8:16, :]
        state = st_ref[i].astype(f32)
        ahead, back = state[:HALF], state[HALF:]
        local_b = own_ref[i].astype(f32)[HALF:]
        decay = jnp.exp(-rate)
        wa = weight * decay * ahead
        wb = weight * decay * back
        a_rows, d_rows, m_rows, x_rows = [], [], [], []
        for g in range(HALF):
            e = powers(rate[g : g + 1])
            rows = slice(16 * g, 16 * g + 16)
            lhs = jnp.concatenate(
                [
                    jnp.where(mask, weight[g : g + 1], 0.0),
                    jnp.where(mask, wa[g : g + 1], 0.0),
                    jnp.where(mask, wb[g : g + 1], 0.0),
                ],
                axis=0,
            ).astype(bf16)
            z = dot_nt(lhs, e)
            taps_s[rows, :] = z[:16]
            yc_s[rows, :] = z[16:32]
            pc_s[rows, :] = z[32:]
            res = dot(jnp.concatenate([lag0[rows], lag1[rows], m1[rows], x1[rows]], axis=0), e)
            a_rows.append(diag_row(mask, res[:16]))
            d_rows.append(diag_row(mask, res[16:32]))
            m_rows.append(diag_row(mask, res[32:48]))
            x_rows.append(diag_row(mask, res[48:]))
        grad_a = jnp.concatenate(a_rows, axis=0) + decay * local_b * ahead
        grad_d = (
            jnp.concatenate(d_rows, axis=0)
            + float(W) * jnp.exp(-float(W + 1) * rate) * ahead * back
            + decay * ahead * jnp.concatenate(m_rows, axis=0)
            + decay * back * jnp.concatenate(x_rows, axis=0)
        )
        skip_sum = jnp.sum(xf * mf, axis=1, keepdims=True)
        skip_row = jnp.sum(jnp.where(eye, skip_sum, 0.0), axis=0, keepdims=True)
        skip_part = jnp.concatenate(
            [jnp.broadcast_to(skip_row, (16, W)), jnp.zeros((16, W), f32)], axis=1
        )
        grad_ref[i] = jnp.concatenate([grad_a, grad_d, skip_part], axis=0).astype(bf16)
        skip_gain = jnp.sum(
            jnp.where(eye, par_ref[i, 16:17, :W], 0.0), axis=1, keepdims=True
        )
        spec_h = dot(taps_s[...].astype(bf16), fwd_ref[...])
        y = dot(cmul(spec_x, spec_h), inv_ref[...]) + yc_s[...] + skip_gain * xf
        p = (
            dot(cmul(spec_m, spec_h), invr_ref[...])
            + dot(pc_s[...].astype(bf16), flip_ref[...])
            + skip_gain * mf
        )
        mixed = y.astype(bf16)
        pgrad = p.astype(bf16)
        gated_ref[sl, :] = mul16(q, mixed)
        gq_ref[sl, :] = mul16(c, mixed)
        gk_ref[sl, :] = mul16(pgrad, v)
        gv_ref[sl, :] = mul16(pgrad, k)
        return carry

    lax.fori_loop(0, grad_ref.shape[0], step, 0)


def body(query, key_in, value_in, cotangent, residue, log_rate, bias):
    shards = lax.axis_size("ctx")
    channels, width = query.shape
    fwd, fwdr, inv, invr, flip = tables()
    rate = jnp.exp(log_rate)
    root = jnp.sqrt(-jnp.expm1(-2.0 * rate))
    rate_rows = rate.reshape(HALF, LANES)
    weight_rows = (residue * root).reshape(HALF, LANES)
    bias_rows = jnp.pad(bias.reshape(1, W), ((0, 7), (0, LANES - W)))
    own_par = jnp.concatenate([rate_rows, weight_rows, bias_rows], axis=0)
    par = lax.all_gather(own_par, "ctx")

    sub = 4
    block = sub * 128
    grid = (channels // block,)
    data = pl.BlockSpec((block, width), lambda i: (i, 0))
    rows24 = pl.BlockSpec((sub, 24, LANES), lambda i: (i, 0, 0))
    rows16 = pl.BlockSpec((sub, 16, LANES), lambda i: (i, 0, 0))
    rows32 = pl.BlockSpec((sub, 32, LANES), lambda i: (i, 0, 0))
    whole = lambda r, c: pl.BlockSpec((r, c), lambda i: (0, 0))
    params = pltpu.CompilerParams(vmem_limit_bytes=48 * 1024 * 1024)

    own_states = pl.pallas_call(
        states_kernel,
        grid=grid,
        in_specs=[data] * 4 + [rows24, whole(W, W)],
        out_specs=rows16,
        out_shape=jax.ShapeDtypeStruct((shards, 16, LANES), bf16),
        compiler_params=params,
        name="states",
    )(query, key_in, value_in, cotangent, par, flip)

    gathered = lax.all_to_all(own_states, "ctx", split_axis=0, concat_axis=0, tiled=True)
    scanned = pl.pallas_call(
        scan_kernel,
        out_shape=jax.ShapeDtypeStruct((shards, 16, LANES), bf16),
        scratch_shapes=[pltpu.VMEM((shards, HALF, LANES), f32)],
        compiler_params=params,
        name="scan",
    )(gathered, rate_rows)
    states = lax.all_to_all(scanned, "ctx", split_axis=0, concat_axis=0, tiled=True)

    out = jax.ShapeDtypeStruct((channels, width), bf16)
    gated, gq, gk, gv, grads = pl.pallas_call(
        mix_kernel,
        grid=grid,
        in_specs=[data] * 4
        + [rows24, rows16, rows16, whole(W, 2 * W), whole(W, 2 * W), whole(2 * W, W),
           whole(2 * W, W), whole(W, W)],
        out_specs=[data] * 4 + [rows32],
        out_shape=[out] * 4 + [jax.ShapeDtypeStruct((shards, 32, LANES), bf16)],
        scratch_shapes=[pltpu.VMEM((W, W), f32)] * 3,
        compiler_params=params,
        name="mix",
    )(query, key_in, value_in, cotangent, par, own_states, states, fwd, fwdr, inv, invr, flip)

    parts = lax.all_to_all(grads, "ctx", split_axis=0, concat_axis=0, tiled=True)
    total = lax.psum(jnp.sum(parts.astype(f32), axis=0)[:24], "dp")
    modes = residue.shape[1]
    grad_a = total[:HALF].reshape(-1, modes)
    grad_d = total[HALF:16].reshape(-1, modes)
    scale = 1.0 / math.sqrt(float(shards * width * lax.axis_size("dp")))
    grad_residue = root * grad_a * scale
    grad_rate = rate * residue * (jnp.exp(-2.0 * rate) / root * grad_a - root * grad_d) * scale
    grad_bias = total[16, :W] * scale
    return gated, gq, gk, gv, grad_residue, grad_rate, grad_bias


def solution(mesh):
    tok = P(None, ("dp", "ctx"))
    chan = P("ctx", None)
    return jax.shard_map(
        body,
        mesh=mesh,
        in_specs=(tok, tok, tok, tok, chan, chan, P("ctx")),
        out_specs=(tok, tok, tok, tok, chan, chan, P("ctx")),
        check_vma=False,
    )
```

time: 1210 us -> 281 us (0.23)
  other arithmetic: 608 us -> 3.36 us
  matrix products: 389 us -> 0 us
  Pallas kernels: 0 us -> 82.8 us
  local copies, waits for them, and re-layouts: 56 us -> 4.45 us
  waiting for transfers between devices: 57.4 us -> 106 us
  starting transfers between devices: 20.5 us -> 0.04 us
  between operations: 1.1 us -> 14.2 us
    reduce_sum x48 -> x1, other arithmetic: 567 us -> 0.17 us  [body(): total = lax.psum(jnp.sum(parts.astype(f32), axis=0)[:24], 'dp')]
    dot_general x448 -> x0, matrix products: 389 us -> none  [the longest x32 54.1 us: inverse_real(): jnp.einsum('kp,cks->cps', first_sin, turned_im, precision=precise)]
    all_gather x0 -> x1, waiting for transfers between devices: none -> 106 us  [body(): par = lax.all_gather(own_par, 'ctx')]
    pallas_call x0 -> x3, Pallas kernels: none -> 82.8 us  [the longest x1 58.5 us: body(): pl.pallas_call(mix_kernel, grid=grid, in_specs=[data] * 4 + [rows24, rows...]
    all_to_all x3 -> x0, waiting for transfers between devices: 57.4 us -> none  [the longest x1 28.8 us: body(): lax.all_to_all(mixed_grad, 'ctx', split_axis=0, concat_axis=1, tiled=True)]
    dynamic_update_slice x32 -> x0, local copies, waits for them, and re-layouts: 34.3 us -> none  [the longest x16 20.7 us: body(): lax.map(backward_block, (signal_blocks, blocked(grad_chan), spec_re, spec...]
    all_to_all x1 -> x3, blocking collectives: 33.8 us -> 58.2 us  [the longest x1 22.6 us: body(): lax.all_to_all(grads, 'ctx', split_axis=0, concat_axis=0, tiled=True)]
    sin x64 -> x0, other arithmetic: 23.3 us -> none  [the longest x32 14.5 us: make_tables(): jnp.sin(0.5 * omega_angle)]
  transfers between devices with their start and end apart: 3 -> 1, of which waited for: 2 -> 1; matrix products, arithmetic and copies ran while one was open for 0% -> 0% of each run, Pallas kernels for 0% -> 0%
where the time goes in v1:
time: 281 us; the launch traced here: 280 us
  waiting for transfers between devices  106 us (38%)
  Pallas kernels  82.8 us (29%)
  blocking collectives  69.3 us (25%)
  between operations  14.2 us (5%)
  local copies, waits for them, and re-layouts  4.45 us (2%)
  other arithmetic  3.36 us (1%)
    all_gather x1, waiting for transfers between devices, body(): par = lax.all_gather(own_par, 'ctx')  106 us
    pallas_call x1, Pallas kernels, body(): pl.pallas_call(mix_kernel, grid=grid, in_specs=[data] * 4 + [rows24, rows...  58.5 us
    pallas_call x1, Pallas kernels, body(): pl.pallas_call(states_kernel, grid=grid, in_specs=[data] * 4 + [rows24, w...  23.5 us
    all_to_all x1, blocking collectives, body(): lax.all_to_all(grads, 'ctx', split_axis=0, concat_axis=0, tiled=True)  22.6 us
    all_to_all x1, blocking collectives, body(): lax.all_to_all(own_states, 'ctx', split_axis=0, concat_axis=0, tiled=True)  18.6 us
    all_to_all x1, blocking collectives, body(): lax.all_to_all(scanned, 'ctx', split_axis=0, concat_axis=0, tiled=True)  17 us
    psum x1, blocking collectives, body(): total = lax.psum(jnp.sum(parts.astype(f32), axis=0)[:24], 'dp')  11.2 us
  transfers between devices with their start and end apart: 1, of which 1 were waited for; matrix products, arithmetic and copies ran while one was open for 0% of the time, Pallas kernels for 0%

profile of v1, /device:TPU:0, one launch (start us, length us, event | category | flops | bytes accessed | tf_op | source)
XLA Modules:
  0.0 280.0 jit_solution(5089452412517684705)
XLA Ops:
  7.2 0.0 all-gather.3.cloned.1.call-start
  7.2 0.7 fusion.3
  8.0 0.1 copy.26
  8.1 0.1 reshape.31.rate_ref
  8.1 0.1 copy.27
  8.2 0.1 reshape.32
  8.3 1.3 select_maximum_fusion
  9.6 0.0 all-gather.3.cloned.1.call-update
  9.6 105.9 %all-gather.3.cloned.1.call-done = f32[1536,256]{1,0:T(8,128)} async-done(((f32[24,256]{1,0:T(8,128)}), f32[1536,256]{1,0:T(8,128)}) %all-gather.3.cloned.1.call-update) | async-done | bytes 1572880 | tf_op jit(solution)/shard_map/all_gather | solution.py:201
  115.5 1.6 copy-done
  117.1 1.4 copy-done.2
  118.5 0.8 copy-done.3
  119.3 23.5 %states.1.own_ref = bf16[64,16,256]{2,1,0:T(8,128)(2,1)S(1)} custom-call(bf16[8192,128]{1,0:T(8,128)(2,1)S(1)} %copy-done, bf16[8192,128]{1,0:T(8,128)(2,1)} %k_ref.3, bf16[8192,128]{1,0:T(8,128)(2,1)} %v_ref.3, bf16[8192,128]{1,0:T(8,128)(2,1)} %c_ref.3, f32[64,24,256]{2,1,0:T(8,128)S(1)} %bitcast.4, bf16[128,128]{1,0:T(8,128)(2,1)S(1)} %copy-done.3), custom_call_target="tpu_custom_call" | custom-call | tf_op jit(solution)/shard_map/states/pallas_call | solution.py:213
  142.8 0.0 copy-start.1
  142.8 0.0 copy-start.4
  142.8 0.0 copy-start.5
  142.8 0.0 copy-start.6
  142.9 0.0 copy-start.7
  142.9 18.6 %all_to_all.15.st_ref = bf16[64,16,256]{2,1,0:T(8,128)(2,1)S(1)} all-to-all(bf16[64,16,256]{2,1,0:T(8,128)(2,1)S(1)} %states.1.own_ref), channel_id=1, replica_groups=mesh['dp'=2,'ctx'=64] {'ctx'}, dimensions={0} | all-to-all | bytes 1048576 | tf_op jit(solution)/shard_map/all_to_all | solution.py:223
  161.5 0.7 scan.1
  162.2 17.0 %all_to_all.16.st_ref = bf16[64,16,256]{2,1,0:T(8,128)(2,1)S(1)} all-to-all(bf16[64,16,256]{2,1,0:T(8,128)(2,1)S(1)} %scan.1), channel_id=1, replica_groups=mesh['dp'=2,'ctx'=64] {'ctx'}, dimensions={0} | all-to-all | bytes 1048576 | tf_op jit(solution)/shard_map/all_to_all | solution.py:231
  179.2 0.0 copy-done.4
  179.2 58.5 %mix.1 = (bf16[8192,128]{1,0:T(8,128)(2,1)}, bf16[8192,128]{1,0:T(8,128)(2,1)}, bf16[8192,128]{1,0:T(8,128)(2,1)}, bf16[8192,128]{1,0:T(8,128)(2,1)}, bf16[64,32,256]{2,1,0:T(8,128)(2,1)S(1)}) custom-call(bf16[8192,128]{1,0:T(8,128)(2,1)S(1)} %copy-done.1, bf16[8192,128]{1,0:T(8,128)(2,1)} %k_ref.3, bf16[8192,128]{1,0:T(8,128)(2,1)} %v_ref.3, ...), custom_call_target="tpu_custom_call" | custom-call | tf_op jit(solution)/shard_map/mix/pallas_call | solution.py:234
  237.8 22.6 %all_to_all.17 = bf16[64,32,256]{2,1,0:T(8,128)(2,1)S(1)} all-to-all(bf16[64,32,256]{2,1,0:T(8,128)(2,1)S(1)} %get-tuple-element.16), channel_id=1, replica_groups=mesh['dp'=2,'ctx'=64] {'ctx'}, dimensions={0} | all-to-all | bytes 2097152 | tf_op jit(solution)/shard_map/all_to_all | solution.py:247
  260.4 0.2 convert_reduce_fusion
  260.5 11.2 %psum.7 = f32[24,256]{1,0:T(8,128)S(1)} all-reduce(f32[24,256]{1,0:T(8,128)S(1)} %slice.16), channel_id=1, replica_groups=mesh['dp'=2,'ctx'=64] {'dp'}, use_global_device_ids=true, to_apply=%region_1.2 | all-reduce | flops 6144 | bytes 49152 | tf_op jit(solution)/shard_map/psum | solution.py:248
  271.7 0.5 fusion.1
  272.2 0.1 reshape.35
  272.3 0.1 copy.30
  272.4 0.1 reshape.34
  272.5 0.1 copy.28
  272.5 0.7 multiply_multiply_fusion
  (13 shorter events, 0.0 us)
Async XLA Ops:
  7.2 108.3 %all-gather.3.cloned.1.call-start = ((), (), s32[]{:S(2)}) async-start(), calls=%async_computation.3 | async-start | bytes 1597440 | tf_op jit(solution)/shard_map/all_gather | solution.py:201
  115.5 1.6 copy-start
  117.1 1.4 copy-start.2
  118.5 0.8 copy-start.3
  142.8 36.4 %copy-start.1 = (bf16[8192,128]{1,0:T(8,128)(2,1)S(1)}, bf16[8192,128]{1,0:T(8,128)(2,1)}, u32[]{:S(2)}) copy-start(bf16[8192,128]{1,0:T(8,128)(2,1)} %q_ref.3) | copy-start | bytes 6291460
  142.8 36.4 %copy-start.4 = (bf16[256,128]{1,0:T(8,128)(2,1)S(1)}, bf16[256,128]{1,0:T(8,128)(2,1)}, u32[]{:S(2)}) copy-start(bf16[256,128]{1,0:T(8,128)(2,1)} %constant.30.invr_ref) | copy-start | bytes 196612
  142.8 36.4 %copy-start.5 = (bf16[256,128]{1,0:T(8,128)(2,1)S(1)}, bf16[256,128]{1,0:T(8,128)(2,1)}, u32[]{:S(2)}) copy-start(bf16[256,128]{1,0:T(8,128)(2,1)} %constant.29.inv_ref) | copy-start | bytes 196612
  142.8 36.4 %copy-start.6 = (bf16[128,256]{1,0:T(8,128)(2,1)S(1)}, bf16[128,256]{1,0:T(8,128)(2,1)}, u32[]{:S(2)}) copy-start(bf16[128,256]{1,0:T(8,128)(2,1)} %constant.28.fwdr_ref) | copy-start | bytes 196612
  142.9 36.4 %copy-start.7 = (bf16[128,256]{1,0:T(8,128)(2,1)S(1)}, bf16[128,256]{1,0:T(8,128)(2,1)}, u32[]{:S(2)}) copy-start(bf16[128,256]{1,0:T(8,128)(2,1)} %constant.27.fwd_ref) | copy-start | bytes 196612
  237.8 34.7 %copy-start.8 = (f32[128,16]{0,1:T(8,128)S(1)}, f32[128,16]{0,1:T(8,128)}, u32[]{:S(2)}) copy-start(f32[128,16]{0,1:T(8,128)} %param.17) | copy-start | bytes 24580
  237.8 34.7 %copy-start.9 = (f32[128,16]{0,1:T(8,128)S(1)}, f32[128,16]{0,1:T(8,128)}, u32[]{:S(2)}) copy-start(f32[128,16]{0,1:T(8,128)} %param.16) | copy-start | bytes 24580
Sparse Core Ops, SparseCore 0:
  10.3 105.1 all-gather.2

commit v2 on v1

--- a/solution.py
+++ b/solution.py
@@ -56,6 +56,11 @@
     return jnp.sum(jnp.where(mask, rows, 0.0), axis=0, keepdims=True)
 
 
+def get_par(par_ref, i):
+    rows = par_ref[lax.rem(i, 2), lax.div(i, 2)].astype(f32)
+    return rows[:8] + rows[8:16], rows[16:24], rows[24:25, :W] + rows[25:26, :W]
+
+
 def mul16(a, b):
     return (a.astype(f32) * b.astype(f32)).astype(bf16)
 
@@ -69,8 +74,9 @@
         m = mul16(c_ref[sl, :], q_ref[sl, :])
         xr = dot(x, flip_ref[...]).astype(bf16)
         ahead, back = [], []
+        rate = get_par(par_ref, i)[0]
         for g in range(HALF):
-            e = powers(par_ref[i, g : g + 1, :])
+            e = powers(rate[g : g + 1])
             rows = slice(16 * g, 16 * g + 16)
             res = dot(jnp.concatenate([xr[rows], m[rows]], axis=0), e)
             ahead.append(diag_row(mask, res[:16]))
@@ -81,22 +87,132 @@
     lax.fori_loop(0, out_ref.shape[0], step, 0)
 
 
-def scan_kernel(st_ref, rate_ref, out_ref, hold):
+def peer_of(me, d, count):
+    return lax.rem(me + d, count)
+
+
+def greet(offsets, me, count, extra=()):
+    barrier = pltpu.get_barrier_semaphore()
+    first, stop, step = offsets
+
+    def tell(i, carry):
+        pl.semaphore_signal(
+            barrier, inc=1, device_id={"ctx": peer_of(me, first + i * step, count)},
+            device_id_type=pl.DeviceIdType.MESH,
+        )
+        return carry
+
+    number = (stop - first) // step
+    lax.fori_loop(0, number, tell, 0)
+    for who in extra:
+        pl.semaphore_signal(barrier, inc=1, device_id=who, device_id_type=pl.DeviceIdType.MESH)
+    pl.semaphore_wait(barrier, number + len(extra))
+
+
+def start_all(src, dst, me, count, send_sem, recv_sem, local_sem):
+    def send(d, carry):
+        peer = peer_of(me, d, count)
+        pltpu.make_async_remote_copy(
+            src_ref=src.at[peer], dst_ref=dst.at[me], send_sem=send_sem, recv_sem=recv_sem,
+            device_id={"ctx": peer}, device_id_type=pl.DeviceIdType.MESH,
+        ).start()
+        return carry
+
+    lax.fori_loop(1, count, send, 0)
+    return pltpu.make_async_copy(src.at[me], dst.at[me], local_sem)
+
+
+def wait_bytes(ref, sem):
+    pltpu.make_async_copy(ref, ref, sem).wait()
+
+
+def gather_kernel(own_ref, out_ref, send_sem, recv_sem, pair_sem, local_sem):
+    count = 2 * out_ref.shape[1]
+    me = lax.axis_index("ctx")
+    core, chip = lax.rem(me, 2), lax.div(me, 2)
+    other = me + 1 - 2 * core
+    greet((2, count, 2), me, count, extra=({"ctx": other},))
+
+    def send(d, carry):
+        peer = peer_of(me, 2 * d, count)
+        pltpu.make_async_remote_copy(
+            src_ref=own_ref, dst_ref=out_ref.at[core, chip], send_sem=send_sem, recv_sem=recv_sem,
+            device_id={"ctx": peer}, device_id_type=pl.DeviceIdType.MESH,
+        ).start()
+        return carry
+
+    chips = out_ref.shape[1]
+    lax.fori_loop(1, chips, send, 0)
+    keep = pltpu.make_async_copy(own_ref, out_ref.at[core, chip], local_sem)
+    keep.start()
+    keep.wait()
+    some = out_ref.at[0, pl.ds(0, chips - 1)]
+    wait_bytes(some, recv_sem)
+    across = pltpu.make_async_remote_copy(
+        src_ref=out_ref.at[core], dst_ref=out_ref.at[core], send_sem=pair_sem.at[0],
+        recv_sem=pair_sem.at[1], device_id={"ctx": other}, device_id_type=pl.DeviceIdType.MESH,
+    )
+    across.start()
+    wait_bytes(some, send_sem)
+    across.wait()
+
+
+def scan_kernel(
+    st_ref, rate_ref, out_ref, came, ready, hold, send_sem, recv_sem, local_sem
+):
     parts = st_ref.shape[0]
+    me = lax.axis_index("ctx")
+    greet((1, parts, 1), me, parts)
+    keep = start_all(st_ref, came, me, parts, send_sem.at[0], recv_sem.at[0], local_sem.at[0])
+    keep.start()
+    keep.wait()
+    rest = came.at[pl.ds(0, parts - 1)]
+    wait_bytes(rest, recv_sem.at[0])
     decay = jnp.exp(-float(W) * rate_ref[...])
 
     def ahead(p, s):
         hold[p] = s
-        return s * decay + st_ref[p].astype(f32)[:HALF]
+        return s * decay + came[p].astype(f32)[:HALF]
 
     lax.fori_loop(0, parts, ahead, jnp.zeros((HALF, LANES), f32))
 
     def back(i, s):
         p = parts - 1 - i
-        out_ref[p] = jnp.concatenate([hold[p], s], axis=0).astype(bf16)
-        return s * decay + st_ref[p].astype(f32)[HALF:]
+        ready[p] = jnp.concatenate([hold[p], s], axis=0).astype(bf16)
+        return s * decay + came[p].astype(f32)[HALF:]
 
     lax.fori_loop(0, parts, back, jnp.zeros((HALF, LANES), f32))
+    keep = start_all(ready, out_ref, me, parts, send_sem.at[1], recv_sem.at[1], local_sem.at[1])
+    keep.start()
+    wait_bytes(rest, send_sem.at[0])
+    keep.wait()
+    wait_bytes(out_ref.at[pl.ds(0, parts - 1)], recv_sem.at[1])
+    wait_bytes(rest, send_sem.at[1])
+
+
+def reduce_kernel(
+    grad_ref, out_ref, came, mine, theirs, send_sem, recv_sem, local_sem, pair_sem
+):
+    parts = grad_ref.shape[0]
+    me = lax.axis_index("ctx")
+    twin = {"dp": 1 - lax.axis_index("dp")}
+    greet((1, parts, 1), me, parts, extra=(twin,))
+    keep = start_all(grad_ref, came, me, parts, send_sem, recv_sem, local_sem)
+    keep.start()
+    keep.wait()
+    rest = came.at[pl.ds(0, parts - 1)]
+    wait_bytes(rest, recv_sem)
+    mine[...] = lax.fori_loop(
+        0, parts, lambda p, s: s + came[p].astype(f32), jnp.zeros(came.shape[1:], f32)
+    )
+    swap = pltpu.make_async_remote_copy(
+        src_ref=mine, dst_ref=theirs, send_sem=pair_sem.at[0], recv_sem=pair_sem.at[1],
+        device_id=twin, device_id_type=pl.DeviceIdType.MESH,
+    )
+    swap.start()
+    wait_bytes(rest, send_sem)
+    swap.wait()
+    out_ref[...] = mine[...] + theirs[...]
 
 
 def cmul(a, b):
@@ -125,8 +241,7 @@
         lag1 = (lag * lag_no).astype(bf16)
         m1 = (mf * (lag_no + 1.0)).astype(bf16)
         x1 = (xr * lag_no).astype(bf16)
-        rate = par_ref[i, 0:8, :]
-        weight = par_ref[i, 8:16, :]
+        rate, weight, bias_row = get_par(par_ref, i)
         state = st_ref[i].astype(f32)
         ahead, back = state[:HALF], state[HALF:]
         local_b = own_ref[i].astype(f32)[HALF:]
@@ -168,7 +283,7 @@
         )
         grad_ref[i] = jnp.concatenate([grad_a, grad_d, skip_part], axis=0).astype(bf16)
         skip_gain = jnp.sum(
-            jnp.where(eye, par_ref[i, 16:17, :W], 0.0), axis=1, keepdims=True
+            jnp.where(eye, bias_row, 0.0), axis=1, keepdims=True
         )
         spec_h = dot(taps_s[...].astype(bf16), fwd_ref[...])
         y = dot(cmul(spec_x, spec_h), inv_ref[...]) + yc_s[...] + skip_gain * xf
@@ -196,15 +311,42 @@
     root = jnp.sqrt(-jnp.expm1(-2.0 * rate))
     rate_rows = rate.reshape(HALF, LANES)
     weight_rows = (residue * root).reshape(HALF, LANES)
-    bias_rows = jnp.pad(bias.reshape(1, W), ((0, 7), (0, LANES - W)))
-    own_par = jnp.concatenate([rate_rows, weight_rows, bias_rows], axis=0)
-    par = lax.all_gather(own_par, "ctx")
+    bias_row = jnp.pad(bias.reshape(1, W), ((0, 0), (0, LANES - W)))
+    upper = lambda z: lax.reduce_precision(z, 8, 7)
+    own_par = jnp.concatenate(
+        [
+            rate_rows,
+            rate_rows - upper(rate_rows),
+            weight_rows,
+            bias_row,
+            bias_row - upper(bias_row),
+            jnp.zeros((6, LANES), f32),
+        ],
+        axis=0,
+    ).astype(bf16)
+    vmem = pl.BlockSpec(memory_space=pltpu.VMEM)
+    dma = pltpu.SemaphoreType.DMA
+
+    def remote(number):
+        return pltpu.CompilerParams(
+            collective_id=number, has_side_effects=True, vmem_limit_bytes=24 * 1024 * 1024
+        )
+
+    par = pl.pallas_call(
+        gather_kernel,
+        in_specs=[vmem],
+        out_specs=vmem,
+        out_shape=jax.ShapeDtypeStruct((2, shards // 2, 32, LANES), bf16),
+        scratch_shapes=[dma, dma, dma((2,)), dma],
+        compiler_params=remote(1),
+        name="gather",
+    )(own_par)
 
     sub = 4
     block = sub * 128
     grid = (channels // block,)
     data = pl.BlockSpec((block, width), lambda i: (i, 0))
-    rows24 = pl.BlockSpec((sub, 24, LANES), lambda i: (i, 0, 0))
+    rows_par = pl.BlockSpec((2, sub // 2, 32, LANES), lambda i: (0, i, 0, 0))
     rows16 = pl.BlockSpec((sub, 16, LANES), lambda i: (i, 0, 0))
     rows32 = pl.BlockSpec((sub, 32, LANES), lambda i: (i, 0, 0))
     whole = lambda r, c: pl.BlockSpec((r, c), lambda i: (0, 0))
@@ -213,29 +355,36 @@
     own_states = pl.pallas_call(
         states_kernel,
         grid=grid,
-        in_specs=[data] * 4 + [rows24, whole(W, W)],
+        in_specs=[data] * 4 + [rows_par, whole(W, W)],
         out_specs=rows16,
         out_shape=jax.ShapeDtypeStruct((shards, 16, LANES), bf16),
         compiler_params=params,
         name="states",
     )(query, key_in, value_in, cotangent, par, flip)
 
-    gathered = lax.all_to_all(own_states, "ctx", split_axis=0, concat_axis=0, tiled=True)
-    scanned = pl.pallas_call(
+    states = pl.pallas_call(
         scan_kernel,
+        in_specs=[vmem, vmem],
+        out_specs=vmem,
         out_shape=jax.ShapeDtypeStruct((shards, 16, LANES), bf16),
-        scratch_shapes=[pltpu.VMEM((shards, HALF, LANES), f32)],
-        compiler_params=params,
+        scratch_shapes=[
+            pltpu.VMEM((shards, 16, LANES), bf16),
+            pltpu.VMEM((shards, 16, LANES), bf16),
+            pltpu.VMEM((shards, HALF, LANES), f32),
+            dma((2,)),
+            dma((2,)),
+            dma((2,)),
+        ],
+        compiler_params=remote(2),
         name="scan",
-    )(gathered, rate_rows)
-    states = lax.all_to_all(scanned, "ctx", split_axis=0, concat_axis=0, tiled=True)
+    )(own_states, rate_rows)
 
     out = jax.ShapeDtypeStruct((channels, width), bf16)
     gated, gq, gk, gv, grads = pl.pallas_call(
         mix_kernel,
         grid=grid,
         in_specs=[data] * 4
-        + [rows24, rows16, rows16, whole(W, 2 * W), whole(W, 2 * W), whole(2 * W, W),
+        + [rows_par, rows16, rows16, whole(W, 2 * W), whole(W, 2 * W), whole(2 * W, W),
            whole(2 * W, W), whole(W, W)],
         out_specs=[data] * 4 + [rows32],
         out_shape=[out] * 4 + [jax.ShapeDtypeStruct((shards, 32, LANES), bf16)],
@@ -244,8 +393,23 @@
         name="mix",
     )(query, key_in, value_in, cotangent, par, own_states, states, fwd, fwdr, inv, invr, flip)
 
-    parts = lax.all_to_all(grads, "ctx", split_axis=0, concat_axis=0, tiled=True)
-    total = lax.psum(jnp.sum(parts.astype(f32), axis=0)[:24], "dp")
+    total = pl.pallas_call(
+        reduce_kernel,
+        in_specs=[vmem],
+        out_specs=vmem,
+        out_shape=jax.ShapeDtypeStruct((32, LANES), f32),
+        scratch_shapes=[
+            pltpu.VMEM((shards, 32, LANES), bf16),
+            pltpu.VMEM((32, LANES), f32),
+            pltpu.VMEM((32, LANES), f32),
+            dma,
+            dma,
+            dma,
+            dma((2,)),
+        ],
+        compiler_params=remote(3),
+        name="reduce",
+    )(grads)
     modes = residue.shape[1]
     grad_a = total[:HALF].reshape(-1, modes)
     grad_d = total[HALF:16].reshape(-1, modes)

time: 281 us -> 158 us (0.56)
  waiting for transfers between devices: 106 us -> 0 us
  blocking collectives: 69.3 us -> 0 us
  Pallas kernels: 82.8 us -> 149 us
  between operations: 14.2 us -> 0.79 us
    all_gather x1 -> x0, waiting for transfers between devices: 106 us -> none  [body(): par = lax.all_gather(own_par, 'ctx')]
    pallas_call x3 -> x5, Pallas kernels: 82.8 us -> 149 us  [the longest x1 59.1 us: body(): pl.pallas_call(mix_kernel, grid=grid, in_specs=[data] * 4 + [rows_par, ro...]
    all_to_all x3 -> x0, blocking collectives: 58.2 us -> none  [the longest x1 22.6 us: body(): lax.all_to_all(grads, 'ctx', split_axis=0, concat_axis=0, tiled=True)]
    psum x1 -> x0, blocking collectives: 11.2 us -> none  [body(): total = lax.psum(jnp.sum(parts.astype(f32), axis=0)[:24], 'dp')]
  transfers between devices with their start and end apart: 1 -> 0, of which waited for: 1 -> 0; matrix products, arithmetic and copies ran while one was open for 0% -> 0% of each run, Pallas kernels for 0% -> 0%
where the time goes in v2:
time: 158 us
  Pallas kernels  149 us (94%)
  local copies, waits for them, and re-layouts  5.36 us (3%)
  other arithmetic  2.58 us (2%)
    pallas_call x1, Pallas kernels, body(): pl.pallas_call(mix_kernel, grid=grid, in_specs=[data] * 4 + [rows_par, ro...  59.1 us
    pallas_call x1, Pallas kernels, body(): pl.pallas_call(reduce_kernel, in_specs=[vmem], out_specs=vmem, out_shape=...  25.6 us
    pallas_call x1, Pallas kernels, body(): pl.pallas_call(scan_kernel, in_specs=[vmem, vmem], out_specs=vmem, out_sh...  24.2 us
    pallas_call x1, Pallas kernels, body(): pl.pallas_call(states_kernel, grid=grid, in_specs=[data] * 4 + [rows_par,...  23.7 us
    pallas_call x1, Pallas kernels, body(): pl.pallas_call(gather_kernel, in_specs=[vmem], out_specs=vmem, out_shape=...  16.4 us
    unnamed x20, local copies, waits for them, and re-layouts  3.97 us

profile of v2, /device:TPU:0, one launch (start us, length us, event | category | flops | bytes accessed | tf_op | source)
XLA Modules:
  0.0 157.6 jit_solution(10993233896665265243)
XLA Ops:
  0.6 0.7 fusion.1
  1.3 0.7 pad_convert_fusion
  2.0 0.7 multiply_convert_fusion
  2.7 0.1 copy.30
  2.8 0.1 reshape.33
  2.9 0.1 copy.29
  3.0 0.1 reshape.32.rate_ref
  3.2 16.4 %gather.1.par_ref = bf16[2,32,32,256]{3,2,1,0:T(8,128)(2,1)S(1)} custom-call(bf16[32,256]{1,0:T(8,128)(2,1)S(1)} %concatenate.4.own_ref), custom_call_target="tpu_custom_call" | custom-call | tf_op jit(solution)/shard_map/gather/pallas_call | solution.py:335
  19.6 0.0 copy-start
  19.6 1.6 %copy-done = bf16[8192,128]{1,0:T(8,128)(2,1)S(1)} copy-done((bf16[8192,128]{1,0:T(8,128)(2,1)S(1)}, bf16[8192,128]{1,0:T(8,128)(2,1)}, u32[]{:S(2)}) %copy-start) | copy-done | bytes 2097176
  21.2 1.6 %copy-done.1 = bf16[8192,128]{1,0:T(8,128)(2,1)S(1)} copy-done((bf16[8192,128]{1,0:T(8,128)(2,1)S(1)}, bf16[8192,128]{1,0:T(8,128)(2,1)}, u32[]{:S(2)}) %copy-start.1) | copy-done | bytes 2097176
  22.8 0.8 copy-done.2
  23.6 0.0 copy-start.7
  23.6 23.7 %states.1.st_ref.own_ref = bf16[64,16,256]{2,1,0:T(8,128)(2,1)S(1)} custom-call(bf16[8192,128]{1,0:T(8,128)(2,1)S(1)} %copy-done, bf16[8192,128]{1,0:T(8,128)(2,1)S(1)} %copy-done.1, bf16[8192,128]{1,0:T(8,128)(2,1)} %v_ref.3, bf16[8192,128]{1,0:T(8,128)(2,1)} %c_ref.3, bf16[2,32,32,256]{3,2,1,0:T(8,128)(2,1)S(1)} %gather.1.par_ref, ...), custom_call_target="tpu_custom_call" | custom-call | tf_op jit(solution)/shard_map/states/pallas_call | solution.py:355
  47.2 24.2 %scan.1.st_ref = bf16[64,16,256]{2,1,0:T(8,128)(2,1)S(1)} custom-call(bf16[64,16,256]{2,1,0:T(8,128)(2,1)S(1)} %states.1.st_ref.own_ref, f32[8,256]{1,0:T(8,128)S(1)} %reshape.32.rate_ref), custom_call_target="tpu_custom_call" | custom-call | tf_op jit(solution)/shard_map/scan/pallas_call | solution.py:365
  71.4 0.0 copy-done.3
  71.4 0.0 copy-done.4
  71.4 0.0 copy-done.5
  71.4 0.0 copy-done.6
  71.5 0.0 copy-done.7
  71.5 0.0 copy-start.8
  71.5 0.0 copy-start.9
  71.5 59.1 %mix.1 = (bf16[8192,128]{1,0:T(8,128)(2,1)}, bf16[8192,128]{1,0:T(8,128)(2,1)}, bf16[8192,128]{1,0:T(8,128)(2,1)}, bf16[8192,128]{1,0:T(8,128)(2,1)}, bf16[64,32,256]{2,1,0:T(8,128)(2,1)S(1)}) custom-call(bf16[8192,128]{1,0:T(8,128)(2,1)S(1)} %copy-done, bf16[8192,128]{1,0:T(8,128)(2,1)} %k_ref.3, bf16[8192,128]{1,0:T(8,128)(2,1)} %v_ref.3, ...), custom_call_target="tpu_custom_call" | custom-call | tf_op jit(solution)/shard_map/mix/pallas_call | solution.py:383
  130.5 25.6 %reduce.1 = f32[32,256]{1,0:T(8,128)S(1)} custom-call(bf16[64,32,256]{2,1,0:T(8,128)(2,1)S(1)} %get-tuple-element.16.grad_ref), custom_call_target="tpu_custom_call" | custom-call | tf_op jit(solution)/shard_map/reduce/pallas_call | solution.py:396
  156.1 0.5 multiply_bitcast_fusion
  156.7 0.1 reshape.36
  156.7 0.1 copy.33
  156.8 0.1 reshape.35
  156.9 0.1 copy.31
  156.9 0.0 copy-done.8
  157.0 0.0 copy-done.9
  157.0 0.7 multiply_multiply_fusion
  (10 shorter events, 0.1 us)
Async XLA Ops:
  19.6 1.6 %copy-start = (bf16[8192,128]{1,0:T(8,128)(2,1)S(1)}, bf16[8192,128]{1,0:T(8,128)(2,1)}, u32[]{:S(2)}) copy-start(bf16[8192,128]{1,0:T(8,128)(2,1)} %q_ref.3) | copy-start | bytes 6291460
  21.2 1.6 %copy-start.1 = (bf16[8192,128]{1,0:T(8,128)(2,1)S(1)}, bf16[8192,128]{1,0:T(8,128)(2,1)}, u32[]{:S(2)}) copy-start(bf16[8192,128]{1,0:T(8,128)(2,1)} %k_ref.3) | copy-start | bytes 6291460
  22.8 0.8 copy-start.2
  23.5 47.9 %copy-start.3 = (bf16[128,128]{1,0:T(8,128)(2,1)S(1)}, bf16[128,128]{1,0:T(8,128)(2,1)}, u32[]{:S(2)}) copy-start(bf16[128,128]{1,0:T(8,128)(2,1)} %constant.28.flip_ref) | copy-start | bytes 98308
  23.5 47.9 %copy-start.4 = (bf16[256,128]{1,0:T(8,128)(2,1)S(1)}, bf16[256,128]{1,0:T(8,128)(2,1)}, u32[]{:S(2)}) copy-start(bf16[256,128]{1,0:T(8,128)(2,1)} %constant.32.invr_ref) | copy-start | bytes 196612
  23.5 47.9 %copy-start.5 = (bf16[256,128]{1,0:T(8,128)(2,1)S(1)}, bf16[256,128]{1,0:T(8,128)(2,1)}, u32[]{:S(2)}) copy-start(bf16[256,128]{1,0:T(8,128)(2,1)} %constant.31.inv_ref) | copy-start | bytes 196612
  23.5 47.9 %copy-start.6 = (bf16[128,256]{1,0:T(8,128)(2,1)S(1)}, bf16[128,256]{1,0:T(8,128)(2,1)}, u32[]{:S(2)}) copy-start(bf16[128,256]{1,0:T(8,128)(2,1)} %constant.30.fwdr_ref) | copy-start | bytes 196612
  23.6 47.9 %copy-start.7 = (bf16[128,256]{1,0:T(8,128)(2,1)S(1)}, bf16[128,256]{1,0:T(8,128)(2,1)}, u32[]{:S(2)}) copy-start(bf16[128,256]{1,0:T(8,128)(2,1)} %constant.29.fwd_ref) | copy-start | bytes 196612
  71.5 85.5 %copy-start.8 = (f32[128,16]{0,1:T(8,128)S(1)}, f32[128,16]{0,1:T(8,128)}, u32[]{:S(2)}) copy-start(f32[128,16]{0,1:T(8,128)} %param.16) | copy-start | bytes 24580
  71.5 85.5 %copy-start.9 = (f32[128,16]{0,1:T(8,128)S(1)}, f32[128,16]{0,1:T(8,128)}, u32[]{:S(2)}) copy-start(f32[128,16]{0,1:T(8,128)} %param.17) | copy-start | bytes 24580

commit v3 on v1

v3 whole, which is shorter than its diff:
```python
import functools
import math

import jax
import jax.numpy as jnp
import numpy as np
from jax import lax
from jax.experimental import pallas as pl
from jax.experimental.pallas import tpu as pltpu
from jax.sharding import PartitionSpec as P

bf16 = jnp.bfloat16
f32 = jnp.float32
W = 128
HALF = 8
MESH = pl.DeviceIdType.MESH
LANES = 256


def tables():
    n = np.arange(W)[:, None]
    f = np.arange(W)[None, :]
    angle = ((2 * f + 1) * n % (4 * W)) * (2.0 * math.pi / (4 * W))
    fwd = np.concatenate([np.cos(angle), -np.sin(angle)], axis=1)
    inv = fwd.T / W
    flip = np.eye(W)[::-1]
    cast = lambda z: jnp.asarray(np.ascontiguousarray(z), f32).astype(bf16)
    return cast(fwd), cast(fwd[::-1]), cast(inv), cast(inv[:, ::-1]), cast(flip)


def dot(a, b):
    return jnp.dot(a, b, preferred_element_type=f32)


def dot_nt(a, b):
    return lax.dot_general(a, b, (((1,), (1,)), ((), ())), preferred_element_type=f32)


def powers(rate_row):
    rate8 = jnp.broadcast_to(rate_row, (8, LANES))
    row = lax.broadcasted_iota(jnp.int32, (8, LANES), 0).astype(f32)
    out = jnp.exp(-rate8 * row)
    for step in (8, 16, 32, 64):
        mult = jnp.exp(-rate8 * float(step))
        parts = [out[i : i + 8] * mult for i in range(0, step, 8)]
        out = jnp.concatenate([out] + parts, axis=0)
    return out.astype(bf16)


def diag_mask():
    row = lax.broadcasted_iota(jnp.int32, (16, LANES), 0)
    lane = lax.broadcasted_iota(jnp.int32, (16, LANES), 1)
    return row == lane // 16


def diag_row(mask, rows):
    return jnp.sum(jnp.where(mask, rows, 0.0), axis=0, keepdims=True)


def mul16(a, b):
    return (a.astype(f32) * b.astype(f32)).astype(bf16)


def cmul(a, b):
    ar, ai, br, bi = a[:, :W], a[:, W:], b[:, :W], b[:, W:]
    return jnp.concatenate([ar * br - ai * bi, ar * bi + ai * br], axis=1).astype(bf16)


def wait_bytes(ref, sem):
    pltpu.make_async_copy(ref, ref, sem).wait()


def mixer_kernel(
    q_hbm, k_hbm, v_hbm, c_hbm, own_par, own_rate, fwd_ref, fwdr_ref, inv_ref, invr_ref, flip_ref,
    mixed_hbm, pgrad_hbm, total_ref,
    inp, away, sig, rev, lags, skip, par, keep, st_out, came, hold, ready, got, grad_out,
    grad_in, mine, theirs, expand, stage,
    load_sem, par_sem, pair_sem, st_sem, back_sem, grad_sem, out_sem, twin_sem,
):
    chips = q_hbm.shape[0]
    me = lax.axis_index("ctx")
    core, chip = lax.rem(me, 2), lax.div(me, 2)
    near = {"ctx": me + 1 - 2 * core}
    twin = {"dp": 1 - lax.axis_index("dp")}

    def peer(b):
        return {"ctx": 2 * b + core}

    def after(i):
        return lax.rem(chip + i, chips)

    def remote(src, dst, sems, who):
        return pltpu.make_async_remote_copy(
            src_ref=src, dst_ref=dst, send_sem=sems.at[0], recv_sem=sems.at[1],
            device_id=who, device_id_type=MESH,
        )

    for order in range(2):
        side = 1 - core if order == 0 else core
        for n, ref in enumerate((q_hbm, k_hbm, v_hbm, c_hbm)):
            pltpu.make_async_copy(ref.at[:, side], inp.at[order, n], load_sem.at[order]).start()

    barrier = pltpu.get_barrier_semaphore()

    def tell(i, carry):
        pl.semaphore_signal(barrier, inc=1, device_id=peer(after(i)), device_id_type=MESH)
        return carry

    lax.fori_loop(1, chips, tell, 0)
    pl.semaphore_signal(barrier, inc=1, device_id=near, device_id_type=MESH)
    pl.semaphore_signal(barrier, inc=1, device_id=twin, device_id_type=MESH)
    pl.semaphore_wait(barrier, chips + 1)

    def send_par(i, carry):
        remote(own_par, par.at[chip], par_sem, peer(after(i))).start()
        return carry

    lax.fori_loop(1, chips, send_par, 0)
    par[chip] = own_par[...]

    def products(order, dst):
        def step(b, carry):
            dst[0, b] = mul16(inp[order, 1, b], inp[order, 2, b])
            dst[1, b] = mul16(inp[order, 3, b], inp[order, 0, b])
            return carry

        lax.fori_loop(0, chips, step, 0)

    wait_bytes(inp.at[0], load_sem.at[0])
    products(0, away)
    trade = remote(away, sig.at[core], pair_sem, near)
    trade.start()
    wait_bytes(inp.at[1], load_sem.at[1])
    products(1, sig.at[core])
    trade.wait()

    eye = lax.broadcasted_iota(jnp.int32, (W, W), 0) == lax.broadcasted_iota(jnp.int32, (W, W), 1)
    lane = lax.broadcasted_iota(jnp.int32, (W, W), 1).astype(f32)
    mask = diag_mask()

    def local_lags(b, carry):
        x = jnp.concatenate([sig[0, 0, b], sig[1, 0, b]], axis=0)
        m = jnp.concatenate([sig[0, 1, b], sig[1, 1, b]], axis=0)
        xr = dot(x, flip_ref[...]).astype(bf16)
        rev[0, b] = xr[:W]
        rev[1, b] = xr[W:]
        both = dot(cmul(dot(x, fwd_ref[...]), dot(m, fwdr_ref[...])), invr_ref[...])
        lag = both[:W] + both[W:]
        lags[0, b] = lag.astype(bf16)
        lags[1, b] = (lag * lane).astype(bf16)
        xm = x.astype(f32) * m.astype(f32)
        sums = jnp.sum(xm[:W] + xm[W:], axis=1, keepdims=True)
        skip[b] = jnp.broadcast_to(
            jnp.sum(jnp.where(eye, sums, 0.0), axis=0, keepdims=True), (HALF, W)
        )
        return carry

    lax.fori_loop(0, chips, local_lags, 0)
    wait_bytes(par.at[pl.ds(0, chips - 1)], par_sem.at[1])

    def get_rate(b):
        rows = par[b].astype(f32)
        return rows, rows[:8] + rows[8:16]

    def mode_sums(i, carry):
        b = after(i)
        rate = get_rate(b)[1]
        far = jnp.exp(-float(W) * rate)
        parts = [rev[0, b], rev[1, b], sig[0, 1, b], sig[1, 1, b], lags[0, b], lags[1, b]]
        for chunk in range(2):
            parts.append((parts[2 + chunk].astype(f32) * (lane + 1.0)).astype(bf16))
            parts.append((parts[chunk].astype(f32) * lane).astype(bf16))
        found = [[] for _ in parts]
        for g in range(HALF):
            e = powers(rate[g : g + 1])
            rows = slice(16 * g, 16 * g + 16)
            res = dot(jnp.concatenate([part[rows] for part in parts], axis=0), e)
            for n in range(len(parts)):
                found[n].append(diag_row(mask, res[16 * n : 16 * n + 16]))
        found = [jnp.concatenate(rows, axis=0) for rows in found]
        for n in range(len(parts)):
            keep[b, n] = found[n]
        st = jnp.concatenate([found[0] * far + found[1], found[2] + far * found[3]], axis=0)
        st_out[b] = st.astype(bf16)

        @pl.when(i < chips)
        def _():
            remote(st_out.at[b], came.at[chip], st_sem, peer(b)).start()

        return carry

    lax.fori_loop(1, chips + 1, mode_sums, 0)
    came[chip] = st_out[chip]
    wait_bytes(came.at[pl.ds(0, chips - 1)], st_sem.at[1])

    decay2 = jnp.exp(-2.0 * float(W) * own_rate[...])

    def ahead(p, s):
        hold[p] = s
        return s * decay2 + came[p].astype(f32)[:HALF]

    lax.fori_loop(0, chips, ahead, jnp.zeros((HALF, LANES), f32))

    def back(i, s):
        p = chips - 1 - i
        ready[p] = jnp.concatenate([hold[p], s], axis=0).astype(bf16)
        return s * decay2 + came[p].astype(f32)[HALF:]

    lax.fori_loop(0, chips, back, jnp.zeros((HALF, LANES), f32))

    def send_back(i, carry):
        b = after(i)
        remote(ready.at[b], got.at[chip], back_sem, peer(b)).start()
        return carry

    lax.fori_loop(1, chips, send_back, 0)
    got[chip] = ready[chip]
    wait_bytes(got.at[pl.ds(0, chips - 1)], back_sem.at[1])

    def finish(i, carry):
        b = after(i)
        rows, rate = get_rate(b)
        weight = rows[16:24]
        bias_row = rows[24:25, :W] + rows[25:26, :W]
        state = got[b].astype(f32)
        near_decay = jnp.exp(-rate)
        far = jnp.exp(-float(W) * rate)
        s0, r1 = state[:HALF], state[HALF:]
        s1 = far * s0 + keep[b, 0]
        r0 = far * r1 + keep[b, 3]
        grad_a = keep[b, 4] + near_decay * (keep[b, 2] * s0 + keep[b, 3] * s1)
        grad_d = keep[b, 5] + near_decay * (
            float(W) * far * (s0 * r0 + s1 * r1)
            + s0 * keep[b, 6] + r0 * keep[b, 7] + s1 * keep[b, 8] + r1 * keep[b, 9]
        )
        skip_part = jnp.concatenate([skip[b], jnp.zeros((HALF, W), f32)], axis=1)
        grad_out[b] = jnp.concatenate([grad_a, grad_d, skip_part, skip_part], axis=0).astype(bf16)

        @pl.when(i < chips)
        def _():
            remote(grad_out.at[b], grad_in.at[chip], grad_sem, peer(b)).start()

        wa = weight * near_decay
        terms = [weight, wa * s0, wa * s1, wa * r0, wa * r1]
        for g in range(HALF):
            e = powers(rate[g : g + 1])
            lhs = jnp.concatenate(
                [jnp.where(mask, term[g : g + 1], 0.0) for term in terms], axis=0
            ).astype(bf16)
            z = dot_nt(lhs, e)
            for n in range(len(terms)):
                expand[n, 16 * g : 16 * g + 16] = z[16 * n : 16 * n + 16]
        x = jnp.concatenate([sig[0, 0, b], sig[1, 0, b]], axis=0)
        m = jnp.concatenate([sig[0, 1, b], sig[1, 1, b]], axis=0)
        spec_h = dot(expand[0].astype(bf16), fwd_ref[...])
        spec_h = jnp.concatenate([spec_h, spec_h], axis=0)
        gain = jnp.sum(jnp.where(eye, bias_row, 0.0), axis=1, keepdims=True)
        gain = jnp.concatenate([gain, gain], axis=0)
        y = dot(cmul(dot(x, fwd_ref[...]), spec_h), inv_ref[...])
        y += jnp.concatenate([expand[1], expand[2]], axis=0) + gain * x.astype(f32)
        p = dot(cmul(dot(m, fwdr_ref[...]), spec_h), invr_ref[...])
        p += dot(
            jnp.concatenate([expand[3], expand[4]], axis=0).astype(bf16), flip_ref[...]
        ) + gain * m.astype(f32)
        y, p = y.astype(bf16), p.astype(bf16)
        for chunk in range(2):
            stage[chunk, 0, b] = y[W * chunk : W * chunk + W]
            stage[chunk, 1, b] = p[W * chunk : W * chunk + W]
        for n, out in enumerate((mixed_hbm, pgrad_hbm)):
            pltpu.make_async_copy(stage.at[core, n, b], out.at[b, core], out_sem.at[2]).start()
            remote(stage.at[1 - core, n, b], out.at[b, core], out_sem, near).start()
        return carry

    lax.fori_loop(1, chips + 1, finish, 0)

    grad_in[chip] = grad_out[chip]
    wait_bytes(grad_in.at[pl.ds(0, chips - 1)], grad_sem.at[1])
    mine[...] = lax.fori_loop(
        0, chips, lambda p, s: s + grad_in[p].astype(f32), jnp.zeros(grad_in.shape[1:], f32)
    )
    swap = remote(mine, theirs, twin_sem, twin)
    swap.start()
    wait_bytes(own_many(par, chips), par_sem.at[0])
    wait_bytes(own_many(st_out, chips), st_sem.at[0])
    wait_bytes(own_many(ready, chips), back_sem.at[0])
    wait_bytes(own_many(grad_out, chips), grad_sem.at[0])
    for n in range(3):
        wait_bytes(stage.at[0], out_sem.at[n])
    swap.wait()
    total_ref[...] = mine[...] + theirs[...]


def own_many(ref, chips):
    return ref.at[pl.ds(0, chips - 1)]


def body(query, key_in, value_in, cotangent, residue, log_rate, bias):
    shards = lax.axis_size("ctx")
    channels, width = query.shape
    fwd, fwdr, inv, invr, flip = tables()
    rate = jnp.exp(log_rate)
    root = jnp.sqrt(-jnp.expm1(-2.0 * rate))
    rate_rows = rate.reshape(HALF, LANES)
    weight_rows = (residue * root).reshape(HALF, LANES)
    bias_row = jnp.pad(bias.reshape(1, W), ((0, 0), (0, LANES - W)))
    upper = lambda z: lax.reduce_precision(z, 8, 7)
    own_par = jnp.concatenate(
        [
            rate_rows,
            rate_rows - upper(rate_rows),
            weight_rows,
            bias_row,
            bias_row - upper(bias_row),
            jnp.zeros((6, LANES), f32),
        ],
        axis=0,
    ).astype(bf16)
    vmem = pl.BlockSpec(memory_space=pltpu.VMEM)
    dma = pltpu.SemaphoreType.DMA

    def remote(number):
        return pltpu.CompilerParams(
            collective_id=number, has_side_effects=True, vmem_limit_bytes=52 * 1024 * 1024
        )

    chips = shards // 2
    split = lambda z: z.reshape(chips, 2, W, width)
    anywhere = pl.BlockSpec(memory_space=pl.ANY)
    part = jax.ShapeDtypeStruct((chips, 2, W, width), bf16)
    mixed, pgrad, total = pl.pallas_call(
        mixer_kernel,
        in_specs=[anywhere] * 4 + [vmem] * 7,
        out_specs=[anywhere, anywhere, vmem],
        out_shape=[part, part, jax.ShapeDtypeStruct((32, LANES), f32)],
        scratch_shapes=[
            pltpu.VMEM((2, 4, chips, W, W), bf16),
            pltpu.VMEM((2, chips, W, W), bf16),
            pltpu.VMEM((2, 2, chips, W, W), bf16),
            pltpu.VMEM((2, chips, W, W), bf16),
            pltpu.VMEM((2, chips, W, W), bf16),
            pltpu.VMEM((chips, HALF, W), f32),
            pltpu.VMEM((chips, 32, LANES), bf16),
            pltpu.VMEM((chips, 10, HALF, LANES), f32),
            pltpu.VMEM((chips, 16, LANES), bf16),
            pltpu.VMEM((chips, 16, LANES), bf16),
            pltpu.VMEM((chips, HALF, LANES), f32),
            pltpu.VMEM((chips, 16, LANES), bf16),
            pltpu.VMEM((chips, 16, LANES), bf16),
            pltpu.VMEM((chips, 32, LANES), bf16),
            pltpu.VMEM((chips, 32, LANES), bf16),
            pltpu.VMEM((32, LANES), f32),
            pltpu.VMEM((32, LANES), f32),
            pltpu.VMEM((5, W, W), f32),
            pltpu.VMEM((2, 2, chips, W, W), bf16),
            dma((2,)),
            dma((2,)),
            dma((2,)),
            dma((2,)),
            dma((2,)),
            dma((2,)),
            dma((3,)),
            dma((2,)),
        ],
        compiler_params=remote(1),
        name="mixer",
    )(split(query), split(key_in), split(value_in), split(cotangent), own_par, rate_rows,
      fwd, fwdr, inv, invr, flip)
    mixed = mixed.reshape(channels, width)
    pgrad = pgrad.reshape(channels, width)
    gated, gq = mul16(query, mixed), mul16(cotangent, mixed)
    gk, gv = mul16(pgrad, value_in), mul16(pgrad, key_in)

    modes = residue.shape[1]
    grad_a = total[:HALF].reshape(-1, modes)
    grad_d = total[HALF:16].reshape(-1, modes)
    scale = 1.0 / math.sqrt(float(shards * width * lax.axis_size("dp")))
    grad_residue = root * grad_a * scale
    grad_rate = rate * residue * (jnp.exp(-2.0 * rate) / root * grad_a - root * grad_d) * scale
    grad_bias = total[16, :W] * scale
    return gated, gq, gk, gv, grad_residue, grad_rate, grad_bias


def solution(mesh):
    tok = P(None, ("dp", "ctx"))
    chan = P("ctx", None)
    return jax.shard_map(
        body,
        mesh=mesh,
        in_specs=(tok, tok, tok, tok, chan, chan, P("ctx")),
        out_specs=(tok, tok, tok, tok, chan, chan, P("ctx")),
        check_vma=False,
    )
```

time: 281 us -> 92.7 us (0.33)
  waiting for transfers between devices: 106 us -> 0 us
  blocking collectives: 69.3 us -> 0 us
  between operations: 14.2 us -> 0.7 us
  Pallas kernels: 82.8 us -> 76.4 us
  other arithmetic: 3.36 us -> 9.61 us
    all_gather x1 -> x0, waiting for transfers between devices: 106 us -> none  [body(): par = lax.all_gather(own_par, 'ctx')]
    all_to_all x3 -> x0, blocking collectives: 58.2 us -> none  [the longest x1 22.6 us: body(): lax.all_to_all(grads, 'ctx', split_axis=0, concat_axis=0, tiled=True)]
    psum x1 -> x0, blocking collectives: 11.2 us -> none  [body(): total = lax.psum(jnp.sum(parts.astype(f32), axis=0)[:24], 'dp')]
    convert_element_type x0 -> x1, other arithmetic: none -> 7.03 us  [mul16(): return (a.astype(f32) * b.astype(f32)).astype(bf16)]
    pallas_call x3 -> x1, Pallas kernels: 82.8 us -> 76.4 us  [body(): pl.pallas_call(mixer_kernel, in_specs=[anywhere] * 4 + [vmem] * 7, out_sp...]
  transfers between devices with their start and end apart: 1 -> 0, of which waited for: 1 -> 0; matrix products, arithmetic and copies ran while one was open for 0% -> 0% of each run, Pallas kernels for 0% -> 0%
where the time goes in v3:
time: 92.7 us; the launch traced here: 92.3 us
  Pallas kernels  76.4 us (82%)
  other arithmetic  9.61 us (10%)
  local copies, waits for them, and re-layouts  5.51 us (6%)
    pallas_call x1, Pallas kernels, body(): pl.pallas_call(mixer_kernel, in_specs=[anywhere] * 4 + [vmem] * 7, out_sp...  76.4 us
    convert_element_type x1, other arithmetic, mul16(): return (a.astype(f32) * b.astype(f32)).astype(bf16)  7.03 us
    unnamed x16, local copies, waits for them, and re-layouts  4.12 us

profile of v3, /device:TPU:0, one launch (start us, length us, event | category | flops | bytes accessed | tf_op | source)
XLA Modules:
  0.0 92.3 jit_solution(4046736652914752189)
XLA Ops:
  0.6 0.7 fusion.5
  1.3 0.7 pad_convert_fusion
  2.0 0.7 multiply_convert_fusion
  2.7 0.1 copy.30
  2.8 0.1 reshape.55
  2.9 0.1 copy.29
  3.0 0.1 reshape.54.own_rate
  3.2 0.0 copy-start
  3.2 0.8 copy-done
  4.0 0.0 copy-start.1
  4.0 0.8 copy-done.1
  4.9 0.0 copy-start.2
  4.9 0.8 copy-done.2
  5.7 0.0 copy-start.3
  5.7 0.8 copy-done.3
  6.5 0.0 copy-start.4
  6.5 0.8 copy-done.4
  7.3 0.0 copy-start.6
  7.3 0.0 copy-start.7
  7.3 0.0 copy-start.5
  7.3 76.4 %mixer.1 = (bf16[32,2,128,128]{3,2,1,0:T(8,128)(2,1)}, bf16[32,2,128,128]{3,2,1,0:T(8,128)(2,1)}, f32[32,256]{1,0:T(8,128)S(1)}) custom-call(bf16[32,2,128,128]{3,2,1,0:T(8,128)(2,1)} %bitcast.16, bf16[32,2,128,128]{3,2,1,0:T(8,128)(2,1)} %bitcast.17, bf16[32,2,128,128]{3,2,1,0:T(8,128)(2,1)} %bitcast.18, bf16[32,2,128,128]{3,2,1,0:T(8,128)(2,1)} %bitcast.15, ...), custom_call_target="tpu_custom_call" | custom-call | tf_op jit(solution)/shard_map/mixer/pallas_call | solution.py:330
  83.8 0.5 multiply_bitcast_fusion
  84.3 0.1 reshape.58
  84.4 0.1 copy.33
  84.4 0.1 reshape.57
  84.5 0.1 copy.31
  84.6 0.0 copy-done.6
  84.6 0.0 copy-done.7
  84.6 0.7 multiply_multiply_fusion
  85.2 0.0 copy-done.5
  85.2 7.0 %fusion.1 = (bf16[8192,128]{1,0:T(8,128)(2,1)}, bf16[8192,128]{1,0:T(8,128)(2,1)}, bf16[8192,128]{1,0:T(8,128)(2,1)}, bf16[8192,128]{1,0:T(8,128)(2,1)}) fusion(bf16[8192,128]{1,0:T(8,128)(2,1)S(1)} %copy-done.5, bf16[32,2,128,128]{3,2,1,0:T(8,128)(2,1)} %get-tuple-element.10, bf16[8192,128]{1,0:T(8,128)(2,1)} %param.12, bf16[8192,128]{1,0:T(8,128)(2,1)} %param.14, ...), kind=kLoop, calls=%fused_computation.5 | loop fusion | flops 14680064 | bytes 20971520 | tf_op jit(solution)/shard_map/convert_element_type | solution.py:61
  (4 shorter events, 0.0 us)
Async XLA Ops:
  3.2 0.8 copy-start
  4.0 0.8 copy-start.1
  4.9 0.8 copy-start.2
  5.7 0.8 copy-start.3
  6.5 0.8 copy-start.4
  7.3 77.3 %copy-start.6 = (f32[128,16]{0,1:T(8,128)S(1)}, f32[128,16]{0,1:T(8,128)}, u32[]{:S(2)}) copy-start(f32[128,16]{0,1:T(8,128)} %param.16) | copy-start | bytes 24580
  7.3 77.3 %copy-start.7 = (f32[128,16]{0,1:T(8,128)S(1)}, f32[128,16]{0,1:T(8,128)}, u32[]{:S(2)}) copy-start(f32[128,16]{0,1:T(8,128)} %param.17) | copy-start | bytes 24580
  7.3 77.9 %copy-start.5 = (bf16[8192,128]{1,0:T(8,128)(2,1)S(1)}, bf16[8192,128]{1,0:T(8,128)(2,1)}, u32[]{:S(2)}) copy-start(bf16[8192,128]{1,0:T(8,128)(2,1)} %param.15) | copy-start | bytes 6291460

commit v4 on v3

--- a/solution.py
+++ b/solution.py
@@ -24,8 +24,9 @@
     fwd = np.concatenate([np.cos(angle), -np.sin(angle)], axis=1)
     inv = fwd.T / W
     flip = np.eye(W)[::-1]
-    cast = lambda z: jnp.asarray(np.ascontiguousarray(z), f32).astype(bf16)
-    return cast(fwd), cast(fwd[::-1]), cast(inv), cast(inv[:, ::-1]), cast(flip)
+    pad = np.concatenate([flip, np.zeros((W, W))], axis=1)
+    packed = np.concatenate([fwd, fwd[::-1], np.concatenate([inv, inv[:, ::-1]], axis=1), pad])
+    return jnp.asarray(packed, f32).astype(bf16)
 
 
 def dot(a, b):
@@ -71,10 +72,8 @@
 
 
 def mixer_kernel(
-    q_hbm, k_hbm, v_hbm, c_hbm, own_par, own_rate, fwd_ref, fwdr_ref, inv_ref, invr_ref, flip_ref,
-    mixed_hbm, pgrad_hbm, total_ref,
-    inp, away, sig, rev, lags, skip, par, keep, st_out, came, hold, ready, got, grad_out,
-    grad_in, mine, theirs, expand, stage,
+    q_hbm, k_hbm, v_hbm, c_hbm, tab_hbm, own_ref, mixed_hbm, pgrad_hbm, total_ref, tab, inp, away, sig, rev, lags, skip, par, keep, st_out, came, hold, ready, got, grad_out,
+    grad_in, mine, theirs, stage,
     load_sem, par_sem, pair_sem, st_sem, back_sem, grad_sem, out_sem, twin_sem,
 ):
     chips = q_hbm.shape[0]
@@ -100,6 +99,14 @@
         for n, ref in enumerate((q_hbm, k_hbm, v_hbm, c_hbm)):
             pltpu.make_async_copy(ref.at[:, side], inp.at[order, n], load_sem.at[order]).start()
 
+    pltpu.make_async_copy(tab_hbm, tab, load_sem.at[2]).start()
+    fwd_ref, fwdr_ref = tab.at[0:W], tab.at[W : 2 * W]
+    inv_ref, invr_ref = tab.at[2 * W : 4 * W, 0:W], tab.at[2 * W : 4 * W, W : 2 * W]
+    flip_ref = tab.at[4 * W : 5 * W, 0:W]
+    own = own_ref[...]
+    low = own - own.astype(bf16).astype(f32)
+    par[chip] = jnp.concatenate([own[:8], low[:8], own[8:16], own[16:17], low[16:17], own[18:24]], axis=0).astype(bf16)
+
     barrier = pltpu.get_barrier_semaphore()
 
     def tell(i, carry):
@@ -112,58 +119,76 @@
     pl.semaphore_wait(barrier, chips + 1)
 
     def send_par(i, carry):
-        remote(own_par, par.at[chip], par_sem, peer(after(i))).start()
+        remote(par.at[chip], par.at[chip], par_sem, peer(after(i))).start()
         return carry
 
     lax.fori_loop(1, chips, send_par, 0)
-    par[chip] = own_par[...]
-
-    def products(order, dst):
-        def step(b, carry):
-            dst[0, b] = mul16(inp[order, 1, b], inp[order, 2, b])
-            dst[1, b] = mul16(inp[order, 3, b], inp[order, 0, b])
+
+    pieces = 4
+    count = chips // pieces
+
+    def products(order, dst, first):
+        def step(i, carry):
+            for b in (first + 2 * i, first + 2 * i + 1):
+                dst[0, b] = mul16(inp[order, 1, b], inp[order, 2, b])
+                dst[1, b] = mul16(inp[order, 3, b], inp[order, 0, b])
             return carry
 
-        lax.fori_loop(0, chips, step, 0)
+        lax.fori_loop(0, count // 2, step, 0)
 
     wait_bytes(inp.at[0], load_sem.at[0])
-    products(0, away)
-    trade = remote(away, sig.at[core], pair_sem, near)
-    trade.start()
+    for n in range(pieces):
+        products(0, away, n * count)
+        block = pl.ds(n * count, count)
+        pltpu.make_async_remote_copy(
+            src_ref=away.at[:, block], dst_ref=sig.at[core, :, block], send_sem=pair_sem.at[pieces],
+            recv_sem=pair_sem.at[n], device_id=near, device_id_type=MESH,
+        ).start()
     wait_bytes(inp.at[1], load_sem.at[1])
-    products(1, sig.at[core])
-    trade.wait()
+    for n in range(pieces):
+        products(1, sig.at[core], n * count)
+    wait_bytes(tab, load_sem.at[2])
 
     eye = lax.broadcasted_iota(jnp.int32, (W, W), 0) == lax.broadcasted_iota(jnp.int32, (W, W), 1)
     lane = lax.broadcasted_iota(jnp.int32, (W, W), 1).astype(f32)
     mask = diag_mask()
 
-    def local_lags(b, carry):
-        x = jnp.concatenate([sig[0, 0, b], sig[1, 0, b]], axis=0)
-        m = jnp.concatenate([sig[0, 1, b], sig[1, 1, b]], axis=0)
-        xr = dot(x, flip_ref[...]).astype(bf16)
-        rev[0, b] = xr[:W]
-        rev[1, b] = xr[W:]
-        both = dot(cmul(dot(x, fwd_ref[...]), dot(m, fwdr_ref[...])), invr_ref[...])
-        lag = both[:W] + both[W:]
-        lags[0, b] = lag.astype(bf16)
-        lags[1, b] = (lag * lane).astype(bf16)
-        xm = x.astype(f32) * m.astype(f32)
-        sums = jnp.sum(xm[:W] + xm[W:], axis=1, keepdims=True)
-        skip[b] = jnp.broadcast_to(
-            jnp.sum(jnp.where(eye, sums, 0.0), axis=0, keepdims=True), (HALF, W)
-        )
-        return carry
-
-    lax.fori_loop(0, chips, local_lags, 0)
+    def local_lags(first, some):
+        blocks = [first + n for n in range(some)]
+        xs = [jnp.concatenate([sig[0, 0, b], sig[1, 0, b]], axis=0) for b in blocks]
+        ms = [jnp.concatenate([sig[0, 1, b], sig[1, 1, b]], axis=0) for b in blocks]
+        spec_x = [dot(x, fwd_ref[...]) for x in xs]
+        spec_m = [dot(m, fwdr_ref[...]) for m in ms]
+        turned = [dot(x, flip_ref[...]).astype(bf16) for x in xs]
+        found = [dot(cmul(a, b), invr_ref[...]) for a, b in zip(spec_x, spec_m)]
+        for n, b in enumerate(blocks):
+            rev[0, b] = turned[n][:W]
+            rev[1, b] = turned[n][W:]
+            lag = found[n][:W] + found[n][W:]
+            lags[0, b] = lag.astype(bf16)
+            lags[1, b] = (lag * lane).astype(bf16)
+            xm = xs[n].astype(f32) * ms[n].astype(f32)
+            sums = jnp.sum(xm[:W] + xm[W:], axis=1, keepdims=True)
+            skip[b] = jnp.broadcast_to(
+                jnp.sum(jnp.where(eye, sums, 0.0), axis=0, keepdims=True), (HALF, W)
+            )
+
+    for n in range(pieces):
+        block = pl.ds(n * count, count)
+        wait_bytes(sig.at[core, :, block], pair_sem.at[n])
+
+        def step(i, carry, n=n):
+            local_lags(n * count + 4 * i, 4)
+            return carry
+
+        lax.fori_loop(0, count // 4, step, 0)
     wait_bytes(par.at[pl.ds(0, chips - 1)], par_sem.at[1])
 
     def get_rate(b):
         rows = par[b].astype(f32)
         return rows, rows[:8] + rows[8:16]
 
-    def mode_sums(i, carry):
-        b = after(i)
+    def mode_sums(b):
         rate = get_rate(b)[1]
         far = jnp.exp(-float(W) * rate)
         parts = [rev[0, b], rev[1, b], sig[0, 1, b], sig[1, 1, b], lags[0, b], lags[1, b]]
@@ -178,22 +203,29 @@
             for n in range(len(parts)):
                 found[n].append(diag_row(mask, res[16 * n : 16 * n + 16]))
         found = [jnp.concatenate(rows, axis=0) for rows in found]
-        for n in range(len(parts)):
-            keep[b, n] = found[n]
         st = jnp.concatenate([found[0] * far + found[1], found[2] + far * found[3]], axis=0)
-        st_out[b] = st.astype(bf16)
-
-        @pl.when(i < chips)
+        return found, st.astype(bf16)
+
+    def sum_step(i, carry):
+        blocks = [after(2 * i + 1), after(2 * i + 2)]
+        results = [mode_sums(b) for b in blocks]
+        for b, (found, st) in zip(blocks, results):
+            for n, value in enumerate(found):
+                keep[b, n] = value
+            st_out[b] = st
+        remote(st_out.at[blocks[0]], came.at[chip], st_sem, peer(blocks[0])).start()
+
+        @pl.when(2 * i + 2 < chips)
         def _():
-            remote(st_out.at[b], came.at[chip], st_sem, peer(b)).start()
-
-        return carry
-
-    lax.fori_loop(1, chips + 1, mode_sums, 0)
+            remote(st_out.at[blocks[1]], came.at[chip], st_sem, peer(blocks[1])).start()
+
+        return carry
+
+    lax.fori_loop(0, chips // 2, sum_step, 0)
     came[chip] = st_out[chip]
     wait_bytes(came.at[pl.ds(0, chips - 1)], st_sem.at[1])
 
-    decay2 = jnp.exp(-2.0 * float(W) * own_rate[...])
+    decay2 = jnp.exp(-2.0 * float(W) * own[:8])
 
     def ahead(p, s):
         hold[p] = s
@@ -217,20 +249,20 @@
     got[chip] = ready[chip]
     wait_bytes(got.at[pl.ds(0, chips - 1)], back_sem.at[1])
 
-    def finish(i, carry):
-        b = after(i)
-        rows, rate = get_rate(b)
-        weight = rows[16:24]
-        bias_row = rows[24:25, :W] + rows[25:26, :W]
+    def chunk_states(b, rate):
         state = got[b].astype(f32)
-        near_decay = jnp.exp(-rate)
         far = jnp.exp(-float(W) * rate)
         s0, r1 = state[:HALF], state[HALF:]
-        s1 = far * s0 + keep[b, 0]
-        r0 = far * r1 + keep[b, 3]
+        return s0, far * s0 + keep[b, 0], far * r1 + keep[b, 3], r1
+
+    def send_grads(i, carry):
+        b = after(i)
+        rate = get_rate(b)[1]
+        near_decay = jnp.exp(-rate)
+        s0, s1, r0, r1 = chunk_states(b, rate)
         grad_a = keep[b, 4] + near_decay * (keep[b, 2] * s0 + keep[b, 3] * s1)
         grad_d = keep[b, 5] + near_decay * (
-            float(W) * far * (s0 * r0 + s1 * r1)
+            float(W) * jnp.exp(-float(W) * rate) * (s0 * r0 + s1 * r1)
             + s0 * keep[b, 6] + r0 * keep[b, 7] + s1 * keep[b, 8] + r1 * keep[b, 9]
         )
         skip_part = jnp.concatenate([skip[b], jnp.zeros((HALF, W), f32)], axis=1)
@@ -240,46 +272,66 @@
         def _():
             remote(grad_out.at[b], grad_in.at[chip], grad_sem, peer(b)).start()
 
-        wa = weight * near_decay
-        terms = [weight, wa * s0, wa * s1, wa * r0, wa * r1]
+        return carry
+
+    lax.fori_loop(1, chips + 1, send_grads, 0)
+    grad_in[chip] = grad_out[chip]
+
+    def expand(b):
+        rows, rate = get_rate(b)
+        s0, s1, r0, r1 = chunk_states(b, rate)
+        wa = rows[16:24] * jnp.exp(-rate)
+        terms = [rows[16:24], wa * s0, wa * s1, wa * r0, wa * r1]
+        made = []
         for g in range(HALF):
             e = powers(rate[g : g + 1])
             lhs = jnp.concatenate(
                 [jnp.where(mask, term[g : g + 1], 0.0) for term in terms], axis=0
             ).astype(bf16)
-            z = dot_nt(lhs, e)
-            for n in range(len(terms)):
-                expand[n, 16 * g : 16 * g + 16] = z[16 * n : 16 * n + 16]
+            made.append(dot_nt(lhs, e))
+        return [jnp.concatenate([z[16 * n : 16 * n + 16] for z in made], axis=0) for n in range(5)]
+
+    def convolve(b, taps, y0, y1, p0, p1):
+        rows = par[b].astype(f32)
+        bias_row = rows[24:25, :W] + rows[25:26, :W]
         x = jnp.concatenate([sig[0, 0, b], sig[1, 0, b]], axis=0)
         m = jnp.concatenate([sig[0, 1, b], sig[1, 1, b]], axis=0)
-        spec_h = dot(expand[0].astype(bf16), fwd_ref[...])
+        spec_x, spec_m = dot(x, fwd_ref[...]), dot(m, fwdr_ref[...])
+        spec_h = dot(taps.astype(bf16), fwd_ref[...])
         spec_h = jnp.concatenate([spec_h, spec_h], axis=0)
         gain = jnp.sum(jnp.where(eye, bias_row, 0.0), axis=1, keepdims=True)
         gain = jnp.concatenate([gain, gain], axis=0)
-        y = dot(cmul(dot(x, fwd_ref[...]), spec_h), inv_ref[...])
-        y += jnp.concatenate([expand[1], expand[2]], axis=0) + gain * x.astype(f32)
-        p = dot(cmul(dot(m, fwdr_ref[...]), spec_h), invr_ref[...])
-        p += dot(
-            jnp.concatenate([expand[3], expand[4]], axis=0).astype(bf16), flip_ref[...]
-        ) + gain * m.astype(f32)
-        y, p = y.astype(bf16), p.astype(bf16)
-        for chunk in range(2):
-            stage[chunk, 0, b] = y[W * chunk : W * chunk + W]
-            stage[chunk, 1, b] = p[W * chunk : W * chunk + W]
-        for n, out in enumerate((mixed_hbm, pgrad_hbm)):
-            pltpu.make_async_copy(stage.at[core, n, b], out.at[b, core], out_sem.at[2]).start()
-            remote(stage.at[1 - core, n, b], out.at[b, core], out_sem, near).start()
-        return carry
-
-    lax.fori_loop(1, chips + 1, finish, 0)
-
-    grad_in[chip] = grad_out[chip]
+        y = dot(cmul(spec_x, spec_h), inv_ref[...])
+        y += jnp.concatenate([y0, y1], axis=0) + gain * x.astype(f32)
+        p = dot(cmul(spec_m, spec_h), invr_ref[...])
+        p += dot(jnp.concatenate([p0, p1], axis=0).astype(bf16), flip_ref[...])
+        p += gain * m.astype(f32)
+        return y.astype(bf16), p.astype(bf16)
+
+    def finish(i, carry):
+        blocks = [after(2 * i + 1), after(2 * i + 2)]
+        grown = [expand(b) for b in blocks]
+        results = [convolve(b, *terms) for b, terms in zip(blocks, grown)]
+        for b, result in zip(blocks, results):
+            for chunk in range(2):
+                for n in range(2):
+                    stage[chunk, n, b] = result[n][W * chunk : W * chunk + W]
+        for b in blocks:
+            for n, out in enumerate((mixed_hbm, pgrad_hbm)):
+                pltpu.make_async_copy(stage.at[core, n, b], out.at[b, core], out_sem.at[2]).start()
+                remote(stage.at[1 - core, n, b], out.at[b, core], out_sem, near).start()
+        return carry
+
+    early = 3 * chips // 8
+    lax.fori_loop(0, early, finish, 0)
     wait_bytes(grad_in.at[pl.ds(0, chips - 1)], grad_sem.at[1])
     mine[...] = lax.fori_loop(
         0, chips, lambda p, s: s + grad_in[p].astype(f32), jnp.zeros(grad_in.shape[1:], f32)
     )
     swap = remote(mine, theirs, twin_sem, twin)
     swap.start()
+    lax.fori_loop(early, chips // 2, finish, 0)
+    wait_bytes(away, pair_sem.at[pieces])
     wait_bytes(own_many(par, chips), par_sem.at[0])
     wait_bytes(own_many(st_out, chips), st_sem.at[0])
     wait_bytes(own_many(ready, chips), back_sem.at[0])
@@ -297,24 +349,16 @@
 def body(query, key_in, value_in, cotangent, residue, log_rate, bias):
     shards = lax.axis_size("ctx")
     channels, width = query.shape
-    fwd, fwdr, inv, invr, flip = tables()
     rate = jnp.exp(log_rate)
     root = jnp.sqrt(-jnp.expm1(-2.0 * rate))
-    rate_rows = rate.reshape(HALF, LANES)
-    weight_rows = (residue * root).reshape(HALF, LANES)
-    bias_row = jnp.pad(bias.reshape(1, W), ((0, 0), (0, LANES - W)))
-    upper = lambda z: lax.reduce_precision(z, 8, 7)
-    own_par = jnp.concatenate(
+    own = jnp.concatenate(
         [
-            rate_rows,
-            rate_rows - upper(rate_rows),
-            weight_rows,
-            bias_row,
-            bias_row - upper(bias_row),
-            jnp.zeros((6, LANES), f32),
+            rate.reshape(HALF, LANES),
+            (residue * root).reshape(HALF, LANES),
+            jnp.pad(bias.reshape(1, W), ((0, 7), (0, LANES - W))),
         ],
         axis=0,
-    ).astype(bf16)
+    )
     vmem = pl.BlockSpec(memory_space=pltpu.VMEM)
     dma = pltpu.SemaphoreType.DMA
 
@@ -329,10 +373,11 @@
     part = jax.ShapeDtypeStruct((chips, 2, W, width), bf16)
     mixed, pgrad, total = pl.pallas_call(
         mixer_kernel,
-        in_specs=[anywhere] * 4 + [vmem] * 7,
+        in_specs=[anywhere] * 5 + [vmem],
         out_specs=[anywhere, anywhere, vmem],
         out_shape=[part, part, jax.ShapeDtypeStruct((32, LANES), f32)],
         scratch_shapes=[
+            pltpu.VMEM((5 * W, LANES), bf16),
             pltpu.VMEM((2, 4, chips, W, W), bf16),
             pltpu.VMEM((2, chips, W, W), bf16),
             pltpu.VMEM((2, 2, chips, W, W), bf16),
@@ -350,11 +395,10 @@
             pltpu.VMEM((chips, 32, LANES), bf16),
             pltpu.VMEM((32, LANES), f32),
             pltpu.VMEM((32, LANES), f32),
-            pltpu.VMEM((5, W, W), f32),
             pltpu.VMEM((2, 2, chips, W, W), bf16),
+            dma((3,)),
             dma((2,)),
-            dma((2,)),
-            dma((2,)),
+            dma((5,)),
             dma((2,)),
             dma((2,)),
             dma((2,)),
@@ -363,8 +407,7 @@
         ],
         compiler_params=remote(1),
         name="mixer",
-    )(split(query), split(key_in), split(value_in), split(cotangent), own_par, rate_rows,
-      fwd, fwdr, inv, invr, flip)
+    )(split(query), split(key_in), split(value_in), split(cotangent), tables(), own)
     mixed = mixed.reshape(channels, width)
     pgrad = pgrad.reshape(channels, width)
     gated, gq = mul16(query, mixed), mul16(cotangent, mixed)

time: 92.7 us -> 69.8 us (0.75)
  the two profiles are of different devices: /device:TPU:0 before, /device:TPU:1 now
where the time goes in v4:
time: 69.8 us; the launch traced here: 69.6 us
  Pallas kernels  57.7 us (83%)
  other arithmetic  9.61 us (14%)
  local copies, waits for them, and re-layouts  1.64 us (2%)
    pallas_call x1, Pallas kernels, body(): pl.pallas_call(mixer_kernel, in_specs=[anywhere] * 5 + [vmem], out_specs=...  57.7 us
    convert_element_type x1, other arithmetic, mul16(): return (a.astype(f32) * b.astype(f32)).astype(bf16)  7.03 us

profile of v4, /device:TPU:1, one launch (start us, length us, event | category | flops | bytes accessed | tf_op | source)
XLA Modules:
  0.0 69.6 jit_solution(1182915624589256447)
XLA Ops:
  0.6 0.7 %fusion.6 = (f32[128,16]{0,1:T(8,128)S(1)}, f32[128,16]{0,1:T(8,128)S(1)}) fusion(f32[128,16]{0,1:T(8,128)} %param.13, f32[128,16]{0,1:T(8,128)} %param.12), kind=kLoop, calls=%fused_computation.16 | loop fusion | flops 6144 | bytes 32768 | tf_op jit(solution)/shard_map/exp | solution.py:352
  1.4 0.1 copy.25
  1.5 0.1 reshape.53
  1.6 0.1 copy.26
  1.7 0.1 reshape.54
  1.8 0.7 select_maximum_fusion.own_ref
  2.4 0.0 copy-start
  2.4 1.0 %copy-done = bf16[640,256]{1,0:T(8,128)(2,1)S(1)} copy-done((bf16[640,256]{1,0:T(8,128)(2,1)S(1)}, bf16[640,256]{1,0:T(8,128)(2,1)}, u32[]{:S(2)}) %copy-start) | copy-done | bytes 327704
  3.4 0.0 copy-start.2
  3.4 0.0 copy-start.3
  3.4 0.0 copy-start.1
  3.4 57.7 %mixer.1 = (bf16[32,2,128,128]{3,2,1,0:T(8,128)(2,1)}, bf16[32,2,128,128]{3,2,1,0:T(8,128)(2,1)}, f32[32,256]{1,0:T(8,128)S(1)}) custom-call(bf16[32,2,128,128]{3,2,1,0:T(8,128)(2,1)} %bitcast.16, bf16[32,2,128,128]{3,2,1,0:T(8,128)(2,1)} %bitcast.17, bf16[32,2,128,128]{3,2,1,0:T(8,128)(2,1)} %bitcast.18, bf16[32,2,128,128]{3,2,1,0:T(8,128)(2,1)} %bitcast.15, ...), custom_call_target="tpu_custom_call" | custom-call | tf_op jit(solution)/shard_map/mixer/pallas_call | solution.py:374
  61.1 0.5 multiply_bitcast_fusion
  61.6 0.1 reshape.57
  61.7 0.1 copy.29
  61.8 0.1 reshape.56
  61.9 0.1 copy.27
  61.9 0.0 copy-done.2
  61.9 0.0 copy-done.3
  61.9 0.7 multiply_multiply_fusion
  62.6 0.0 copy-done.1
  62.6 7.0 %fusion.1 = (bf16[8192,128]{1,0:T(8,128)(2,1)}, bf16[8192,128]{1,0:T(8,128)(2,1)}, bf16[8192,128]{1,0:T(8,128)(2,1)}, bf16[8192,128]{1,0:T(8,128)(2,1)}) fusion(bf16[8192,128]{1,0:T(8,128)(2,1)S(1)} %copy-done.1, bf16[32,2,128,128]{3,2,1,0:T(8,128)(2,1)} %get-tuple-element.10, bf16[8192,128]{1,0:T(8,128)(2,1)} %param.8, bf16[8192,128]{1,0:T(8,128)(2,1)} %param.10, ...), kind=kLoop, calls=%fused_computation.5 | loop fusion | flops 14680064 | bytes 20971520 | tf_op jit(solution)/shard_map/convert_element_type | solution.py:62
  (1 shorter events, 0.0 us)
Async XLA Ops:
  2.4 1.0 %copy-start = (bf16[640,256]{1,0:T(8,128)(2,1)S(1)}, bf16[640,256]{1,0:T(8,128)(2,1)}, u32[]{:S(2)}) copy-start(bf16[640,256]{1,0:T(8,128)(2,1)} %constant.13.tab_hbm) | copy-start | bytes 983044
  3.4 58.5 %copy-start.2 = (f32[128,16]{0,1:T(8,128)S(1)}, f32[128,16]{0,1:T(8,128)}, u32[]{:S(2)}) copy-start(f32[128,16]{0,1:T(8,128)} %param.13) | copy-start | bytes 24580
  3.4 58.5 %copy-start.3 = (f32[128,16]{0,1:T(8,128)S(1)}, f32[128,16]{0,1:T(8,128)}, u32[]{:S(2)}) copy-start(f32[128,16]{0,1:T(8,128)} %param.12) | copy-start | bytes 24580
  3.4 59.2 %copy-start.1 = (bf16[8192,128]{1,0:T(8,128)(2,1)S(1)}, bf16[8192,128]{1,0:T(8,128)(2,1)}, u32[]{:S(2)}) copy-start(bf16[8192,128]{1,0:T(8,128)(2,1)} %param.11) | copy-start | bytes 6291460

commit v5 on v4

v5 whole, which is shorter than its diff:
```python
import functools
import math

import jax
import jax.numpy as jnp
import numpy as np
from jax import lax
from jax.experimental import pallas as pl
from jax.experimental.pallas import tpu as pltpu
from jax.sharding import PartitionSpec as P

bf16 = jnp.bfloat16
f32 = jnp.float32
W = 128
HALF = 8
MESH = pl.DeviceIdType.MESH
LANES = 256


def tables():
    n = np.arange(W)[:, None]
    f = np.arange(W)[None, :]
    angle = ((2 * f + 1) * n % (4 * W)) * (2.0 * math.pi / (4 * W))
    fwd = np.concatenate([np.cos(angle), -np.sin(angle)], axis=1)
    inv = fwd.T / W
    flip = np.eye(W)[::-1]
    pad = np.concatenate([flip, np.zeros((W, W))], axis=1)
    packed = np.concatenate([fwd, fwd[::-1], np.concatenate([inv, inv[:, ::-1]], axis=1), pad])
    return jnp.asarray(packed, f32)


def dot(a, b):
    return jnp.dot(a, b, preferred_element_type=f32)


def dot_nt(a, b):
    return lax.dot_general(a, b, (((1,), (1,)), ((), ())), preferred_element_type=f32)


def powers(rate_row):
    rate8 = jnp.broadcast_to(rate_row, (8, LANES))
    row = lax.broadcasted_iota(jnp.int32, (8, LANES), 0).astype(f32)
    out = jnp.exp(-rate8 * row)
    for step in (8, 16, 32, 64):
        mult = jnp.exp(-rate8 * float(step))
        parts = [out[i : i + 8] * mult for i in range(0, step, 8)]
        out = jnp.concatenate([out] + parts, axis=0)
    return out.astype(bf16)


def diag_mask():
    row = lax.broadcasted_iota(jnp.int32, (16, LANES), 0)
    lane = lax.broadcasted_iota(jnp.int32, (16, LANES), 1)
    return row == lane // 16


def diag_row(mask, rows):
    return jnp.sum(jnp.where(mask, rows, 0.0), axis=0, keepdims=True)


def mul16(a, b):
    return (a.astype(f32) * b.astype(f32)).astype(bf16)


def cmul(a, b):
    ar, ai, br, bi = a[:, :W], a[:, W:], b[:, :W], b[:, W:]
    return jnp.concatenate([ar * br - ai * bi, ar * bi + ai * br], axis=1).astype(bf16)


def wait_bytes(ref, sem):
    pltpu.make_async_copy(ref, ref, sem).wait()


def mixer_kernel(
    q_hbm, k_hbm, v_hbm, c_hbm, tab_hbm, own_ref, mixed_hbm, pgrad_hbm, total_ref,
    tab32, tab, inp, away, sig, rev, lags, skip, par, keep, st_out, came, hold, ready, got,
    grad_out, grad_in, mine, theirs, stage,
    load_sem, par_sem, pair_sem, st_sem, back_sem, grad_sem, out_sem, twin_sem,
):
    pairs = q_hbm.shape[0]
    chips = 2 * pairs
    steps = pairs // 2
    quad = HALF // 2
    me = lax.axis_index("ctx")
    core, chip = lax.rem(me, 2), lax.div(me, 2)
    near = {"ctx": me + 1 - 2 * core}
    twin = {"dp": 1 - lax.axis_index("dp")}

    def peer(b):
        return {"ctx": 2 * b + core}

    def after(i):
        return lax.rem(chip + i, chips)

    def remote(src, dst, send, recv, who):
        return pltpu.make_async_remote_copy(
            src_ref=src, dst_ref=dst, send_sem=send, recv_sem=recv,
            device_id=who, device_id_type=MESH,
        )

    for order in range(2):
        side = 1 - core if order == 0 else core
        for half in range(2):
            for n, ref in enumerate((q_hbm, k_hbm, v_hbm, c_hbm)):
                pltpu.make_async_copy(
                    ref.at[:, :, side, half], inp.at[order, n, pl.ds(half * pairs, pairs)],
                    load_sem.at[order],
                ).start()
    pltpu.make_async_copy(tab_hbm, tab32, load_sem.at[2]).start()

    barrier = pltpu.get_barrier_semaphore()

    def tell(i, carry):
        pl.semaphore_signal(barrier, inc=1, device_id=peer(after(i)), device_id_type=MESH)
        return carry

    lax.fori_loop(1, chips, tell, 0)
    pl.semaphore_signal(barrier, inc=1, device_id=near, device_id_type=MESH)
    pl.semaphore_signal(barrier, inc=1, device_id=twin, device_id_type=MESH)

    own = own_ref[...]
    low = own - own.astype(bf16).astype(f32)
    for half in range(2):
        rows = slice(quad * half, quad * half + quad)
        par[chip, half] = jnp.concatenate(
            [
                own[:8][rows],
                low[:8][rows],
                own[8:16][rows],
                own[16 + half : 17 + half],
                low[16 + half : 17 + half],
                own[17 - half : 18 - half],
                low[17 - half : 18 - half],
            ],
            axis=0,
        ).astype(bf16)

    fwd_ref, fwdr_ref = tab.at[0:W], tab.at[W : 2 * W]
    inv_ref, invr_ref = tab.at[2 * W : 4 * W, 0:W], tab.at[2 * W : 4 * W, W : 2 * W]
    flip_ref = tab.at[4 * W : 5 * W, 0:W]

    pieces = 4
    count = chips // pieces

    def products(order, dst, first):
        def step(i, carry):
            for v in (first + 2 * i, first + 2 * i + 1):
                dst[0, v] = mul16(inp[order, 1, v], inp[order, 2, v]).reshape(W, W)
                dst[1, v] = mul16(inp[order, 3, v], inp[order, 0, v]).reshape(W, W)
            return carry

        lax.fori_loop(0, count // 2, step, 0)

    def send_par(i, carry):
        remote(
            par.at[chip], par.at[chip], par_sem.at[0], par_sem.at[1], peer(after(i))
        ).start()
        return carry

    wait_bytes(inp.at[0], load_sem.at[0])
    for n in range(pieces):
        products(0, away, n * count)
        if n == 0:
            pl.semaphore_wait(barrier, chips + 1)
            lax.fori_loop(1, chips, send_par, 0)
        block = pl.ds(n * count, count)
        remote(
            away.at[:, block], sig.at[core, :, block], pair_sem.at[pieces], pair_sem.at[n], near
        ).start()
    wait_bytes(inp.at[1], load_sem.at[1])
    for n in range(pieces):
        products(1, sig.at[core], n * count)
    wait_bytes(tab32, load_sem.at[2])
    tab[...] = tab32[...].astype(bf16)

    row_no = lax.broadcasted_iota(jnp.int32, (W, W), 0)
    lane_no = lax.broadcasted_iota(jnp.int32, (W, W), 1)
    eye = row_no == lane_no
    swapped_eye = lax.rem(row_no + W // 2, W) == lane_no
    lane = lax.broadcasted_iota(jnp.int32, (W, W), 1).astype(f32)
    mask = diag_mask()

    def local_lags(first, some):
        blocks = [first + n for n in range(some)]
        xs = [jnp.concatenate([sig[0, 0, v], sig[1, 0, v]], axis=0) for v in blocks]
        ms = [jnp.concatenate([sig[0, 1, v], sig[1, 1, v]], axis=0) for v in blocks]
        spec_x = [dot(x, fwd_ref[...]) for x in xs]
        spec_m = [dot(m, fwdr_ref[...]) for m in ms]
        turned = [dot(x, flip_ref[...]).astype(bf16) for x in xs]
        found = [dot(cmul(a, b), invr_ref[...]) for a, b in zip(spec_x, spec_m)]
        for n, v in enumerate(blocks):
            rev[0, v] = turned[n][:W]
            rev[1, v] = turned[n][W:]
            lag = found[n][:W] + found[n][W:]
            lags[0, v] = lag.astype(bf16)
            lags[1, v] = (lag * lane).astype(bf16)
            xm = xs[n].astype(f32) * ms[n].astype(f32)
            sums = jnp.sum(xm[:W] + xm[W:], axis=1, keepdims=True)
            for side, where in enumerate((eye, swapped_eye)):
                skip[v, HALF * side : HALF * side + HALF] = jnp.broadcast_to(
                    jnp.sum(jnp.where(where, sums, 0.0), axis=0, keepdims=True), (HALF, W)
                )

    for n in range(pieces):
        block = pl.ds(n * count, count)
        wait_bytes(sig.at[core, :, block], pair_sem.at[n])

        def step(i, carry, n=n):
            local_lags(n * count + 4 * i, 4)
            return carry

        lax.fori_loop(0, count // 4, step, 0)
    wait_bytes(par.at[pl.ds(0, chips - 1)], par_sem.at[1])

    def place(j, n):
        half = lax.div(j, steps)
        u = lax.rem(lax.div(chip, 2) + 2 * lax.rem(j, steps) + 1 + n, pairs)
        return half, u, half * pairs + u

    def halves(first, second, start):
        rows = slice(start, start + quad)
        return jnp.concatenate([first[rows], second[rows]], axis=0)

    def get_par(half, u):
        return par[2 * u, half].astype(f32), par[2 * u + 1, half].astype(f32)

    def get_rate(pair):
        return halves(*pair, 0) + halves(*pair, quad)

    def mode_sums(half, u, v):
        rate = get_rate(get_par(half, u))
        far = jnp.exp(-float(W) * rate)
        parts = [rev[0, v], rev[1, v], sig[0, 1, v], sig[1, 1, v], lags[0, v], lags[1, v]]
        for chunk in range(2):
            parts.append((parts[2 + chunk].astype(f32) * (lane + 1.0)).astype(bf16))
            parts.append((parts[chunk].astype(f32) * lane).astype(bf16))
        found = [[] for _ in parts]
        for g in range(HALF):
            e = powers(rate[g : g + 1])
            rows = slice(16 * g, 16 * g + 16)
            res = dot(jnp.concatenate([part[rows] for part in parts], axis=0), e)
            for n in range(len(parts)):
                found[n].append(diag_row(mask, res[16 * n : 16 * n + 16]))
        found = [jnp.concatenate(rows, axis=0) for rows in found]
        return found, found[0] * far + found[1], found[2] + far * found[3]

    def sum_step(j, carry):
        places = [place(j, n) for n in range(2)]
        results = [mode_sums(*where) for where in places]
        for (half, u, v), (found, ahead, back) in zip(places, results):
            for n, value in enumerate(found):
                keep[v, n] = value
            for n in range(2):
                rows = slice(quad * n, quad * n + quad)
                st_out[half, 2 * u + n] = jnp.concatenate([ahead[rows], back[rows]], axis=0)
        for half, u, v in places:
            for n in range(2):
                b = 2 * u + n

                @pl.when(b != chip)
                def _(b=b, half=half):
                    remote(
                        st_out.at[half, b], came.at[half, chip], st_sem.at[half, 0],
                        st_sem.at[half, 1], peer(b),
                    ).start()

        return carry

    def scan(half):
        came[half, chip] = st_out[half, chip]
        wait_bytes(came.at[half, pl.ds(0, chips - 1)], st_sem.at[half, 1])
        decay2 = jnp.exp(-2.0 * float(W) * own[quad * half : quad * half + quad])

        def ahead(p, s):
            hold[p, 0:quad] = s
            return s * decay2 + came[half, p][:quad]

        lax.fori_loop(0, chips, ahead, jnp.zeros((quad, LANES), f32))

        def back(i, s):
            p = chips - 1 - i
            ready[half, p] = jnp.concatenate([hold[p, 0:quad], s], axis=0)
            return s * decay2 + came[half, p][quad:]

        lax.fori_loop(0, chips, back, jnp.zeros((quad, LANES), f32))

        def send_back(i, carry):
            b = after(i)
            remote(
                ready.at[half, b], got.at[half, chip], back_sem.at[half, 0], back_sem.at[half, 1],
                peer(b),
            ).start()
            return carry

        lax.fori_loop(1, chips, send_back, 0)
        got[half, chip] = ready[half, chip]

    def chunk_states(half, u, v, rate):
        pair = got[half, 2 * u], got[half, 2 * u + 1]
        far = jnp.exp(-float(W) * rate)
        s0, r1 = halves(*pair, 0), halves(*pair, quad)
        return s0, far * s0 + keep[v, 0], far * r1 + keep[v, 3], r1

    def send_grads(half):
        wait_bytes(got.at[half, pl.ds(0, chips - 1)], back_sem.at[half, 1])

        def step(i, carry):
            u = lax.rem(lax.div(chip, 2) + 1 + i, pairs)
            v = half * pairs + u
            rate = get_rate(get_par(half, u))
            near_decay = jnp.exp(-rate)
            s0, s1, r0, r1 = chunk_states(half, u, v, rate)
            grad_a = keep[v, 4] + near_decay * (keep[v, 2] * s0 + keep[v, 3] * s1)
            grad_d = keep[v, 5] + near_decay * (
                float(W) * jnp.exp(-float(W) * rate) * (s0 * r0 + s1 * r1)
                + s0 * keep[v, 6] + r0 * keep[v, 7] + s1 * keep[v, 8] + r1 * keep[v, 9]
            )
            for n in range(2):
                rows = slice(quad * n, quad * n + quad)
                first = 0 if n == half else HALF
                skip_part = jnp.concatenate(
                    [skip[v, first : first + HALF], jnp.zeros((HALF, W), f32)], axis=1
                )
                grad_out[half, 2 * u + n] = jnp.concatenate(
                    [grad_a[rows], grad_d[rows], skip_part], axis=0
                ).astype(bf16)
            for n in range(2):
                b = 2 * u + n

                @pl.when(b != chip)
                def _(b=b):
                    remote(
                        grad_out.at[half, b], grad_in.at[half, chip], grad_sem.at[half, 0],
                        grad_sem.at[half, 1], peer(b),
                    ).start()

            return carry

        lax.fori_loop(0, pairs, step, 0)
        grad_in[half, chip] = grad_out[half, chip]

    def expand(half, u, v):
        pair = get_par(half, u)
        rate, weight = get_rate(pair), halves(*pair, 2 * quad)
        s0, s1, r0, r1 = chunk_states(half, u, v, rate)
        wa = weight * jnp.exp(-rate)
        terms = [weight, wa * s0, wa * s1, wa * r0, wa * r1]
        made = []
        for g in range(HALF):
            e = powers(rate[g : g + 1])
            lhs = jnp.concatenate(
                [jnp.where(mask, term[g : g + 1], 0.0) for term in terms], axis=0
            ).astype(bf16)
            made.append(dot_nt(lhs, e))
        return [jnp.concatenate([z[16 * n : 16 * n + 16] for z in made], axis=0) for n in range(5)]

    def convolve(half, u, v, taps, y0, y1, p0, p1):
        pair = get_par(half, u)
        even, odd = pair[0][12:13, :W] + pair[0][13:14, :W], pair[1][14:15, :W] + pair[1][15:, :W]
        bias_row = jnp.where(lane[:1] < W // 2, even, odd)
        x = jnp.concatenate([sig[0, 0, v], sig[1, 0, v]], axis=0)
        m = jnp.concatenate([sig[0, 1, v], sig[1, 1, v]], axis=0)
        spec_x, spec_m = dot(x, fwd_ref[...]), dot(m, fwdr_ref[...])
        spec_h = dot(taps.astype(bf16), fwd_ref[...])
        spec_h = jnp.concatenate([spec_h, spec_h], axis=0)
        gain = jnp.sum(jnp.where(eye, bias_row, 0.0), axis=1, keepdims=True)
        gain = jnp.concatenate([gain, gain], axis=0)
        y = dot(cmul(spec_x, spec_h), inv_ref[...])
        y += jnp.concatenate([y0, y1], axis=0) + gain * x.astype(f32)
        p = dot(cmul(spec_m, spec_h), invr_ref[...])
        p += dot(jnp.concatenate([p0, p1], axis=0).astype(bf16), flip_ref[...])
        p += gain * m.astype(f32)
        return y.astype(bf16), p.astype(bf16)

    def finish(j, carry):
        places = [place(j, n) for n in range(2)]
        grown = [expand(*where) for where in places]
        results = [convolve(*where, *terms) for where, terms in zip(places, grown)]
        for (half, u, v), result in zip(places, results):
            for chunk in range(2):
                for n in range(2):
                    stage[chunk, n, v] = result[n][W * chunk : W * chunk + W].reshape(2, W // 2, W)
        for half, u, v in places:
            for n, out in enumerate((mixed_hbm, pgrad_hbm)):
                spot = out.at[u, :, core, half]
                pltpu.make_async_copy(stage.at[core, n, v], spot, out_sem.at[2]).start()
                remote(stage.at[1 - core, n, v], spot, out_sem.at[0], out_sem.at[1], near).start()
        return carry

    middle = steps + 5 * steps // 8
    lax.fori_loop(0, middle, sum_step, 0)
    scan(0)
    lax.fori_loop(middle, 2 * steps, sum_step, 0)
    send_grads(0)
    lax.fori_loop(0, steps // 4, finish, 0)
    scan(1)
    lax.fori_loop(steps // 4, steps, finish, 0)
    send_grads(1)
    early = steps + 3 * steps // 4
    lax.fori_loop(steps, early, finish, 0)
    for half in range(2):
        wait_bytes(grad_in.at[half, pl.ds(0, chips - 1)], grad_sem.at[half, 1])
        mine[half] = lax.fori_loop(
            0, chips, lambda p, t: t + grad_in[half, p].astype(f32), jnp.zeros((16, LANES), f32)
        )
    swap = remote(mine, theirs, twin_sem.at[0], twin_sem.at[1], twin)
    swap.start()
    lax.fori_loop(early, 2 * steps, finish, 0)
    wait_bytes(away, pair_sem.at[pieces])
    wait_bytes(par.at[pl.ds(0, chips - 1)], par_sem.at[0])
    for half in range(2):
        wait_bytes(st_out.at[half, pl.ds(0, chips - 1)], st_sem.at[half, 0])
        wait_bytes(ready.at[half, pl.ds(0, chips - 1)], back_sem.at[half, 0])
        wait_bytes(grad_out.at[half, pl.ds(0, chips - 1)], grad_sem.at[half, 0])
    for n in range(3):
        wait_bytes(stage.at[0], out_sem.at[n])
    swap.wait()
    total_ref[...] = mine[...] + theirs[...]


def body(query, key_in, value_in, cotangent, residue, log_rate, bias):
    shards = lax.axis_size("ctx")
    channels, width = query.shape
    rate = jnp.exp(log_rate)
    root = jnp.sqrt(-jnp.expm1(-2.0 * rate))
    bias_rows = jnp.stack([bias, jnp.roll(bias, W // 2)])
    bias_rows = jnp.pad(bias_rows, ((0, 6), (0, LANES - W)))
    own = jnp.concatenate(
        [
            rate.reshape(HALF, LANES),
            (residue * root).reshape(HALF, LANES),
            bias_rows,
        ],
        axis=0,
    )
    vmem = pl.BlockSpec(memory_space=pltpu.VMEM)
    dma = pltpu.SemaphoreType.DMA

    def remote(number):
        return pltpu.CompilerParams(
            collective_id=number, has_side_effects=True, vmem_limit_bytes=52 * 1024 * 1024
        )

    chips = shards // 2
    split = lambda z: z.reshape(chips // 2, 2, 2, 2, W // 2, width)
    anywhere = pl.BlockSpec(memory_space=pl.ANY)
    part = jax.ShapeDtypeStruct((chips // 2, 2, 2, 2, W // 2, width), bf16)
    mixed, pgrad, total = pl.pallas_call(
        mixer_kernel,
        in_specs=[anywhere] * 5 + [vmem],
        out_specs=[anywhere, anywhere, vmem],
        out_shape=[part, part, jax.ShapeDtypeStruct((2, 16, LANES), f32)],
        scratch_shapes=[
            pltpu.VMEM((5 * W, LANES), f32),
            pltpu.VMEM((5 * W, LANES), bf16),
            pltpu.VMEM((2, 4, chips, 2, W // 2, W), bf16),
            pltpu.VMEM((2, chips, W, W), bf16),
            pltpu.VMEM((2, 2, chips, W, W), bf16),
            pltpu.VMEM((2, chips, W, W), bf16),
            pltpu.VMEM((2, chips, W, W), bf16),
            pltpu.VMEM((chips, 2 * HALF, W), f32),
            pltpu.VMEM((chips, 2, 16, LANES), bf16),
            pltpu.VMEM((chips, 10, HALF, LANES), f32),
            pltpu.VMEM((2, chips, HALF, LANES), f32),
            pltpu.VMEM((2, chips, HALF, LANES), f32),
            pltpu.VMEM((chips, HALF, LANES), f32),
            pltpu.VMEM((2, chips, HALF, LANES), f32),
            pltpu.VMEM((2, chips, HALF, LANES), f32),
            pltpu.VMEM((2, chips, 16, LANES), bf16),
            pltpu.VMEM((2, chips, 16, LANES), bf16),
            pltpu.VMEM((2, 16, LANES), f32),
            pltpu.VMEM((2, 16, LANES), f32),
            pltpu.VMEM((2, 2, chips, 2, W // 2, W), bf16),
            dma((3,)),
            dma((2,)),
            dma((5,)),
            dma((2, 2)),
            dma((2, 2)),
            dma((2, 2)),
            dma((3,)),
            dma((2,)),
        ],
        compiler_params=remote(1),
        name="mixer",
    )(split(query), split(key_in), split(value_in), split(cotangent), tables(), own)
    mixed = mixed.reshape(channels, width)
    pgrad = pgrad.reshape(channels, width)
    gated, gq = mul16(query, mixed), mul16(cotangent, mixed)
    gk, gv = mul16(pgrad, value_in), mul16(pgrad, key_in)

    modes = residue.shape[1]
    quad = HALF // 2
    grad_a = total[:, :quad].reshape(-1, modes)
    grad_d = total[:, quad : 2 * quad].reshape(-1, modes)
    skip = jnp.concatenate([total[0, HALF, : W // 2], total[1, HALF, W // 2 : W]])
    scale = 1.0 / math.sqrt(float(shards * width * lax.axis_size("dp")))
    grad_residue = root * grad_a * scale
    grad_rate = rate * residue * (jnp.exp(-2.0 * rate) / root * grad_a - root * grad_d) * scale
    grad_bias = skip * scale
    return gated, gq, gk, gv, grad_residue, grad_rate, grad_bias


def solution(mesh):
    tok = P(None, ("dp", "ctx"))
    chan = P("ctx", None)
    return jax.shard_map(
        body,
        mesh=mesh,
        in_specs=(tok, tok, tok, tok, chan, chan, P("ctx")),
        out_specs=(tok, tok, tok, tok, chan, chan, P("ctx")),
        check_vma=False,
    )
```

time: 69.8 us -> 69 us (0.989)
  the two profiles are of different devices: /device:TPU:1 before, /device:TPU:0 now
where the time goes in v5:
time: 69 us; the launch traced here: 68.8 us
  Pallas kernels  55.7 us (81%)
  other arithmetic  9.76 us (14%)
  local copies, waits for them, and re-layouts  2.64 us (4%)
  between operations  0.7 us (1%)
    pallas_call x1, Pallas kernels, body(): pl.pallas_call(mixer_kernel, in_specs=[anywhere] * 5 + [vmem], out_specs=...  55.7 us
    convert_element_type x1, other arithmetic, mul16(): return (a.astype(f32) * b.astype(f32)).astype(bf16)  7.03 us

profile of v5, /device:TPU:0, one launch (start us, length us, event | category | flops | bytes accessed | tf_op | source)
XLA Modules:
  0.0 68.8 jit_solution(897465968744683244)
XLA Ops:
  0.6 0.8 %fusion.7 = (f32[64]{0:T(128)S(1)}, f32[64]{0:T(128)S(1)}) fusion(f32[128]{0:T(128)} %param.14), kind=kLoop, calls=%fused_computation.22 | loop fusion | bytes 1024 | tf_op jit(solution)/shard_map/jit(_roll_static)/slice | solution.py:426
  1.4 0.1 maximum_bitcast_fusion
  1.5 0.7 select_maximum_fusion
  2.2 0.7 %fusion.6 = (f32[128,16]{0,1:T(8,128)S(1)}, f32[128,16]{0,1:T(8,128)S(1)}) fusion(f32[128,16]{0,1:T(8,128)} %param.13, f32[128,16]{0,1:T(8,128)} %param.12), kind=kLoop, calls=%fused_computation.21 | loop fusion | flops 6144 | bytes 32768 | tf_op jit(solution)/shard_map/exp | solution.py:424
  2.9 0.1 copy.25
  3.0 0.1 reshape.48
  3.1 0.1 copy.26
  3.2 0.1 reshape.49
  3.3 0.0 copy-start
  3.3 1.1 %copy-done = f32[640,256]{1,0:T(8,128)S(1)} copy-done((f32[640,256]{1,0:T(8,128)S(1)}, f32[640,256]{1,0:T(8,128)}, u32[]{:S(2)}) %copy-start) | copy-done | bytes 655384
  4.4 0.0 copy-start.2
  4.4 0.0 copy-start.3
  4.4 0.0 copy-start.1
  4.4 55.7 %mixer.1 = (bf16[16,2,2,2,64,128]{5,4,3,2,1,0:T(8,128)(2,1)}, bf16[16,2,2,2,64,128]{5,4,3,2,1,0:T(8,128)(2,1)}, f32[2,16,256]{2,1,0:T(8,128)S(1)}) custom-call(bf16[16,2,2,2,64,128]{5,4,3,2,1,0:T(8,128)(2,1)} %bitcast.20, bf16[16,2,2,2,64,128]{5,4,3,2,1,0:T(8,128)(2,1)} %bitcast.21, bf16[16,2,2,2,64,128]{5,4,3,2,1,0:T(8,128)(2,1)} %bitcast.22, ...), custom_call_target="tpu_custom_call" | custom-call | tf_op jit(solution)/shard_map/mixer/pallas_call | solution.py:448
  60.1 0.1 slice_bitcast_fusion.1
  60.2 0.6 maximum_multiply_fusion
  60.7 0.1 reshape.51
  60.8 0.1 copy.29
  60.9 0.1 reshape.50
  61.0 0.1 copy.27
  61.0 0.0 copy-done.2
  61.1 0.0 copy-done.3
  61.1 0.7 multiply_multiply_fusion
  61.7 0.0 copy-done.1
  61.7 7.0 %fusion.1 = (bf16[8192,128]{1,0:T(8,128)(2,1)}, bf16[8192,128]{1,0:T(8,128)(2,1)}, bf16[8192,128]{1,0:T(8,128)(2,1)}, bf16[8192,128]{1,0:T(8,128)(2,1)}) fusion(bf16[8192,128]{1,0:T(8,128)(2,1)S(1)} %copy-done.1, bf16[16,2,2,2,64,128]{5,4,3,2,1,0:T(8,128)(2,1)} %get-tuple-element.10, bf16[8192,128]{1,0:T(8,128)(2,1)} %param.8, bf16[8192,128]{1,0:T(8,128)(2,1)} %param.10, ...), kind=kLoop, calls=%fused_computation.5 | loop fusion | flops 14680064 | bytes 20971520 | tf_op jit(solution)/shard_map/convert_element_type | solution.py:62
  (2 shorter events, 0.0 us)
Async XLA Ops:
  3.3 1.1 %copy-start = (f32[640,256]{1,0:T(8,128)S(1)}, f32[640,256]{1,0:T(8,128)}, u32[]{:S(2)}) copy-start(f32[640,256]{1,0:T(8,128)} %constant.10.clone.tab_hbm) | copy-start | bytes 1966084
  4.4 56.6 %copy-start.2 = (f32[128,16]{0,1:T(8,128)S(1)}, f32[128,16]{0,1:T(8,128)}, u32[]{:S(2)}) copy-start(f32[128,16]{0,1:T(8,128)} %param.13) | copy-start | bytes 24580
  4.4 56.6 %copy-start.3 = (f32[128,16]{0,1:T(8,128)S(1)}, f32[128,16]{0,1:T(8,128)}, u32[]{:S(2)}) copy-start(f32[128,16]{0,1:T(8,128)} %param.12) | copy-start | bytes 24580
  4.4 57.3 %copy-start.1 = (bf16[8192,128]{1,0:T(8,128)(2,1)S(1)}, bf16[8192,128]{1,0:T(8,128)(2,1)}, u32[]{:S(2)}) copy-start(bf16[8192,128]{1,0:T(8,128)(2,1)} %param.11) | copy-start | bytes 6291460

commit v6 on v5

--- a/solution.py
+++ b/solution.py
@@ -17,16 +17,11 @@
 LANES = 256
 
 
-def tables():
+def table():
     n = np.arange(W)[:, None]
     f = np.arange(W)[None, :]
     angle = ((2 * f + 1) * n % (4 * W)) * (2.0 * math.pi / (4 * W))
-    fwd = np.concatenate([np.cos(angle), -np.sin(angle)], axis=1)
-    inv = fwd.T / W
-    flip = np.eye(W)[::-1]
-    pad = np.concatenate([flip, np.zeros((W, W))], axis=1)
-    packed = np.concatenate([fwd, fwd[::-1], np.concatenate([inv, inv[:, ::-1]], axis=1), pad])
-    return jnp.asarray(packed, f32)
+    return jnp.asarray(np.concatenate([np.cos(angle), -np.sin(angle)], axis=1), f32)
 
 
 def dot(a, b):
@@ -72,8 +67,9 @@
 
 
 def mixer_kernel(
-    q_hbm, k_hbm, v_hbm, c_hbm, tab_hbm, own_ref, mixed_hbm, pgrad_hbm, total_ref,
-    tab32, tab, inp, away, sig, rev, lags, skip, par, keep, st_out, came, hold, ready, got,
+    q_hbm, k_hbm, v_hbm, c_hbm, tab_ref, rate_ref, weight_ref, bias_ref,
+    mixed_ref, pgrad_ref, total_ref,
+    fwd_ref, fwdr_ref, inv_ref, invr_ref, flip_ref, inp, away, sig, rev, lags, skip, par, keep, st_out, came, hold, ready, got,
     grad_out, grad_in, mine, theirs, stage,
     load_sem, par_sem, pair_sem, st_sem, back_sem, grad_sem, out_sem, twin_sem,
 ):
@@ -106,7 +102,6 @@
                     ref.at[:, :, side, half], inp.at[order, n, pl.ds(half * pairs, pairs)],
                     load_sem.at[order],
                 ).start()
-    pltpu.make_async_copy(tab_hbm, tab32, load_sem.at[2]).start()
 
     barrier = pltpu.get_barrier_semaphore()
 
@@ -118,38 +113,49 @@
     pl.semaphore_signal(barrier, inc=1, device_id=near, device_id_type=MESH)
     pl.semaphore_signal(barrier, inc=1, device_id=twin, device_id_type=MESH)
 
-    own = own_ref[...]
-    low = own - own.astype(bf16).astype(f32)
+    own_rate, own_weight = rate_ref[...], weight_ref[...]
+    own_bias = jnp.broadcast_to(bias_ref[...], (HALF, W))
+    own_bias = jnp.concatenate([own_bias, pltpu.roll(own_bias, W // 2, 1)], axis=1)
+    own_bias = [own_bias[:1], pltpu.roll(own_bias, W, 1)[:1]]
+    lower = lambda z: z - z.astype(bf16).astype(f32)
     for half in range(2):
         rows = slice(quad * half, quad * half + quad)
         par[chip, half] = jnp.concatenate(
             [
-                own[:8][rows],
-                low[:8][rows],
-                own[8:16][rows],
-                own[16 + half : 17 + half],
-                low[16 + half : 17 + half],
-                own[17 - half : 18 - half],
-                low[17 - half : 18 - half],
+                own_rate[rows],
+                lower(own_rate)[rows],
+                own_weight[rows],
+                own_bias[half],
+                lower(own_bias[half]),
+                own_bias[1 - half],
+                lower(own_bias[1 - half]),
             ],
             axis=0,
         ).astype(bf16)
 
-    fwd_ref, fwdr_ref = tab.at[0:W], tab.at[W : 2 * W]
-    inv_ref, invr_ref = tab.at[2 * W : 4 * W, 0:W], tab.at[2 * W : 4 * W, W : 2 * W]
-    flip_ref = tab.at[4 * W : 5 * W, 0:W]
+    row_no = lax.broadcasted_iota(jnp.int32, (W, W), 0)
+    lane_no = lax.broadcasted_iota(jnp.int32, (W, W), 1)
+    fwd = tab_ref[...]
+    flip = (row_no + lane_no == W - 1).astype(f32).astype(bf16)
+    inv = (jnp.transpose(fwd) * (1.0 / W)).astype(bf16)
+    fwd = fwd.astype(bf16)
+    flip_ref[...] = flip
+    fwd_ref[...] = fwd
+    inv_ref[...] = inv
+    fwdr_ref[...] = dot(flip, fwd).astype(bf16)
+    invr_ref[...] = dot(inv, flip).astype(bf16)
 
     pieces = 4
     count = chips // pieces
 
     def products(order, dst, first):
         def step(i, carry):
-            for v in (first + 2 * i, first + 2 * i + 1):
+            for v in [first + 4 * i + n for n in range(4)]:
                 dst[0, v] = mul16(inp[order, 1, v], inp[order, 2, v]).reshape(W, W)
                 dst[1, v] = mul16(inp[order, 3, v], inp[order, 0, v]).reshape(W, W)
             return carry
 
-        lax.fori_loop(0, count // 2, step, 0)
+        lax.fori_loop(0, count // 4, step, 0)
 
     def send_par(i, carry):
         remote(
@@ -170,11 +176,7 @@
     wait_bytes(inp.at[1], load_sem.at[1])
     for n in range(pieces):
         products(1, sig.at[core], n * count)
-    wait_bytes(tab32, load_sem.at[2])
-    tab[...] = tab32[...].astype(bf16)
-
-    row_no = lax.broadcasted_iota(jnp.int32, (W, W), 0)
-    lane_no = lax.broadcasted_iota(jnp.int32, (W, W), 1)
+
     eye = row_no == lane_no
     swapped_eye = lax.rem(row_no + W // 2, W) == lane_no
     lane = lax.broadcasted_iota(jnp.int32, (W, W), 1).astype(f32)
@@ -201,15 +203,18 @@
                     jnp.sum(jnp.where(where, sums, 0.0), axis=0, keepdims=True), (HALF, W)
                 )
 
-    for n in range(pieces):
-        block = pl.ds(n * count, count)
-        wait_bytes(sig.at[core, :, block], pair_sem.at[n])
-
-        def step(i, carry, n=n):
-            local_lags(n * count + 4 * i, 4)
-            return carry
-
-        lax.fori_loop(0, count // 4, step, 0)
+    def lags_of(half):
+        for n in range(half * pieces // 2, (half + 1) * pieces // 2):
+            block = pl.ds(n * count, count)
+            wait_bytes(sig.at[core, :, block], pair_sem.at[n])
+
+            def step(i, carry, n=n):
+                local_lags(n * count + 4 * i, 4)
+                return carry
+
+            lax.fori_loop(0, count // 4, step, 0)
+
+    lags_of(0)
     wait_bytes(par.at[pl.ds(0, chips - 1)], par_sem.at[1])
 
     def place(j, n):
@@ -269,20 +274,20 @@
     def scan(half):
         came[half, chip] = st_out[half, chip]
         wait_bytes(came.at[half, pl.ds(0, chips - 1)], st_sem.at[half, 1])
-        decay2 = jnp.exp(-2.0 * float(W) * own[quad * half : quad * half + quad])
+        decay2 = jnp.exp(-2.0 * float(W) * own_rate[quad * half : quad * half + quad])
 
         def ahead(p, s):
             hold[p, 0:quad] = s
             return s * decay2 + came[half, p][:quad]
 
-        lax.fori_loop(0, chips, ahead, jnp.zeros((quad, LANES), f32))
+        lax.fori_loop(0, chips, ahead, jnp.zeros((quad, LANES), f32), unroll=8)
 
         def back(i, s):
             p = chips - 1 - i
             ready[half, p] = jnp.concatenate([hold[p, 0:quad], s], axis=0)
             return s * decay2 + came[half, p][quad:]
 
-        lax.fori_loop(0, chips, back, jnp.zeros((quad, LANES), f32))
+        lax.fori_loop(0, chips, back, jnp.zeros((quad, LANES), f32), unroll=8)
 
         def send_back(i, carry):
             b = after(i)
@@ -304,9 +309,7 @@
     def send_grads(half):
         wait_bytes(got.at[half, pl.ds(0, chips - 1)], back_sem.at[half, 1])
 
-        def step(i, carry):
-            u = lax.rem(lax.div(chip, 2) + 1 + i, pairs)
-            v = half * pairs + u
+        def made(u, v):
             rate = get_rate(get_par(half, u))
             near_decay = jnp.exp(-rate)
             s0, s1, r0, r1 = chunk_states(half, u, v, rate)
@@ -315,28 +318,38 @@
                 float(W) * jnp.exp(-float(W) * rate) * (s0 * r0 + s1 * r1)
                 + s0 * keep[v, 6] + r0 * keep[v, 7] + s1 * keep[v, 8] + r1 * keep[v, 9]
             )
+            messages = []
             for n in range(2):
                 rows = slice(quad * n, quad * n + quad)
                 first = 0 if n == half else HALF
                 skip_part = jnp.concatenate(
                     [skip[v, first : first + HALF], jnp.zeros((HALF, W), f32)], axis=1
                 )
-                grad_out[half, 2 * u + n] = jnp.concatenate(
-                    [grad_a[rows], grad_d[rows], skip_part], axis=0
-                ).astype(bf16)
-            for n in range(2):
-                b = 2 * u + n
-
-                @pl.when(b != chip)
-                def _(b=b):
-                    remote(
-                        grad_out.at[half, b], grad_in.at[half, chip], grad_sem.at[half, 0],
-                        grad_sem.at[half, 1], peer(b),
-                    ).start()
+                messages.append(
+                    jnp.concatenate([grad_a[rows], grad_d[rows], skip_part], axis=0).astype(bf16)
+                )
+            return messages
+
+        def step(i, carry):
+            us = [lax.rem(lax.div(chip, 2) + 1 + 4 * i + n, pairs) for n in range(4)]
+            results = [made(u, half * pairs + u) for u in us]
+            for u, messages in zip(us, results):
+                for n in range(2):
+                    grad_out[half, 2 * u + n] = messages[n]
+            for u in us:
+                for n in range(2):
+                    b = 2 * u + n
+
+                    @pl.when(b != chip)
+                    def _(b=b):
+                        remote(
+                            grad_out.at[half, b], grad_in.at[half, chip], grad_sem.at[half, 0],
+                            grad_sem.at[half, 1], peer(b),
+                        ).start()
 
             return carry
 
-        lax.fori_loop(0, pairs, step, 0)
+        lax.fori_loop(0, pairs // 4, step, 0)
         grad_in[half, chip] = grad_out[half, chip]
 
     def expand(half, u, v):
@@ -377,18 +390,26 @@
         grown = [expand(*where) for where in places]
         results = [convolve(*where, *terms) for where, terms in zip(places, grown)]
         for (half, u, v), result in zip(places, results):
-            for chunk in range(2):
-                for n in range(2):
-                    stage[chunk, n, v] = result[n][W * chunk : W * chunk + W].reshape(2, W // 2, W)
+            for n, out in enumerate((mixed_ref, pgrad_ref)):
+                both = [
+                    result[n][W * chunk : W * chunk + W].reshape(2, W // 2, W) for chunk in range(2)
+                ]
+                mine_first = core == 0
+                kept = jnp.where(mine_first, both[0], both[1])
+                stage[n, v] = jnp.where(mine_first, both[1], both[0])
+                for side in range(2):
+                    out[u, side, core, half] = kept[side]
         for half, u, v in places:
-            for n, out in enumerate((mixed_hbm, pgrad_hbm)):
-                spot = out.at[u, :, core, half]
-                pltpu.make_async_copy(stage.at[core, n, v], spot, out_sem.at[2]).start()
-                remote(stage.at[1 - core, n, v], spot, out_sem.at[0], out_sem.at[1], near).start()
+            for n, out in enumerate((mixed_ref, pgrad_ref)):
+                remote(
+                    stage.at[n, v], out.at[u, :, core, half], out_sem.at[0], out_sem.at[1], near
+                ).start()
         return carry
 
-    middle = steps + 5 * steps // 8
-    lax.fori_loop(0, middle, sum_step, 0)
+    middle = steps + steps // 8
+    lax.fori_loop(0, steps, sum_step, 0)
+    lags_of(1)
+    lax.fori_loop(steps, middle, sum_step, 0)
     scan(0)
     lax.fori_loop(middle, 2 * steps, sum_step, 0)
     send_grads(0)
@@ -401,7 +422,8 @@
     for half in range(2):
         wait_bytes(grad_in.at[half, pl.ds(0, chips - 1)], grad_sem.at[half, 1])
         mine[half] = lax.fori_loop(
-            0, chips, lambda p, t: t + grad_in[half, p].astype(f32), jnp.zeros((16, LANES), f32)
+            0, chips, lambda p, t: t + grad_in[half, p].astype(f32), jnp.zeros((16, LANES), f32),
+            unroll=8,
         )
     swap = remote(mine, theirs, twin_sem.at[0], twin_sem.at[1], twin)
     swap.start()
@@ -412,8 +434,8 @@
         wait_bytes(st_out.at[half, pl.ds(0, chips - 1)], st_sem.at[half, 0])
         wait_bytes(ready.at[half, pl.ds(0, chips - 1)], back_sem.at[half, 0])
         wait_bytes(grad_out.at[half, pl.ds(0, chips - 1)], grad_sem.at[half, 0])
-    for n in range(3):
-        wait_bytes(stage.at[0], out_sem.at[n])
+    for n in range(2):
+        wait_bytes(stage, out_sem.at[n])
     swap.wait()
     total_ref[...] = mine[...] + theirs[...]
 
@@ -423,16 +445,8 @@
     channels, width = query.shape
     rate = jnp.exp(log_rate)
     root = jnp.sqrt(-jnp.expm1(-2.0 * rate))
-    bias_rows = jnp.stack([bias, jnp.roll(bias, W // 2)])
-    bias_rows = jnp.pad(bias_rows, ((0, 6), (0, LANES - W)))
-    own = jnp.concatenate(
-        [
-            rate.reshape(HALF, LANES),
-            (residue * root).reshape(HALF, LANES),
-            bias_rows,
-        ],
-        axis=0,
-    )
+    rate_rows = rate.reshape(HALF, LANES)
+    weight_rows = (residue * root).reshape(HALF, LANES)
     vmem = pl.BlockSpec(memory_space=pltpu.VMEM)
     dma = pltpu.SemaphoreType.DMA
 
@@ -447,12 +461,15 @@
     part = jax.ShapeDtypeStruct((chips // 2, 2, 2, 2, W // 2, width), bf16)
     mixed, pgrad, total = pl.pallas_call(
         mixer_kernel,
-        in_specs=[anywhere] * 5 + [vmem],
-        out_specs=[anywhere, anywhere, vmem],
+        in_specs=[anywhere] * 4 + [vmem] * 4,
+        out_specs=[vmem] * 3,
         out_shape=[part, part, jax.ShapeDtypeStruct((2, 16, LANES), f32)],
         scratch_shapes=[
-            pltpu.VMEM((5 * W, LANES), f32),
-            pltpu.VMEM((5 * W, LANES), bf16),
+            pltpu.VMEM((W, 2 * W), bf16),
+            pltpu.VMEM((W, 2 * W), bf16),
+            pltpu.VMEM((2 * W, W), bf16),
+            pltpu.VMEM((2 * W, W), bf16),
+            pltpu.VMEM((W, W), bf16),
             pltpu.VMEM((2, 4, chips, 2, W // 2, W), bf16),
             pltpu.VMEM((2, chips, W, W), bf16),
             pltpu.VMEM((2, 2, chips, W, W), bf16),
@@ -470,19 +487,20 @@
             pltpu.VMEM((2, chips, 16, LANES), bf16),
             pltpu.VMEM((2, 16, LANES), f32),
             pltpu.VMEM((2, 16, LANES), f32),
-            pltpu.VMEM((2, 2, chips, 2, W // 2, W), bf16),
-            dma((3,)),
+            pltpu.VMEM((2, chips, 2, W // 2, W), bf16),
+            dma((2,)),
             dma((2,)),
             dma((5,)),
             dma((2, 2)),
             dma((2, 2)),
             dma((2, 2)),
-            dma((3,)),
+            dma((2,)),
             dma((2,)),
         ],
         compiler_params=remote(1),
         name="mixer",
-    )(split(query), split(key_in), split(value_in), split(cotangent), tables(), own)
+    )(split(query), split(key_in), split(value_in), split(cotangent), table(), rate_rows,
+      weight_rows, bias.reshape(1, W))
     mixed = mixed.reshape(channels, width)
     pgrad = pgrad.reshape(channels, width)
     gated, gq = mul16(query, mixed), mul16(cotangent, mixed)

time: 69 us -> 69.3 us (level)
  Pallas kernels: 55.7 us -> 57.1 us
  other arithmetic: 9.76 us -> 9.02 us
    pallas_call x1, Pallas kernels: 55.7 us -> 57.1 us  [body(): pl.pallas_call(mixer_kernel, in_specs=[anywhere] * 4 + [vmem] * 4, out_sp...]
    slice x1 -> x0, local copies, waits for them, and re-layouts: 0.8 us -> none  [body(): bias_rows = jnp.stack([bias, jnp.roll(bias, W // 2)])]
    another operation x2 -> x0, other arithmetic: 0.74 us -> none  [body(): bias_rows = jnp.stack([bias, jnp.roll(bias, W // 2)])]
    mul x0 -> x1, other arithmetic: none -> 0.74 us  [body(): weight_rows = (residue * root).reshape(HALF, LANES)]
    exp x1 -> x0, other arithmetic: 0.73 us -> none  [body(): rate = jnp.exp(log_rate)]
    unnamed x8 -> x10, local copies, waits for them, and re-layouts: 1.09 us -> 1.57 us
where the time goes in v6:
time: 69.3 us; the launch traced here: 69.1 us
  Pallas kernels  57.1 us (82%)
  other arithmetic  9.02 us (13%)
  local copies, waits for them, and re-layouts  2.3 us (3%)
    pallas_call x1, Pallas kernels, body(): pl.pallas_call(mixer_kernel, in_specs=[anywhere] * 4 + [vmem] * 4, out_sp...  57.1 us
    convert_element_type x1, other arithmetic, mul16(): return (a.astype(f32) * b.astype(f32)).astype(bf16)  7.03 us
    unnamed x10, local copies, waits for them, and re-layouts  1.57 us

profile of v6, /device:TPU:0, one launch (start us, length us, event | category | flops | bytes accessed | tf_op | source)
XLA Modules:
  0.0 69.1 jit_solution(15513674488494059387)
XLA Ops:
  0.6 0.7 %fusion.4 = (f32[128,16]{0,1:T(8,128)S(1)}, f32[128,16]{0,1:T(8,128)S(1)}) fusion(f32[128,16]{0,1:T(8,128)} %param.12, f32[128,16]{0,1:T(8,128)} %param.13), kind=kLoop, calls=%fused_computation.11 | loop fusion | flops 6144 | bytes 32768 | tf_op jit(solution)/shard_map/mul | solution.py:449
  1.4 0.1 copy.26
  1.5 0.1 reshape.52.weight_ref
  1.6 0.1 copy.25
  1.7 0.1 reshape.51.rate_ref
  1.8 0.0 copy-start
  1.8 0.9 %copy-done = f32[128,256]{1,0:T(8,128)S(1)} copy-done((f32[128,256]{1,0:T(8,128)S(1)}, f32[128,256]{1,0:T(8,128)}, u32[]{:S(2)}) %copy-start) | copy-done | bytes 131096
  2.7 0.0 copy-start.1
  2.7 0.7 copy-done.1
  3.3 0.0 copy-start.3
  3.3 0.0 copy-start.4
  3.3 0.0 copy-start.2
  3.3 57.1 %mixer.1 = (bf16[16,2,2,2,64,128]{5,4,3,2,1,0:T(8,128)(2,1)}, bf16[16,2,2,2,64,128]{5,4,3,2,1,0:T(8,128)(2,1)}, f32[2,16,256]{2,1,0:T(8,128)S(1)}) custom-call(bf16[16,2,2,2,64,128]{5,4,3,2,1,0:T(8,128)(2,1)} %bitcast.19, bf16[16,2,2,2,64,128]{5,4,3,2,1,0:T(8,128)(2,1)} %bitcast.20, bf16[16,2,2,2,64,128]{5,4,3,2,1,0:T(8,128)(2,1)} %bitcast.21, ...), custom_call_target="tpu_custom_call" | custom-call | tf_op jit(solution)/shard_map/mixer/pallas_call | solution.py:462
  60.5 0.1 slice_bitcast_fusion.1
  60.5 0.6 maximum_multiply_fusion
  61.1 0.1 reshape.55
  61.2 0.1 copy.29
  61.3 0.1 reshape.54
  61.4 0.1 copy.27
  61.4 0.0 copy-done.3
  61.4 0.0 copy-done.4
  61.4 0.7 multiply_multiply_fusion
  62.1 0.0 copy-done.2
  62.1 7.0 %fusion.1 = (bf16[8192,128]{1,0:T(8,128)(2,1)}, bf16[8192,128]{1,0:T(8,128)(2,1)}, bf16[8192,128]{1,0:T(8,128)(2,1)}, bf16[8192,128]{1,0:T(8,128)(2,1)}) fusion(bf16[8192,128]{1,0:T(8,128)(2,1)S(1)} %copy-done.2, bf16[16,2,2,2,64,128]{5,4,3,2,1,0:T(8,128)(2,1)} %get-tuple-element.10, bf16[8192,128]{1,0:T(8,128)(2,1)} %param.8, bf16[8192,128]{1,0:T(8,128)(2,1)} %param.10, ...), kind=kLoop, calls=%fused_computation.5 | loop fusion | flops 14680064 | bytes 20971520 | tf_op jit(solution)/shard_map/convert_element_type | solution.py:57
  (1 shorter events, 0.0 us)
Async XLA Ops:
  1.8 0.9 %copy-start = (f32[128,256]{1,0:T(8,128)S(1)}, f32[128,256]{1,0:T(8,128)}, u32[]{:S(2)}) copy-start(f32[128,256]{1,0:T(8,128)} %constant.2.clone.tab_ref) | copy-start | bytes 393220
  2.7 0.7 copy-start.1
  3.3 58.1 %copy-start.3 = (f32[128,16]{0,1:T(8,128)S(1)}, f32[128,16]{0,1:T(8,128)}, u32[]{:S(2)}) copy-start(f32[128,16]{0,1:T(8,128)} %param.12) | copy-start | bytes 24580
  3.3 58.1 %copy-start.4 = (f32[128,16]{0,1:T(8,128)S(1)}, f32[128,16]{0,1:T(8,128)}, u32[]{:S(2)}) copy-start(f32[128,16]{0,1:T(8,128)} %param.13) | copy-start | bytes 24580
  3.3 58.8 %copy-start.2 = (bf16[8192,128]{1,0:T(8,128)(2,1)S(1)}, bf16[8192,128]{1,0:T(8,128)(2,1)}, u32[]{:S(2)}) copy-start(bf16[8192,128]{1,0:T(8,128)(2,1)} %param.11) | copy-start | bytes 6291460

commit v7 on v6

--- a/solution.py
+++ b/solution.py
@@ -215,6 +215,7 @@
             lax.fori_loop(0, count // 4, step, 0)
 
     lags_of(0)
+    lags_of(1)
     wait_bytes(par.at[pl.ds(0, chips - 1)], par_sem.at[1])
 
     def place(j, n):
@@ -406,9 +407,8 @@
                 ).start()
         return carry
 
-    middle = steps + steps // 8
+    middle = steps + 5 * steps // 8
     lax.fori_loop(0, steps, sum_step, 0)
-    lags_of(1)
     lax.fori_loop(steps, middle, sum_step, 0)
     scan(0)
     lax.fori_loop(middle, 2 * steps, sum_step, 0)
@@ -452,7 +452,7 @@
 
     def remote(number):
         return pltpu.CompilerParams(
-            collective_id=number, has_side_effects=True, vmem_limit_bytes=52 * 1024 * 1024
+            collective_id=number, has_side_effects=True, vmem_limit_bytes=49 * 1024 * 1024
         )
 
     chips = shards // 2

time: 69.3 us -> 67.9 us (0.980)
  Pallas kernels: 57.1 us -> 54.2 us
  local copies, waits for them, and re-layouts: 2.3 us -> 3.63 us
    pallas_call x1, Pallas kernels: 57.1 us -> 54.2 us  [body(): pl.pallas_call(mixer_kernel, in_specs=[anywhere] * 4 + [vmem] * 4, out_sp...]
    unnamed x10, local copies, waits for them, and re-layouts: 1.57 us -> 2.89 us
where the time goes in v7:
time: 67.9 us; the launch traced here: 67.7 us
  Pallas kernels  54.2 us (80%)
  other arithmetic  9.1 us (13%)
  local copies, waits for them, and re-layouts  3.63 us (5%)
  between operations  0.7 us (1%)
    pallas_call x1, Pallas kernels, body(): pl.pallas_call(mixer_kernel, in_specs=[anywhere] * 4 + [vmem] * 4, out_sp...  54.2 us
    convert_element_type x1, other arithmetic, mul16(): return (a.astype(f32) * b.astype(f32)).astype(bf16)  7.11 us
    unnamed x10, local copies, waits for them, and re-layouts  2.89 us

profile of v7, /device:TPU:0, one launch (start us, length us, event | category | flops | bytes accessed | tf_op | source)
XLA Modules:
  0.0 67.7 jit_solution(14748865925474613383)
XLA Ops:
  0.6 0.7 %fusion.4 = (f32[128,16]{0,1:T(8,128)S(1)}, f32[128,16]{0,1:T(8,128)S(1)}) fusion(f32[128,16]{0,1:T(8,128)} %param.12, f32[128,16]{0,1:T(8,128)} %param.13), kind=kLoop, calls=%fused_computation.11 | loop fusion | flops 6144 | bytes 32768 | tf_op jit(solution)/shard_map/mul | solution.py:449
  1.4 0.1 copy.26
  1.5 0.1 reshape.52.weight_ref
  1.6 0.1 copy.25
  1.7 0.1 reshape.51.rate_ref
  1.8 0.0 copy-start.1
  1.8 0.9 %copy-done.1 = f32[128,256]{1,0:T(8,128)S(1)} copy-done((f32[128,256]{1,0:T(8,128)S(1)}, f32[128,256]{1,0:T(8,128)}, u32[]{:S(2)}) %copy-start.1) | copy-done | bytes 131096
  2.7 0.0 copy-start.2
  2.7 0.7 copy-done.2
  3.3 0.0 copy-start.3
  3.3 0.0 copy-start.4
  3.3 54.2 %mixer.1 = (bf16[16,2,2,2,64,128]{5,4,3,2,1,0:T(8,128)(2,1)S(1)}, bf16[16,2,2,2,64,128]{5,4,3,2,1,0:T(8,128)(2,1)S(1)}, f32[2,16,256]{2,1,0:T(8,128)S(1)}) custom-call(bf16[16,2,2,2,64,128]{5,4,3,2,1,0:T(8,128)(2,1)} %bitcast.19, bf16[16,2,2,2,64,128]{5,4,3,2,1,0:T(8,128)(2,1)} %bitcast.20, bf16[16,2,2,2,64,128]{5,4,3,2,1,0:T(8,128)(2,1)} %bitcast.21, ...), custom_call_target="tpu_custom_call" | custom-call | tf_op jit(solution)/shard_map/mixer/pallas_call | solution.py:462
  57.6 0.0 copy-start
  57.6 1.3 %copy-done = bf16[16,2,2,2,64,128]{5,4,3,2,1,0:T(8,128)(2,1)} copy-done((bf16[16,2,2,2,64,128]{5,4,3,2,1,0:T(8,128)(2,1)}, bf16[16,2,2,2,64,128]{5,4,3,2,1,0:T(8,128)(2,1)S(1)}, u32[]{:S(2)}) %copy-start) | copy-done | bytes 2097176
  58.9 0.1 slice_bitcast_fusion.1
  59.0 0.6 maximum_multiply_fusion
  59.6 0.1 reshape.55
  59.7 0.1 copy.29
  59.7 0.1 reshape.54
  59.8 0.1 copy.27
  59.9 0.0 copy-done.3
  59.9 0.0 copy-done.4
  59.9 0.7 multiply_multiply_fusion
  60.6 7.1 %fusion.1 = (bf16[8192,128]{1,0:T(8,128)(2,1)}, bf16[8192,128]{1,0:T(8,128)(2,1)}, bf16[8192,128]{1,0:T(8,128)(2,1)}, bf16[8192,128]{1,0:T(8,128)(2,1)}) fusion(bf16[8192,128]{1,0:T(8,128)(2,1)} %param.11, bf16[16,2,2,2,64,128]{5,4,3,2,1,0:T(8,128)(2,1)S(1)} %get-tuple-element.10, bf16[8192,128]{1,0:T(8,128)(2,1)} %param.8, bf16[8192,128]{1,0:T(8,128)(2,1)} %param.10, ...), kind=kLoop, calls=%fused_computation.5 | loop fusion | flops 14680064 | bytes 20971520 | tf_op jit(solution)/shard_map/convert_element_type | solution.py:57
  (1 shorter events, 0.0 us)
Async XLA Ops:
  1.8 0.9 %copy-start.1 = (f32[128,256]{1,0:T(8,128)S(1)}, f32[128,256]{1,0:T(8,128)}, u32[]{:S(2)}) copy-start(f32[128,256]{1,0:T(8,128)} %constant.2.clone.tab_ref) | copy-start | bytes 393220
  2.7 0.7 copy-start.2
  3.3 56.6 %copy-start.3 = (f32[128,16]{0,1:T(8,128)S(1)}, f32[128,16]{0,1:T(8,128)}, u32[]{:S(2)}) copy-start(f32[128,16]{0,1:T(8,128)} %param.12) | copy-start | bytes 24580
  3.3 56.6 %copy-start.4 = (f32[128,16]{0,1:T(8,128)S(1)}, f32[128,16]{0,1:T(8,128)}, u32[]{:S(2)}) copy-start(f32[128,16]{0,1:T(8,128)} %param.13) | copy-start | bytes 24580
  57.6 1.3 %copy-start = (bf16[16,2,2,2,64,128]{5,4,3,2,1,0:T(8,128)(2,1)}, bf16[16,2,2,2,64,128]{5,4,3,2,1,0:T(8,128)(2,1)S(1)}, u32[]{:S(2)}) copy-start(bf16[16,2,2,2,64,128]{5,4,3,2,1,0:T(8,128)(2,1)S(1)} %get-tuple-element.11) | copy-start | bytes 6291460

commit v8 on v7

--- a/solution.py
+++ b/solution.py
@@ -207,12 +207,7 @@
         for n in range(half * pieces // 2, (half + 1) * pieces // 2):
             block = pl.ds(n * count, count)
             wait_bytes(sig.at[core, :, block], pair_sem.at[n])
-
-            def step(i, carry, n=n):
-                local_lags(n * count + 4 * i, 4)
-                return carry
-
-            lax.fori_loop(0, count // 4, step, 0)
+            local_lags(n * count, count)
 
     lags_of(0)
     lags_of(1)

time: 67.9 us -> 67.9 us (level)
  no operation moved by 1% of the time
where the time goes in v8:
time: 67.9 us; the launch traced here: 67.7 us
  Pallas kernels  54.2 us (80%)
  other arithmetic  9.1 us (13%)
  local copies, waits for them, and re-layouts  3.63 us (5%)
  between operations  0.7 us (1%)
    pallas_call x1, Pallas kernels, body(): pl.pallas_call(mixer_kernel, in_specs=[anywhere] * 4 + [vmem] * 4, out_sp...  54.2 us
    convert_element_type x1, other arithmetic, mul16(): return (a.astype(f32) * b.astype(f32)).astype(bf16)  7.11 us
    unnamed x10, local copies, waits for them, and re-layouts  2.89 us

profile of v8, /device:TPU:0, one launch (start us, length us, event | category | flops | bytes accessed | tf_op | source)
XLA Modules:
  0.0 67.7 jit_solution(6339128708026468062)
XLA Ops:
  0.6 0.7 %fusion.4 = (f32[128,16]{0,1:T(8,128)S(1)}, f32[128,16]{0,1:T(8,128)S(1)}) fusion(f32[128,16]{0,1:T(8,128)} %param.12, f32[128,16]{0,1:T(8,128)} %param.13), kind=kLoop, calls=%fused_computation.11 | loop fusion | flops 6144 | bytes 32768 | tf_op jit(solution)/shard_map/mul | solution.py:444
  1.4 0.1 copy.26
  1.5 0.1 reshape.52.weight_ref
  1.6 0.1 copy.25
  1.7 0.1 reshape.51.rate_ref
  1.8 0.0 copy-start.1
  1.8 0.9 %copy-done.1 = f32[128,256]{1,0:T(8,128)S(1)} copy-done((f32[128,256]{1,0:T(8,128)S(1)}, f32[128,256]{1,0:T(8,128)}, u32[]{:S(2)}) %copy-start.1) | copy-done | bytes 131096
  2.7 0.0 copy-start.2
  2.7 0.7 copy-done.2
  3.3 0.0 copy-start.3
  3.3 0.0 copy-start.4
  3.3 54.2 %mixer.1 = (bf16[16,2,2,2,64,128]{5,4,3,2,1,0:T(8,128)(2,1)S(1)}, bf16[16,2,2,2,64,128]{5,4,3,2,1,0:T(8,128)(2,1)S(1)}, f32[2,16,256]{2,1,0:T(8,128)S(1)}) custom-call(bf16[16,2,2,2,64,128]{5,4,3,2,1,0:T(8,128)(2,1)} %bitcast.19, bf16[16,2,2,2,64,128]{5,4,3,2,1,0:T(8,128)(2,1)} %bitcast.20, bf16[16,2,2,2,64,128]{5,4,3,2,1,0:T(8,128)(2,1)} %bitcast.21, ...), custom_call_target="tpu_custom_call" | custom-call | tf_op jit(solution)/shard_map/mixer/pallas_call | solution.py:457
  57.6 0.0 copy-start
  57.6 1.3 %copy-done = bf16[16,2,2,2,64,128]{5,4,3,2,1,0:T(8,128)(2,1)} copy-done((bf16[16,2,2,2,64,128]{5,4,3,2,1,0:T(8,128)(2,1)}, bf16[16,2,2,2,64,128]{5,4,3,2,1,0:T(8,128)(2,1)S(1)}, u32[]{:S(2)}) %copy-start) | copy-done | bytes 2097176
  58.9 0.1 slice_bitcast_fusion.1
  59.0 0.6 maximum_multiply_fusion
  59.6 0.1 reshape.55
  59.6 0.1 copy.29
  59.7 0.1 reshape.54
  59.8 0.1 copy.27
  59.9 0.0 copy-done.3
  59.9 0.0 copy-done.4
  59.9 0.7 multiply_multiply_fusion
  60.5 7.1 %fusion.1 = (bf16[8192,128]{1,0:T(8,128)(2,1)}, bf16[8192,128]{1,0:T(8,128)(2,1)}, bf16[8192,128]{1,0:T(8,128)(2,1)}, bf16[8192,128]{1,0:T(8,128)(2,1)}) fusion(bf16[8192,128]{1,0:T(8,128)(2,1)} %param.11, bf16[16,2,2,2,64,128]{5,4,3,2,1,0:T(8,128)(2,1)S(1)} %get-tuple-element.10, bf16[8192,128]{1,0:T(8,128)(2,1)} %param.8, bf16[8192,128]{1,0:T(8,128)(2,1)} %param.10, ...), kind=kLoop, calls=%fused_computation.5 | loop fusion | flops 14680064 | bytes 20971520 | tf_op jit(solution)/shard_map/convert_element_type | solution.py:57
  (1 shorter events, 0.0 us)
Async XLA Ops:
  1.8 0.9 %copy-start.1 = (f32[128,256]{1,0:T(8,128)S(1)}, f32[128,256]{1,0:T(8,128)}, u32[]{:S(2)}) copy-start(f32[128,256]{1,0:T(8,128)} %constant.2.clone.tab_ref) | copy-start | bytes 393220
  2.7 0.7 copy-start.2
  3.3 56.5 %copy-start.3 = (f32[128,16]{0,1:T(8,128)S(1)}, f32[128,16]{0,1:T(8,128)}, u32[]{:S(2)}) copy-start(f32[128,16]{0,1:T(8,128)} %param.12) | copy-start | bytes 24580
  3.3 56.5 %copy-start.4 = (f32[128,16]{0,1:T(8,128)S(1)}, f32[128,16]{0,1:T(8,128)}, u32[]{:S(2)}) copy-start(f32[128,16]{0,1:T(8,128)} %param.13) | copy-start | bytes 24580
  57.6 1.3 %copy-start = (bf16[16,2,2,2,64,128]{5,4,3,2,1,0:T(8,128)(2,1)}, bf16[16,2,2,2,64,128]{5,4,3,2,1,0:T(8,128)(2,1)S(1)}, u32[]{:S(2)}) copy-start(bf16[16,2,2,2,64,128]{5,4,3,2,1,0:T(8,128)(2,1)S(1)} %get-tuple-element.11) | copy-start | bytes 6291460
